TPU v7x, 512 devices: a whole 4x8x8 slice. The times are simulated.
512 devices in a mesh: segment: 8 (over z), dom: 64 (over x, y, core).
Axes of the slice: x: 4, y: 8, z: 8, core: 2. Of those that a mesh axis runs over, the one named last changes fastest.
Arguments:
- features: bfloat16 [32768, 512], P('dom'), may hold values from -6 to 6
- history: bfloat16 [24, 32768, 512], P('segment', 'dom'), may hold values from 0 to 1.5
- weights: bfloat16 [24, 512, 512], P('segment'), may hold values from -0.25 to 0.25
- send_rows: int32 [64, 64, 16], P('dom'), may hold values from 0 to 511
- send_count: int32 [64, 64], P('dom'), may hold values from 0 to 16, as said below
- adj_src: int32 [256, 6], P('dom'), may hold values from 0 to 8, as said below
- adj_blocks: bfloat16 [256, 6, 128, 128], P('dom'), as said below
Outputs:
- fresh: bfloat16 [8, 32768, 512], P('segment', 'dom')
Inputs may be any that keep to these rules, and one draw needn't show every extreme that they name: `send_count`: every sender has one receiver with exactly 16 live slots, and every receiver one such sender. `adj_src`: the entries of a row are distinct; the first one of every destination tile is 0, its own local tile. `adj_blocks`: non-negative.
All inputs are finite; a program needn't handle non-finite values.
Results may differ from a plain program's by a relative error of at most 0.0033.
Values may be sent and summed in bfloat16 or wider, within the bound.
No kernel may reach another device: no remote copies, remote signals or barrier semaphores. Data moves between devices by JAX's collectives and lax.ppermute only.
A program may use at most 128 MiB of HBM per device.

v0:
```python
import jax
import jax.numpy as jnp
from jax import lax
from jax.sharding import PartitionSpec as P

MICRO = 4


def from_behind(block, axis, distance):
    devices = range(lax.axis_size(axis))
    route = [(i - distance, i) for i in devices if i - distance in devices]
    return lax.ppermute(block, axis, route)


def mixing(block_part, picked):
    return jnp.einsum("tkab,tkbd->tad", block_part, picked, preferred_element_type=jnp.float32)


def local(features, history, weights, send_rows, send_count, adj_src, adj_blocks):
    rows_dev = features.shape[0]
    feature_width = features.shape[1]
    levels = weights.shape[0]
    tile_rows = adj_blocks.shape[2]
    slot_count = send_rows.shape[2]
    part_count = send_rows.shape[1]
    segment_count = lax.axis_size("segment")
    segment_index = lax.axis_index("segment")
    batch_rows = rows_dev // MICRO
    batch_tiles = batch_rows // tile_rows
    picked_rows = history[:, send_rows[0]]
    live_slot = jnp.arange(slot_count)[None, :] < send_count[0][:, None]
    outgoing = jnp.where(live_slot[None, :, :, None], picked_rows, jnp.zeros((), jnp.bfloat16))
    halo_count = part_count * slot_count // tile_rows
    arrived = lax.all_to_all(outgoing, "dom", split_axis=1, concat_axis=1, tiled=True)
    halo_tiles = arrived.reshape(levels, halo_count, tile_rows, feature_width)
    layer_ids = (segment_index * levels + jnp.arange(levels)).astype(jnp.float32)
    beta_values = jnp.log1p(1.0 / (layer_ids + 1.0))
    fresh_out = jnp.zeros((rows_dev, feature_width), jnp.bfloat16)
    incoming = jnp.zeros((batch_rows, feature_width), jnp.bfloat16)
    moments = MICRO + segment_count - 1
    for moment in range(moments):
        batch_pos = moment - segment_index
        active = (batch_pos >= 0) & (batch_pos < MICRO)
        batch_id = jnp.clip(batch_pos, 0, MICRO - 1)
        initial = lax.dynamic_slice_in_dim(features, batch_id * batch_rows, batch_rows, 0)
        hidden = jnp.where(segment_index == 0, initial, incoming)
        for layer_pos in range(levels):
            source_ids = lax.dynamic_slice_in_dim(adj_src, batch_id * batch_tiles, batch_tiles, 0)
            block_part = lax.dynamic_slice_in_dim(
                adj_blocks, batch_id * batch_tiles, batch_tiles, 0
            )
            local_tiles = hidden.reshape(batch_tiles, tile_rows, feature_width)
            sources = jnp.concatenate([local_tiles, halo_tiles[layer_pos]], axis=0)
            summed = mixing(block_part, sources[source_ids]).reshape(batch_rows, feature_width)
            support = 0.9 * summed + 0.1 * initial.astype(jnp.float32)
            branch = jnp.dot(
                support.astype(jnp.bfloat16), weights[layer_pos], preferred_element_type=jnp.float32
            )
            beta = beta_values[layer_pos]
            hidden = jax.nn.relu((1.0 - beta) * support + beta * branch).astype(jnp.bfloat16)
        updated = lax.dynamic_update_slice_in_dim(fresh_out, hidden, batch_id * batch_rows, 0)
        fresh_out = jnp.where(active, updated, fresh_out)
        if moment + 1 < moments:
            incoming = from_behind(hidden, "segment", 1)
    return fresh_out[None]


def solution(mesh):
    placed = (
        P("dom", None),
        P("segment", "dom", None),
        P("segment", None, None),
        P("dom", None, None),
        P("dom", None),
        P("dom", None),
        P("dom", None, None, None),
    )
    return jax.shard_map(
        local, mesh=mesh, in_specs=placed, out_specs=P("segment", "dom", None), check_vma=False
    )
```

profile of v0, /device:TPU:6, one launch (start us, length us, event | category | flops | bytes accessed | tf_op | source)
XLA Modules:
  0.0 445.8 jit_solution(18085705306745713929)
XLA Ops:
  1.7 17.4 %gather_fusion = bf16[1024,3,512]{2,0,1:T(8,128)(2,1)} fusion(bf16[3,512,512]{2,1,0:T(8,128)(2,1)S(1)} %copy-done, s32[1024]{0:T(1024)S(1)} %broadcast_clamp_fusion), kind=kCustom, calls=%fused_computation | custom fusion | bytes 6295552 | tf_op jit(solution)/shard_map/gather | solution.py:30
  19.2 3.8 fusion
  23.0 11.2 %all-to-all-start = ((bf16[3,64,16,512]{3,2,0,1:T(8,128)(2,1)}), bf16[3,64,16,512]{3,2,0,1:T(8,128)(2,1)}, u32[]{:S(2)}, u32[]{:S(2)}) async-start(bf16[3,64,16,512]{3,2,0,1:T(8,128)(2,1)} %fusion), calls=%async_computation | async-start | bytes 6291456 | tf_op jit(solution)/shard_map/all_to_all | solution.py:34
  37.9 67.7 %all-to-all-done = bf16[3,64,16,512]{3,2,0,1:T(8,128)(2,1)} async-done(((bf16[3,64,16,512]{3,2,0,1:T(8,128)(2,1)}), bf16[3,64,16,512]{3,2,0,1:T(8,128)(2,1)}, u32[]{:S(2)}, u32[]{:S(2)}) %all-to-all-start) | async-done | bytes 3145760 | tf_op jit(solution)/shard_map/all_to_all | solution.py:34
  108.9 2.8 gather_fusion.1
  116.2 2.8 gather_fusion.2
  123.5 2.8 gather_fusion.3
  131.3 4.1 collective-permute-start
  140.2 2.8 gather_fusion.4
  147.5 2.8 gather_fusion.5
  154.9 2.8 gather_fusion.6
  161.8 4.4 collective-permute-start.1
  166.2 3.6 collective-permute-done.1
  171.9 2.8 gather_fusion.7
  179.3 2.8 gather_fusion.8
  186.6 2.8 gather_fusion.9
  193.5 4.4 collective-permute-start.2
  197.9 3.1 collective-permute-done.2
  203.1 2.8 gather_fusion.10
  210.4 2.8 gather_fusion.11
  217.8 2.8 gather_fusion.12
  224.7 5.4 %collective-permute-start.3 = (bf16[128,512]{1,0:T(8,128)(2,1)S(1)}, bf16[128,512]{1,0:T(8,128)(2,1)S(1)}, u32[]{:S(2)}, u32[]{:S(2)}) collective-permute-start(bf16[128,512]{1,0:T(8,128)(2,1)S(1)} %get-tuple-element.29), channel_id=1, source_target_pairs={{0,64},{64,128},{128,192},{192,256},{256,320},{320,384},{384,448},... | collective-permute-start | bytes 393224 | tf_op jit(solution)/shard_map/ppermute | solution.py:12
  234.7 2.8 gather_fusion.13
  242.1 2.8 gather_fusion.14
  249.4 2.8 gather_fusion.15
  256.3 5.7 %collective-permute-start.4 = (bf16[128,512]{1,0:T(8,128)(2,1)S(1)}, bf16[128,512]{1,0:T(8,128)(2,1)S(1)}, u32[]{:S(2)}, u32[]{:S(2)}) collective-permute-start(bf16[128,512]{1,0:T(8,128)(2,1)S(1)} %get-tuple-element.31), channel_id=1, source_target_pairs={{0,64},{64,128},{128,192},{192,256},{256,320},{320,384},{384,448},... | collective-permute-start | bytes 393224 | tf_op jit(solution)/shard_map/ppermute | solution.py:12
  266.4 2.8 gather_fusion.16
  273.8 2.8 gather_fusion.17
  281.1 2.8 gather_fusion.18
  288.0 5.6 %collective-permute-start.5 = (bf16[128,512]{1,0:T(8,128)(2,1)S(1)}, bf16[128,512]{1,0:T(8,128)(2,1)S(1)}, u32[]{:S(2)}, u32[]{:S(2)}) collective-permute-start(bf16[128,512]{1,0:T(8,128)(2,1)S(1)} %get-tuple-element.33), channel_id=1, source_target_pairs={{0,64},{64,128},{128,192},{192,256},{256,320},{320,384},{384,448},... | collective-permute-start | bytes 393224 | tf_op jit(solution)/shard_map/ppermute | solution.py:12
  298.2 2.8 gather_fusion.19
  305.5 2.8 gather_fusion.20
  312.9 2.8 gather_fusion.21
  319.8 5.6 %collective-permute-start.6 = (bf16[128,512]{1,0:T(8,128)(2,1)S(1)}, bf16[128,512]{1,0:T(8,128)(2,1)S(1)}, u32[]{:S(2)}, u32[]{:S(2)}) collective-permute-start(bf16[128,512]{1,0:T(8,128)(2,1)S(1)} %get-tuple-element.35), channel_id=1, source_target_pairs={{0,64},{64,128},{128,192},{192,256},{256,320},{320,384},{384,448},... | collective-permute-start | bytes 393224 | tf_op jit(solution)/shard_map/ppermute | solution.py:12
  330.0 2.8 gather_fusion.22
  337.3 2.8 gather_fusion.23
  344.6 2.8 gather_fusion.24
  351.5 5.6 %collective-permute-start.7 = (bf16[128,512]{1,0:T(8,128)(2,1)S(1)}, bf16[128,512]{1,0:T(8,128)(2,1)S(1)}, u32[]{:S(2)}, u32[]{:S(2)}) collective-permute-start(bf16[128,512]{1,0:T(8,128)(2,1)S(1)} %get-tuple-element.37), channel_id=1, source_target_pairs={{0,64},{64,128},{128,192},{192,256},{256,320},{320,384},{384,448},... | collective-permute-start | bytes 393224 | tf_op jit(solution)/shard_map/ppermute | solution.py:12
  361.7 2.8 gather_fusion.25
  369.0 2.8 gather_fusion.26
  376.4 2.8 gather_fusion.27
  383.3 5.6 %collective-permute-start.8 = (bf16[128,512]{1,0:T(8,128)(2,1)S(1)}, bf16[128,512]{1,0:T(8,128)(2,1)S(1)}, u32[]{:S(2)}, u32[]{:S(2)}) collective-permute-start(bf16[128,512]{1,0:T(8,128)(2,1)S(1)} %get-tuple-element.39), channel_id=1, source_target_pairs={{0,64},{64,128},{128,192},{192,256},{256,320},{320,384},{384,448},... | collective-permute-start | bytes 393224 | tf_op jit(solution)/shard_map/ppermute | solution.py:12
  393.4 2.8 gather_fusion.28
  400.8 2.8 gather_fusion.29
  408.1 2.8 gather_fusion.30
  415.0 5.6 %collective-permute-start.9 = (bf16[128,512]{1,0:T(8,128)(2,1)S(1)}, bf16[128,512]{1,0:T(8,128)(2,1)S(1)}, u32[]{:S(2)}, u32[]{:S(2)}) collective-permute-start(bf16[128,512]{1,0:T(8,128)(2,1)S(1)} %get-tuple-element.41), channel_id=1, source_target_pairs={{0,64},{64,128},{128,192},{192,256},{256,320},{320,384},{384,448},... | collective-permute-start | bytes 393224 | tf_op jit(solution)/shard_map/ppermute | solution.py:12
  425.2 2.8 gather_fusion.31
  438.8 2.9 gather_fusion.33
  (149 shorter events, 194.8 us)
Async XLA Ops:
  0.0 1.7 copy-start
  23.0 13.9 %copy-start.3 = (s32[4,6]{1,0:T(4,128)S(1)}, s32[4,6]{1,0:T(4,128)}, u32[]{:S(2)}) copy-start(s32[4,6]{1,0:T(4,128)} %param.12) | copy-start | bytes 292
  23.0 82.6 %all-to-all-start = ((bf16[3,64,16,512]{3,2,0,1:T(8,128)(2,1)}), bf16[3,64,16,512]{3,2,0,1:T(8,128)(2,1)}, u32[]{:S(2)}, u32[]{:S(2)}) async-start(bf16[3,64,16,512]{3,2,0,1:T(8,128)(2,1)} %fusion), calls=%async_computation | async-start | bytes 6291456 | tf_op jit(solution)/shard_map/all_to_all | solution.py:34
  131.3 6.8 %collective-permute-start = (bf16[128,512]{1,0:T(8,128)(2,1)S(1)}, bf16[128,512]{1,0:T(8,128)(2,1)S(1)}, u32[]{:S(2)}, u32[]{:S(2)}) collective-permute-start(bf16[128,512]{1,0:T(8,128)(2,1)S(1)} %get-tuple-element.23), channel_id=1, source_target_pairs={{0,64},{64,128},{128,192},{192,256},{256,320},{320,384},{384,448},... | collective-permute-start | bytes 393224 | tf_op jit(solution)/shard_map/ppermute | solution.py:12
  161.8 8.0 %collective-permute-start.1 = (bf16[128,512]{1,0:T(8,128)(2,1)S(1)}, bf16[128,512]{1,0:T(8,128)(2,1)S(1)}, u32[]{:S(2)}, u32[]{:S(2)}) collective-permute-start(bf16[128,512]{1,0:T(8,128)(2,1)S(1)} %get-tuple-element.25), channel_id=1, source_target_pairs={{0,64},{64,128},{128,192},{192,256},{256,320},{320,384},{384,448},... | collective-permute-start | bytes 393224 | tf_op jit(solution)/shard_map/ppermute | solution.py:12
  193.5 7.5 %collective-permute-start.2 = (bf16[128,512]{1,0:T(8,128)(2,1)S(1)}, bf16[128,512]{1,0:T(8,128)(2,1)S(1)}, u32[]{:S(2)}, u32[]{:S(2)}) collective-permute-start(bf16[128,512]{1,0:T(8,128)(2,1)S(1)} %get-tuple-element.27), channel_id=1, source_target_pairs={{0,64},{64,128},{128,192},{192,256},{256,320},{320,384},{384,448},... | collective-permute-start | bytes 393224 | tf_op jit(solution)/shard_map/ppermute | solution.py:12
  224.7 8.0 %collective-permute-start.3 = (bf16[128,512]{1,0:T(8,128)(2,1)S(1)}, bf16[128,512]{1,0:T(8,128)(2,1)S(1)}, u32[]{:S(2)}, u32[]{:S(2)}) collective-permute-start(bf16[128,512]{1,0:T(8,128)(2,1)S(1)} %get-tuple-element.29), channel_id=1, source_target_pairs={{0,64},{64,128},{128,192},{192,256},{256,320},{320,384},{384,448},... | collective-permute-start | bytes 393224 | tf_op jit(solution)/shard_map/ppermute | solution.py:12
  256.3 8.0 %collective-permute-start.4 = (bf16[128,512]{1,0:T(8,128)(2,1)S(1)}, bf16[128,512]{1,0:T(8,128)(2,1)S(1)}, u32[]{:S(2)}, u32[]{:S(2)}) collective-permute-start(bf16[128,512]{1,0:T(8,128)(2,1)S(1)} %get-tuple-element.31), channel_id=1, source_target_pairs={{0,64},{64,128},{128,192},{192,256},{256,320},{320,384},{384,448},... | collective-permute-start | bytes 393224 | tf_op jit(solution)/shard_map/ppermute | solution.py:12
  288.0 8.1 %collective-permute-start.5 = (bf16[128,512]{1,0:T(8,128)(2,1)S(1)}, bf16[128,512]{1,0:T(8,128)(2,1)S(1)}, u32[]{:S(2)}, u32[]{:S(2)}) collective-permute-start(bf16[128,512]{1,0:T(8,128)(2,1)S(1)} %get-tuple-element.33), channel_id=1, source_target_pairs={{0,64},{64,128},{128,192},{192,256},{256,320},{320,384},{384,448},... | collective-permute-start | bytes 393224 | tf_op jit(solution)/shard_map/ppermute | solution.py:12
  319.8 8.1 %collective-permute-start.6 = (bf16[128,512]{1,0:T(8,128)(2,1)S(1)}, bf16[128,512]{1,0:T(8,128)(2,1)S(1)}, u32[]{:S(2)}, u32[]{:S(2)}) collective-permute-start(bf16[128,512]{1,0:T(8,128)(2,1)S(1)} %get-tuple-element.35), channel_id=1, source_target_pairs={{0,64},{64,128},{128,192},{192,256},{256,320},{320,384},{384,448},... | collective-permute-start | bytes 393224 | tf_op jit(solution)/shard_map/ppermute | solution.py:12
  351.5 8.1 %collective-permute-start.7 = (bf16[128,512]{1,0:T(8,128)(2,1)S(1)}, bf16[128,512]{1,0:T(8,128)(2,1)S(1)}, u32[]{:S(2)}, u32[]{:S(2)}) collective-permute-start(bf16[128,512]{1,0:T(8,128)(2,1)S(1)} %get-tuple-element.37), channel_id=1, source_target_pairs={{0,64},{64,128},{128,192},{192,256},{256,320},{320,384},{384,448},... | collective-permute-start | bytes 393224 | tf_op jit(solution)/shard_map/ppermute | solution.py:12
  383.3 8.1 %collective-permute-start.8 = (bf16[128,512]{1,0:T(8,128)(2,1)S(1)}, bf16[128,512]{1,0:T(8,128)(2,1)S(1)}, u32[]{:S(2)}, u32[]{:S(2)}) collective-permute-start(bf16[128,512]{1,0:T(8,128)(2,1)S(1)} %get-tuple-element.39), channel_id=1, source_target_pairs={{0,64},{64,128},{128,192},{192,256},{256,320},{320,384},{384,448},... | collective-permute-start | bytes 393224 | tf_op jit(solution)/shard_map/ppermute | solution.py:12
  415.0 8.1 %collective-permute-start.9 = (bf16[128,512]{1,0:T(8,128)(2,1)S(1)}, bf16[128,512]{1,0:T(8,128)(2,1)S(1)}, u32[]{:S(2)}, u32[]{:S(2)}) collective-permute-start(bf16[128,512]{1,0:T(8,128)(2,1)S(1)} %get-tuple-element.41), channel_id=1, source_target_pairs={{0,64},{64,128},{128,192},{192,256},{256,320},{320,384},{384,448},... | collective-permute-start | bytes 393224 | tf_op jit(solution)/shard_map/ppermute | solution.py:12
  425.2 2.9 copy-start.2
  438.8 7.1 %copy-start.1 = (bf16[3,512,512]{2,1,0:T(8,128)(2,1)S(1)}, bf16[3,512,512]{2,1,0:T(8,128)(2,1)}, u32[]{:S(2)}) copy-start(bf16[3,512,512]{2,1,0:T(8,128)(2,1)} %param.8) | copy-start | bytes 4718596
where the time goes:
time: 455 us; the launch traced here: 446 us
  matrix products  119 us (26%)
  local copies, waits for them, and re-layouts  114 us (25%)
  waiting for transfers between devices  92.4 us (20%)
  starting transfers between devices  63.1 us (14%)
  other arithmetic  53.8 us (12%)
    gather x33, local copies, waits for them, and re-layouts, local(): sources[source_ids]  91.4 us
    dot_general x33, matrix products, local(): jnp.dot(support.astype(jnp.bfloat16), weights[layer_pos], preferred_eleme...  71 us
    all_to_all x1, waiting for transfers between devices, local(): lax.all_to_all(outgoing, 'dom', split_axis=1, concat_axis=1, tiled=True)  67.7 us
    ppermute x10, starting transfers between devices, from_behind(): return lax.ppermute(block, axis, route)  51.8 us
    dot_general x33, matrix products, mixing(): jnp.einsum('tkab,tkbd->tad', block_part, picked, preferred_element_type=j...  48.3 us
    concatenate x33, other arithmetic, local(): sources = jnp.concatenate([local_tiles, halo_tiles[layer_pos]], axis=0)  38 us
    ppermute x10, waiting for transfers between devices, from_behind(): return lax.ppermute(block, axis, route)  24.7 us
    gather x1, local copies, waits for them, and re-layouts, local(): picked_rows = history[:, send_rows[0]]  17.4 us
  transfers between devices with their start and end apart: 11, of which 11 were waited for; matrix products, arithmetic and copies ran while one was open for 1% of the time, Pallas kernels for 0%

commit v1 on v0

v1 whole, which is shorter than its diff:
```python
import jax
import jax.numpy as jnp
import numpy as np
from jax import lax
from jax.experimental import pallas as pl
from jax.experimental.pallas import tpu as pltpu
from jax.sharding import PartitionSpec as P

MICRO = 4
CORES = 2
BOTH = ("segment", "dom")


def chain_kernel(segments, levels, betas, *refs):
    x_ref, a_ref = refs[:2]
    w_refs = refs[2 : 2 + segments]
    h_refs = refs[2 + segments : 2 + segments * (1 + levels)]
    out_ref, w_buf, h_buf, w_sem, h_sem = refs[2 + segments * (1 + levels) :]
    mine = lax.axis_index("segment")

    def w_copy(j, s):
        return pltpu.make_async_copy(w_refs[j], w_buf.at[s], w_sem.at[s])

    def h_copy(j, i, s):
        return pltpu.make_async_copy(h_refs[i * segments + j], h_buf.at[s, i], h_sem.at[s, i])

    for s in range(segments):
        shard = lax.rem(mine - s + segments, segments)
        for j in range(segments):

            @pl.when(shard == j)
            def _():
                for i in range(levels):
                    h_copy(j, i, s).start()
                w_copy(j, s).start()

    a = a_ref[...]
    x = x_ref[...]
    for s in range(segments):
        w_copy(0, s).wait()
        for i in range(levels):
            h_copy(0, i, s).wait()
            beta = betas[s * levels + i]
            summed = jnp.dot(a, x, preferred_element_type=jnp.float32)
            support = 0.9 * summed + h_buf[s, i].astype(jnp.float32)
            branch = jnp.dot(
                support.astype(jnp.bfloat16), w_buf[s, i], preferred_element_type=jnp.float32
            )
            x = jnp.maximum((1.0 - beta) * support + beta * branch, 0.0).astype(jnp.bfloat16)
        out_ref[s] = x


def chain(x, a, weight_shards, halo_shards):
    segments = len(weight_shards)
    levels, width, _ = weight_shards[0].shape
    rows = x.shape[0]
    order = np.arange(segments * levels, dtype=np.float32)
    betas = [float(b) for b in np.log1p(np.float32(1.0) / (order + np.float32(1.0)))]
    anywhere = pl.BlockSpec(memory_space=pl.ANY)
    vmem = pl.BlockSpec(memory_space=pltpu.VMEM)
    flat_halo = [h for level in halo_shards for h in level]
    return pl.pallas_call(
        lambda *refs: chain_kernel(segments, levels, betas, *refs),
        out_shape=jax.ShapeDtypeStruct((segments, rows, width), jnp.bfloat16),
        in_specs=[vmem, vmem] + [anywhere] * (len(weight_shards) + len(flat_halo)),
        out_specs=vmem,
        scratch_shapes=[
            pltpu.VMEM((segments, levels, width, width), jnp.bfloat16),
            pltpu.VMEM((segments, levels, rows, width), jnp.bfloat16),
            pltpu.SemaphoreType.DMA((segments,)),
            pltpu.SemaphoreType.DMA((segments, levels)),
        ],
        compiler_params=pltpu.CompilerParams(vmem_limit_bytes=32 * 1024 * 1024),
        cost_estimate=pl.CostEstimate(
            flops=2 * segments * levels * rows * width * (width + rows),
            bytes_accessed=2 * segments * levels * width * (width + rows),
            transcendentals=0,
        ),
    )(x, a, *weight_shards, *flat_halo)


def local(features, history, weights, send_rows, send_count, adj_src, adj_blocks):
    rows_dev, width = features.shape
    levels = weights.shape[0]
    tile_rows = adj_blocks.shape[2]
    part_count, slot_count = send_rows.shape[1:]
    halo_rows = part_count * slot_count
    halo_tiles = halo_rows // tile_rows
    segments = lax.axis_size("segment")
    parts = lax.axis_size("dom")
    mine = lax.axis_index("segment")
    core = lax.rem(lax.axis_index("dom"), CORES)

    def owner_index(z, pair):
        return z * parts + pair * CORES + z % CORES

    def along_owners(block, step):
        route = [
            (owner_index(z, pair), owner_index((z + step) % segments, pair))
            for z in range(segments)
            for pair in range(parts // CORES)
        ]
        return lax.ppermute(block, BOTH, route)

    def to_owner(block, step):
        route = [
            (z * parts + d, (z + step) % segments * parts + d)
            for z in range(segments)
            for d in range(parts)
            if (z + step) % segments % CORES == d % CORES
        ]
        return lax.ppermute(block, BOTH, route)

    def from_owner(block, step):
        route = [
            (z * parts + d, (z + step) % segments * parts + d)
            for z in range(segments)
            for d in range(parts)
            if z % CORES == d % CORES
        ]
        return lax.ppermute(block, BOTH, route)

    live = jnp.arange(slot_count)[None, :] < send_count[0][:, None]
    wanted = jnp.where(live, send_rows[0], -1).reshape(halo_rows)
    pick = (wanted[:, None] == jnp.arange(rows_dev)[None, :]).astype(jnp.bfloat16)
    arrived = []
    for i in range(levels):
        outgoing = jnp.dot(pick, history[i], preferred_element_type=jnp.float32)
        outgoing = outgoing.astype(jnp.bfloat16).reshape(part_count, slot_count, width)
        arrived.append(
            lax.all_to_all(outgoing, "dom", split_axis=0, concat_axis=0, tiled=True)
        )

    shards = [weights] + [None] * (segments - 1)
    for k in range(1, segments // 2 + 1):
        shards[k] = along_owners(shards[k - 1], 1)
    for k in range(1, segments - segments // 2):
        shards[segments - k] = along_owners(shards[(segments - k + 1) % segments], -1)

    spread = sum(
        jnp.where(
            (adj_src[:, k, None] - 1 == jnp.arange(halo_tiles)[None, :])[:, None, :, None],
            adj_blocks[:, k, :, None, :],
            jnp.zeros((), jnp.bfloat16),
        )
        for k in range(1, adj_src.shape[1])
    ).reshape(rows_dev, halo_rows)

    halo_shards = []
    for i in range(levels):
        summed = jnp.dot(
            spread, arrived[i].reshape(halo_rows, width), preferred_element_type=jnp.float32
        )
        part = (0.9 * summed + 0.1 * features.astype(jnp.float32)).astype(jnp.bfloat16)
        part = part.reshape(MICRO, tile_rows, width)
        level = []
        for k in range(segments):
            target = lax.rem(mine + k, segments)
            block = lax.dynamic_index_in_dim(part, target // CORES, 0, keepdims=False)
            level.append(block if k == 0 else to_owner(block, k))
        halo_shards.append(level)

    tile = mine // CORES
    x = lax.dynamic_slice_in_dim(features, tile * tile_rows, tile_rows, 0)
    a = lax.dynamic_index_in_dim(adj_blocks[:, 0], tile, 0, keepdims=False)
    done = chain(x, a, shards, halo_shards)

    odd = lax.rem(mine + core, CORES)
    got = []
    for k in range(segments):
        target = lax.rem(mine + k, segments)
        block = lax.dynamic_index_in_dim(done, target, 0, keepdims=False)
        got.append(block if k == 0 else from_owner(block, k))
    pairs = jnp.stack(
        [jnp.where(odd == 0, got[k], got[k + 1]) for k in range(0, segments, CORES)]
    )
    last = (mine - core - odd + segments) // CORES
    tiles = [
        lax.dynamic_index_in_dim(pairs, lax.rem(last - m + MICRO, MICRO), 0, keepdims=False)
        for m in range(MICRO)
    ]
    return jnp.concatenate(tiles, axis=0)[None]


def solution(mesh):
    placed = (
        P("dom", None),
        P("segment", "dom", None),
        P("segment", None, None),
        P("dom", None, None),
        P("dom", None),
        P("dom", None),
        P("dom", None, None, None),
    )
    return jax.shard_map(
        local, mesh=mesh, in_specs=placed, out_specs=P("segment", "dom", None), check_vma=False
    )
```

time: 455 us -> 266 us (0.58); the launches traced: 446 us -> 264 us
  matrix products: 119 us -> 12.2 us
  local copies, waits for them, and re-layouts: 114 us -> 27.2 us
  starting transfers between devices: 63.1 us -> 125 us
  other arithmetic: 53.8 us -> 3.01 us
  Pallas kernels: 0 us -> 13.6 us
  waiting for transfers between devices: 92.4 us -> 81.9 us
    gather x34 -> x0, local copies, waits for them, and re-layouts: 109 us -> none  [the longest x33 91.4 us: local(): sources[source_ids]]
    dot_general x66 -> x6, matrix products: 119 us -> 12.2 us  [the longest x3 8.4 us: local(): outgoing = jnp.dot(pick, history[i], preferred_element_type=jnp.float32)]
    all_to_all x1 -> x3, waiting for transfers between devices: 67.7 us -> 19.8 us  [local(): lax.all_to_all(outgoing, 'dom', split_axis=0, concat_axis=0, tiled=True)]
    ppermute x10 -> x35, starting transfers between devices: 51.8 us -> 95.7 us  [the longest x21 46 us: to_owner(): return lax.ppermute(block, BOTH, route)]
    concatenate x33 -> x0, other arithmetic: 38 us -> none  [local(): sources = jnp.concatenate([local_tiles, halo_tiles[layer_pos]], axis=0)]
    ppermute x10 -> x35, waiting for transfers between devices: 24.7 us -> 62.1 us  [the longest x21 38.9 us: to_owner(): return lax.ppermute(block, BOTH, route)]
    unnamed x9 -> x79, local copies, waits for them, and re-layouts: 1.88 us -> 21.4 us
    all_to_all x1 -> x3, starting transfers between devices: 11.2 us -> 29.7 us  [local(): lax.all_to_all(outgoing, 'dom', split_axis=0, concat_axis=0, tiled=True)]
  transfers between devices with their start and end apart: 11 -> 38, of which waited for: 11 -> 17; matrix products, arithmetic and copies ran while one was open for 1% -> 6% of each run, Pallas kernels for 0% -> 0%
where the time goes in v1:
time: 266 us; the launch traced here: 264 us
  starting transfers between devices  125 us (47%)
  waiting for transfers between devices  81.9 us (31%)
  local copies, waits for them, and re-layouts  27.2 us (10%)
  Pallas kernels  13.6 us (5%)
  matrix products  12.2 us (5%)
  other arithmetic  3.01 us (1%)
    ppermute x21, starting transfers between devices, to_owner(): return lax.ppermute(block, BOTH, route)  46 us
    ppermute x21, waiting for transfers between devices, to_owner(): return lax.ppermute(block, BOTH, route)  38.9 us
    ppermute x7, starting transfers between devices, along_owners(): return lax.ppermute(block, BOTH, route)  31.1 us
    all_to_all x3, starting transfers between devices, local(): lax.all_to_all(outgoing, 'dom', split_axis=0, concat_axis=0, tiled=True)  29.7 us
    unnamed x79, local copies, waits for them, and re-layouts  21.4 us
    all_to_all x3, waiting for transfers between devices, local(): lax.all_to_all(outgoing, 'dom', split_axis=0, concat_axis=0, tiled=True)  19.8 us
    ppermute x7, starting transfers between devices, from_owner(): return lax.ppermute(block, BOTH, route)  18.7 us
    ppermute x7, waiting for transfers between devices, along_owners(): return lax.ppermute(block, BOTH, route)  16.5 us
  transfers between devices with their start and end apart: 38, of which 17 were waited for; matrix products, arithmetic and copies ran while one was open for 6% of the time, Pallas kernels for 0%

profile of v1, /device:TPU:6, one launch (start us, length us, event | category | flops | bytes accessed | tf_op | source)
XLA Modules:
  0.0 264.4 jit_solution(11475787498043828218)
XLA Ops:
  1.7 2.8 %fusion.5 = bf16[1024,512]{1,0:T(8,128)(2,1)} fusion(s32[1024]{0:T(1024)S(1)} %broadcast_select_fusion, bf16[3,512,512]{2,1,0:T(8,128)(2,1)} %param.8), kind=kOutput, calls=%fused_computation.6 | convolution fusion | flops 537919488 | bytes 1576960 | tf_op jit(solution)/shard_map/dot_general | solution.py:128
  4.5 10.9 %all-to-all-start.2 = ((bf16[64,16,512]{2,1,0:T(8,128)(2,1)}), bf16[64,16,512]{2,1,0:T(8,128)(2,1)S(1)}, u32[]{:S(2)}, u32[]{:S(2)}) async-start(bf16[64,16,512]{2,1,0:T(8,128)(2,1)} %bitcast.137), calls=%async_computation.2 | async-start | bytes 2097152 | tf_op jit(solution)/shard_map/all_to_all | solution.py:131
  15.5 4.0 %collective-permute-start = (bf16[3,512,512]{2,1,0:T(8,128)(2,1)S(1)}, bf16[3,512,512]{2,1,0:T(8,128)(2,1)}, u32[]{:S(2)}, u32[]{:S(2)}) collective-permute-start(bf16[3,512,512]{2,1,0:T(8,128)(2,1)S(1)} %copy-done), channel_id=1, source_target_pairs={{0,65},{2,67},{4,69},{6,71},{8,73},{10,75},{12,77},{14,79},{16,81}... | collective-permute-start | bytes 4718600 | tf_op jit(solution)/shard_map/ppermute | solution.py:103
  19.5 2.8 %fusion.4 = bf16[1024,512]{1,0:T(8,128)(2,1)} fusion(s32[1024]{0:T(1024)S(1)} %broadcast_select_fusion, bf16[3,512,512]{2,1,0:T(8,128)(2,1)} %param.8), kind=kOutput, calls=%fused_computation.5 | convolution fusion | flops 537919488 | bytes 1576960 | tf_op jit(solution)/shard_map/dot_general | solution.py:128
  22.3 19.8 %all-to-all-done.2 = bf16[64,16,512]{2,1,0:T(8,128)(2,1)S(1)} async-done(((bf16[64,16,512]{2,1,0:T(8,128)(2,1)}), bf16[64,16,512]{2,1,0:T(8,128)(2,1)S(1)}, u32[]{:S(2)}, u32[]{:S(2)}) %all-to-all-start.2) | async-done | bytes 1048608 | tf_op jit(solution)/shard_map/all_to_all | solution.py:131
  43.1 8.1 %all-to-all-start.1 = ((bf16[64,16,512]{2,1,0:T(8,128)(2,1)}), bf16[64,16,512]{2,1,0:T(8,128)(2,1)S(1)}, u32[]{:S(2)}, u32[]{:S(2)}) async-start(bf16[64,16,512]{2,1,0:T(8,128)(2,1)} %bitcast.132), calls=%async_computation.1 | async-start | bytes 2097152 | tf_op jit(solution)/shard_map/all_to_all | solution.py:131
  51.2 10.7 %collective-permute-start.4 = (bf16[3,512,512]{2,1,0:T(8,128)(2,1)S(1)}, bf16[3,512,512]{2,1,0:T(8,128)(2,1)}, u32[]{:S(2)}, u32[]{:S(2)}) collective-permute-start(bf16[3,512,512]{2,1,0:T(8,128)(2,1)S(1)} %copy-done), channel_id=1, source_target_pairs={{0,449},{2,451},{4,453},{6,455},{8,457},{10,459},{12,461},{14,463}... | collective-permute-start | bytes 4718600 | tf_op jit(solution)/shard_map/ppermute | solution.py:103
  61.9 1.9 collective-permute-start.1
  63.8 16.0 %collective-permute-done.4.refs_9_ = bf16[3,512,512]{2,1,0:T(8,128)(2,1)} collective-permute-done((bf16[3,512,512]{2,1,0:T(8,128)(2,1)S(1)}, bf16[3,512,512]{2,1,0:T(8,128)(2,1)}, u32[]{:S(2)}, u32[]{:S(2)}) %collective-permute-start.4) | collective-permute-done | bytes 1572896 | tf_op jit(solution)/shard_map/ppermute | solution.py:103
  79.8 5.3 %collective-permute-start.5 = (bf16[3,512,512]{2,1,0:T(8,128)(2,1)}, bf16[3,512,512]{2,1,0:T(8,128)(2,1)}, u32[]{:S(2)}, u32[]{:S(2)}) collective-permute-start(bf16[3,512,512]{2,1,0:T(8,128)(2,1)} %collective-permute-done.4.refs_9_), channel_id=1, source_target_pairs={{0,449},{2,451},{4,453},{6,455},{8,457},{10,459},{12,461},{14,463}... | collective-permute-start | bytes 4718600 | tf_op jit(solution)/shard_map/ppermute | solution.py:103
  85.2 1.9 collective-permute-start.2
  87.6 2.8 %fusion.3 = bf16[1024,512]{1,0:T(8,128)(2,1)} fusion(s32[1024]{0:T(1024)S(1)} %broadcast_select_fusion, bf16[3,512,512]{2,1,0:T(8,128)(2,1)} %param.8), kind=kOutput, calls=%fused_computation.4 | convolution fusion | flops 537919488 | bytes 1576960 | tf_op jit(solution)/shard_map/dot_general | solution.py:128
  90.4 10.6 %all-to-all-start = ((bf16[64,16,512]{2,1,0:T(8,128)(2,1)}), bf16[64,16,512]{2,1,0:T(8,128)(2,1)}, u32[]{:S(2)}, u32[]{:S(2)}) async-start(bf16[64,16,512]{2,1,0:T(8,128)(2,1)} %bitcast.133), calls=%async_computation | async-start | bytes 2097152 | tf_op jit(solution)/shard_map/all_to_all | solution.py:131
  103.4 5.3 %collective-permute-start.6 = (bf16[3,512,512]{2,1,0:T(8,128)(2,1)}, bf16[3,512,512]{2,1,0:T(8,128)(2,1)}, u32[]{:S(2)}, u32[]{:S(2)}) collective-permute-start(bf16[3,512,512]{2,1,0:T(8,128)(2,1)} %collective-permute-done.5.refs_8_), channel_id=1, source_target_pairs={{0,449},{2,451},{4,453},{6,455},{8,457},{10,459},{12,461},{14,463}... | collective-permute-start | bytes 4718600 | tf_op jit(solution)/shard_map/ppermute | solution.py:103
  108.7 1.9 collective-permute-start.3
  113.4 3.4 %collective-permute-start.26 = (bf16[128,512]{1,0:T(8,128)(2,1)S(1)}, bf16[128,512]{1,0:T(8,128)(2,1)S(1)}, u32[]{:S(2)}, u32[]{:S(2)}) collective-permute-start(bf16[128,512]{1,0:T(8,128)(2,1)S(1)} %get-tuple-element.28), channel_id=1, source_target_pairs={{0,384},{2,386},{4,388},{6,390},{8,392},{10,394},{12,396},{14,398}... | collective-permute-start | bytes 393224 | tf_op jit(solution)/shard_map/ppermute | solution.py:112
  116.8 1.3 collective-permute-start.25
  118.8 1.6 collective-permute-done.27.refs_33_
  120.4 2.1 collective-permute-start.24
  122.6 15.5 %collective-permute-done.26.refs_32_ = bf16[128,512]{1,0:T(8,128)(2,1)S(1)} collective-permute-done((bf16[128,512]{1,0:T(8,128)(2,1)S(1)}, bf16[128,512]{1,0:T(8,128)(2,1)S(1)}, u32[]{:S(2)}, u32[]{:S(2)}) %collective-permute-start.26) | collective-permute-done | bytes 131104 | tf_op jit(solution)/shard_map/ppermute | solution.py:112
  139.3 3.2 %collective-permute-start.22 = (bf16[128,512]{1,0:T(8,128)(2,1)S(1)}, bf16[128,512]{1,0:T(8,128)(2,1)S(1)}, u32[]{:S(2)}, u32[]{:S(2)}) collective-permute-start(bf16[128,512]{1,0:T(8,128)(2,1)S(1)} %get-tuple-element.32), channel_id=1, source_target_pairs={{0,128},{2,130},{4,132},{6,134},{8,136},{10,138},{12,140},{14,142}... | collective-permute-start | bytes 393224 | tf_op jit(solution)/shard_map/ppermute | solution.py:112
  144.6 4.4 %collective-permute-done.23.refs_29_ = bf16[128,512]{1,0:T(8,128)(2,1)S(1)} collective-permute-done((bf16[128,512]{1,0:T(8,128)(2,1)S(1)}, bf16[128,512]{1,0:T(8,128)(2,1)S(1)}, u32[]{:S(2)}, u32[]{:S(2)}) %collective-permute-start.23) | collective-permute-done | bytes 131104 | tf_op jit(solution)/shard_map/ppermute | solution.py:112
  152.0 4.5 %collective-permute-start.19 = (bf16[128,512]{1,0:T(8,128)(2,1)S(1)}, bf16[128,512]{1,0:T(8,128)(2,1)S(1)}, u32[]{:S(2)}, u32[]{:S(2)}) collective-permute-start(bf16[128,512]{1,0:T(8,128)(2,1)S(1)} %get-tuple-element.36), channel_id=1, source_target_pairs={{0,384},{2,386},{4,388},{6,390},{8,392},{10,394},{12,396},{14,398}... | collective-permute-start | bytes 393224 | tf_op jit(solution)/shard_map/ppermute | solution.py:112
  156.5 2.4 fusion.9
  158.9 1.4 collective-permute-start.18
  160.4 2.1 collective-permute-start.17
  162.5 2.1 collective-permute-done.19.refs_24_
  166.8 2.8 %collective-permute-done.18.refs_23_ = bf16[128,512]{1,0:T(8,128)(2,1)S(1)} collective-permute-done((bf16[128,512]{1,0:T(8,128)(2,1)S(1)}, bf16[128,512]{1,0:T(8,128)(2,1)S(1)}, u32[]{:S(2)}, u32[]{:S(2)}) %collective-permute-start.18) | collective-permute-done | bytes 131104 | tf_op jit(solution)/shard_map/ppermute | solution.py:112
  169.6 2.3 collective-permute-start.15
  171.9 1.3 collective-permute-start.14
  173.2 1.9 collective-permute-done.16.refs_21_
  176.3 2.4 collective-permute-done.15.refs_20_
  179.4 6.2 %collective-permute-start.12 = (bf16[128,512]{1,0:T(8,128)(2,1)}, bf16[128,512]{1,0:T(8,128)(2,1)S(1)}, u32[]{:S(2)}, u32[]{:S(2)}) collective-permute-start(bf16[128,512]{1,0:T(8,128)(2,1)} %get-tuple-element.44), channel_id=1, source_target_pairs={{0,384},{2,386},{4,388},{6,390},{8,392},{10,394},{12,396},{14,398}... | collective-permute-start | bytes 393224 | tf_op jit(solution)/shard_map/ppermute | solution.py:112
  188.2 2.0 collective-permute-start.10
  190.2 2.8 %collective-permute-done.12.refs_16_ = bf16[128,512]{1,0:T(8,128)(2,1)S(1)} collective-permute-done((bf16[128,512]{1,0:T(8,128)(2,1)}, bf16[128,512]{1,0:T(8,128)(2,1)S(1)}, u32[]{:S(2)}, u32[]{:S(2)}) %collective-permute-start.12) | collective-permute-done | bytes 131104 | tf_op jit(solution)/shard_map/ppermute | solution.py:112
  196.5 4.8 %collective-permute-start.8 = (bf16[128,512]{1,0:T(8,128)(2,1)}, bf16[128,512]{1,0:T(8,128)(2,1)S(1)}, u32[]{:S(2)}, u32[]{:S(2)}) collective-permute-start(bf16[128,512]{1,0:T(8,128)(2,1)} %get-tuple-element.48), channel_id=1, source_target_pairs={{0,128},{2,130},{4,132},{6,134},{8,136},{10,138},{12,140},{14,142}... | collective-permute-start | bytes 393224 | tf_op jit(solution)/shard_map/ppermute | solution.py:112
  202.6 1.4 dynamic-slice_bitcast_fusion.35.refs_1_
  206.6 3.1 %collective-permute-done.7.refs_11_ = bf16[128,512]{1,0:T(8,128)(2,1)} collective-permute-done((bf16[128,512]{1,0:T(8,128)(2,1)}, bf16[128,512]{1,0:T(8,128)(2,1)}, u32[]{:S(2)}, u32[]{:S(2)}) %collective-permute-start.7) | collective-permute-done | bytes 131104 | tf_op jit(solution)/shard_map/ppermute | solution.py:112
  224.1 13.6 %shard_map.73 = bf16[8,128,512]{2,1,0:T(8,128)(2,1)S(1)} custom-call(bf16[128,512]{1,0:T(8,128)(2,1)S(1)} %constant_dynamic-slice_fusion.refs_0_, bf16[128,128]{1,0:T(8,128)(2,1)S(1)} %copy-done.31, bf16[3,512,512]{2,1,0:T(8,128)(2,1)S(1)} %copy-done, bf16[3,512,512]{2,1,0:T(8,128)(2,1)} %collective-permute-done.refs_3_, ...), custom_call_target="tpu_custom_call" | custom-call | flops 2013265920 | bytes 15728640 | tf_op jit(solution)/shard_map/pallas_call | solution.py:62
  237.8 2.9 %collective-permute-start.34 = (bf16[128,512]{1,0:T(8,128)(2,1)S(1)}, bf16[128,512]{1,0:T(8,128)(2,1)S(1)}, u32[]{:S(2)}, u32[]{:S(2)}) collective-permute-start(bf16[128,512]{1,0:T(8,128)(2,1)S(1)} %get-tuple-element.11), channel_id=1, source_target_pairs={{0,448},{2,450},{4,452},{6,454},{8,456},{10,458},{12,460},{14,462}... | collective-permute-start | bytes 393224 | tf_op jit(solution)/shard_map/ppermute | solution.py:121
  240.7 2.4 collective-permute-start.33
  243.1 1.3 collective-permute-start.28
  244.4 1.3 collective-permute-start.32
  245.7 5.7 %collective-permute-start.31 = (bf16[128,512]{1,0:T(8,128)(2,1)S(1)}, bf16[128,512]{1,0:T(8,128)(2,1)S(1)}, u32[]{:S(2)}, u32[]{:S(2)}) collective-permute-start(bf16[128,512]{1,0:T(8,128)(2,1)S(1)} %get-tuple-element.14), channel_id=1, source_target_pairs={{0,256},{2,258},{4,260},{6,262},{8,264},{10,266},{12,268},{14,270}... | collective-permute-start | bytes 393224 | tf_op jit(solution)/shard_map/ppermute | solution.py:121
  251.4 1.3 collective-permute-start.30
  252.7 3.8 %collective-permute-start.29 = (bf16[128,512]{1,0:T(8,128)(2,1)S(1)}, bf16[128,512]{1,0:T(8,128)(2,1)S(1)}, u32[]{:S(2)}, u32[]{:S(2)}) collective-permute-start(bf16[128,512]{1,0:T(8,128)(2,1)S(1)} %get-tuple-element.16), channel_id=1, source_target_pairs={{0,128},{2,130},{4,132},{6,134},{8,136},{10,138},{12,140},{14,142}... | collective-permute-start | bytes 393224 | tf_op jit(solution)/shard_map/ppermute | solution.py:121
  256.6 1.3 collective-permute-done.31
  258.0 5.4 %collective-permute-done.29 = bf16[128,512]{1,0:T(8,128)(2,1)S(1)} collective-permute-done((bf16[128,512]{1,0:T(8,128)(2,1)S(1)}, bf16[128,512]{1,0:T(8,128)(2,1)S(1)}, u32[]{:S(2)}, u32[]{:S(2)}) %collective-permute-start.29) | collective-permute-done | bytes 131104 | tf_op jit(solution)/shard_map/ppermute | solution.py:121
  (137 shorter events, 44.7 us)
Async XLA Ops:
  4.5 10.9 %copy-start = (bf16[3,512,512]{2,1,0:T(8,128)(2,1)S(1)}, bf16[3,512,512]{2,1,0:T(8,128)(2,1)}, u32[]{:S(2)}) copy-start(bf16[3,512,512]{2,1,0:T(8,128)(2,1)} %refs_2_.1) | copy-start | bytes 4718596
  4.5 37.6 %all-to-all-start.2 = ((bf16[64,16,512]{2,1,0:T(8,128)(2,1)}), bf16[64,16,512]{2,1,0:T(8,128)(2,1)S(1)}, u32[]{:S(2)}, u32[]{:S(2)}) async-start(bf16[64,16,512]{2,1,0:T(8,128)(2,1)} %bitcast.137), calls=%async_computation.2 | async-start | bytes 2097152 | tf_op jit(solution)/shard_map/all_to_all | solution.py:131
  15.5 46.5 %collective-permute-start = (bf16[3,512,512]{2,1,0:T(8,128)(2,1)S(1)}, bf16[3,512,512]{2,1,0:T(8,128)(2,1)}, u32[]{:S(2)}, u32[]{:S(2)}) collective-permute-start(bf16[3,512,512]{2,1,0:T(8,128)(2,1)S(1)} %copy-done), channel_id=1, source_target_pairs={{0,65},{2,67},{4,69},{6,71},{8,73},{10,75},{12,77},{14,79},{16,81}... | collective-permute-start | bytes 4718600 | tf_op jit(solution)/shard_map/ppermute | solution.py:103
  22.3 64.8 %copy-start.37 = (s32[4,6]{1,0:T(4,128)S(1)}, s32[4,6]{1,0:T(4,128)}, u32[]{:S(2)}) copy-start(s32[4,6]{1,0:T(4,128)} %param.12) | copy-start | bytes 292
  43.1 47.3 %all-to-all-start.1 = ((bf16[64,16,512]{2,1,0:T(8,128)(2,1)}), bf16[64,16,512]{2,1,0:T(8,128)(2,1)S(1)}, u32[]{:S(2)}, u32[]{:S(2)}) async-start(bf16[64,16,512]{2,1,0:T(8,128)(2,1)} %bitcast.132), calls=%async_computation.1 | async-start | bytes 2097152 | tf_op jit(solution)/shard_map/all_to_all | solution.py:131
  51.2 28.6 %collective-permute-start.4 = (bf16[3,512,512]{2,1,0:T(8,128)(2,1)S(1)}, bf16[3,512,512]{2,1,0:T(8,128)(2,1)}, u32[]{:S(2)}, u32[]{:S(2)}) collective-permute-start(bf16[3,512,512]{2,1,0:T(8,128)(2,1)S(1)} %copy-done), channel_id=1, source_target_pairs={{0,449},{2,451},{4,453},{6,455},{8,457},{10,459},{12,461},{14,463}... | collective-permute-start | bytes 4718600 | tf_op jit(solution)/shard_map/ppermute | solution.py:103
  61.9 23.3 %collective-permute-start.1 = (bf16[3,512,512]{2,1,0:T(8,128)(2,1)}, bf16[3,512,512]{2,1,0:T(8,128)(2,1)}, u32[]{:S(2)}, u32[]{:S(2)}) collective-permute-start(bf16[3,512,512]{2,1,0:T(8,128)(2,1)} %collective-permute-done.refs_3_), channel_id=1, source_target_pairs={{0,65},{2,67},{4,69},{6,71},{8,73},{10,75},{12,77},{14,79},{16,81}... | collective-permute-start | bytes 4718600 | tf_op jit(solution)/shard_map/ppermute | solution.py:103
  79.8 23.5 %collective-permute-start.5 = (bf16[3,512,512]{2,1,0:T(8,128)(2,1)}, bf16[3,512,512]{2,1,0:T(8,128)(2,1)}, u32[]{:S(2)}, u32[]{:S(2)}) collective-permute-start(bf16[3,512,512]{2,1,0:T(8,128)(2,1)} %collective-permute-done.4.refs_9_), channel_id=1, source_target_pairs={{0,449},{2,451},{4,453},{6,455},{8,457},{10,459},{12,461},{14,463}... | collective-permute-start | bytes 4718600 | tf_op jit(solution)/shard_map/ppermute | solution.py:103
  85.2 23.5 %collective-permute-start.2 = (bf16[3,512,512]{2,1,0:T(8,128)(2,1)}, bf16[3,512,512]{2,1,0:T(8,128)(2,1)}, u32[]{:S(2)}, u32[]{:S(2)}) collective-permute-start(bf16[3,512,512]{2,1,0:T(8,128)(2,1)} %collective-permute-done.1.refs_4_), channel_id=1, source_target_pairs={{0,65},{2,67},{4,69},{6,71},{8,73},{10,75},{12,77},{14,79},{16,81}... | collective-permute-start | bytes 4718600 | tf_op jit(solution)/shard_map/ppermute | solution.py:103
  90.4 66.1 %all-to-all-start = ((bf16[64,16,512]{2,1,0:T(8,128)(2,1)}), bf16[64,16,512]{2,1,0:T(8,128)(2,1)}, u32[]{:S(2)}, u32[]{:S(2)}) async-start(bf16[64,16,512]{2,1,0:T(8,128)(2,1)} %bitcast.133), calls=%async_computation | async-start | bytes 2097152 | tf_op jit(solution)/shard_map/all_to_all | solution.py:131
  102.9 15.9 %copy-start.34 = (bf16[4,128,8,128]{3,2,1,0:T(8,128)(2,1)}, bf16[4,128,8,128]{3,2,1,0:T(8,128)(2,1)S(1)}, u32[]{:S(2)}) copy-start(bf16[4,128,8,128]{3,2,1,0:T(8,128)(2,1)S(1)} %select_add_fusion) | copy-start | bytes 3145732
  103.4 106.3 %collective-permute-start.6 = (bf16[3,512,512]{2,1,0:T(8,128)(2,1)}, bf16[3,512,512]{2,1,0:T(8,128)(2,1)}, u32[]{:S(2)}, u32[]{:S(2)}) collective-permute-start(bf16[3,512,512]{2,1,0:T(8,128)(2,1)} %collective-permute-done.5.refs_8_), channel_id=1, source_target_pairs={{0,449},{2,451},{4,453},{6,455},{8,457},{10,459},{12,461},{14,463}... | collective-permute-start | bytes 4718600 | tf_op jit(solution)/shard_map/ppermute | solution.py:103
  108.7 101.0 %collective-permute-start.3 = (bf16[3,512,512]{2,1,0:T(8,128)(2,1)}, bf16[3,512,512]{2,1,0:T(8,128)(2,1)}, u32[]{:S(2)}, u32[]{:S(2)}) collective-permute-start(bf16[3,512,512]{2,1,0:T(8,128)(2,1)} %collective-permute-done.2.refs_5_), channel_id=1, source_target_pairs={{0,65},{2,67},{4,69},{6,71},{8,73},{10,75},{12,77},{14,79},{16,81}... | collective-permute-start | bytes 4718600 | tf_op jit(solution)/shard_map/ppermute | solution.py:103
  112.1 8.3 %collective-permute-start.27 = (bf16[128,512]{1,0:T(8,128)(2,1)S(1)}, bf16[128,512]{1,0:T(8,128)(2,1)S(1)}, u32[]{:S(2)}, u32[]{:S(2)}) collective-permute-start(bf16[128,512]{1,0:T(8,128)(2,1)S(1)} %get-tuple-element.27), channel_id=1, source_target_pairs={{1,449},{3,451},{5,453},{7,455},{9,457},{11,459},{13,461},{15,463}... | collective-permute-start | bytes 393224 | tf_op jit(solution)/shard_map/ppermute | solution.py:112
  113.4 24.6 %collective-permute-start.26 = (bf16[128,512]{1,0:T(8,128)(2,1)S(1)}, bf16[128,512]{1,0:T(8,128)(2,1)S(1)}, u32[]{:S(2)}, u32[]{:S(2)}) collective-permute-start(bf16[128,512]{1,0:T(8,128)(2,1)S(1)} %get-tuple-element.28), channel_id=1, source_target_pairs={{0,384},{2,386},{4,388},{6,390},{8,392},{10,394},{12,396},{14,398}... | collective-permute-start | bytes 393224 | tf_op jit(solution)/shard_map/ppermute | solution.py:112
  116.8 22.5 %collective-permute-start.25 = (bf16[128,512]{1,0:T(8,128)(2,1)S(1)}, bf16[128,512]{1,0:T(8,128)(2,1)S(1)}, u32[]{:S(2)}, u32[]{:S(2)}) collective-permute-start(bf16[128,512]{1,0:T(8,128)(2,1)S(1)} %get-tuple-element.29), channel_id=1, source_target_pairs={{1,321},{3,323},{5,325},{7,327},{9,329},{11,331},{13,333},{15,335}... | collective-permute-start | bytes 393224 | tf_op jit(solution)/shard_map/ppermute | solution.py:112
  120.4 22.9 %collective-permute-start.24 = (bf16[128,512]{1,0:T(8,128)(2,1)S(1)}, bf16[128,512]{1,0:T(8,128)(2,1)S(1)}, u32[]{:S(2)}, u32[]{:S(2)}) collective-permute-start(bf16[128,512]{1,0:T(8,128)(2,1)S(1)} %get-tuple-element.30), channel_id=1, source_target_pairs={{0,256},{2,258},{4,260},{6,262},{8,264},{10,266},{12,268},{14,270}... | collective-permute-start | bytes 393224 | tf_op jit(solution)/shard_map/ppermute | solution.py:112
  138.0 10.9 %collective-permute-start.23 = (bf16[128,512]{1,0:T(8,128)(2,1)S(1)}, bf16[128,512]{1,0:T(8,128)(2,1)S(1)}, u32[]{:S(2)}, u32[]{:S(2)}) collective-permute-start(bf16[128,512]{1,0:T(8,128)(2,1)S(1)} %get-tuple-element.31), channel_id=1, source_target_pairs={{1,193},{3,195},{5,197},{7,199},{9,201},{11,203},{13,205},{15,207}... | collective-permute-start | bytes 393224 | tf_op jit(solution)/shard_map/ppermute | solution.py:112
  139.3 12.0 %collective-permute-start.22 = (bf16[128,512]{1,0:T(8,128)(2,1)S(1)}, bf16[128,512]{1,0:T(8,128)(2,1)S(1)}, u32[]{:S(2)}, u32[]{:S(2)}) collective-permute-start(bf16[128,512]{1,0:T(8,128)(2,1)S(1)} %get-tuple-element.32), channel_id=1, source_target_pairs={{0,128},{2,130},{4,132},{6,134},{8,136},{10,138},{12,140},{14,142}... | collective-permute-start | bytes 393224 | tf_op jit(solution)/shard_map/ppermute | solution.py:112
  143.3 15.6 %collective-permute-start.21 = (bf16[128,512]{1,0:T(8,128)(2,1)}, bf16[128,512]{1,0:T(8,128)(2,1)S(1)}, u32[]{:S(2)}, u32[]{:S(2)}) collective-permute-start(bf16[128,512]{1,0:T(8,128)(2,1)} %get-tuple-element.33), channel_id=1, source_target_pairs={{1,65},{3,67},{5,69},{7,71},{9,73},{11,75},{13,77},{15,79},{17,81}... | collective-permute-start | bytes 393224 | tf_op jit(solution)/shard_map/ppermute | solution.py:112
  149.0 11.4 %collective-permute-start.20 = (bf16[128,512]{1,0:T(8,128)(2,1)S(1)}, bf16[128,512]{1,0:T(8,128)(2,1)S(1)}, u32[]{:S(2)}, u32[]{:S(2)}) collective-permute-start(bf16[128,512]{1,0:T(8,128)(2,1)S(1)} %get-tuple-element.35), channel_id=1, source_target_pairs={{1,449},{3,451},{5,453},{7,455},{9,457},{11,459},{13,461},{15,463}... | collective-permute-start | bytes 393224 | tf_op jit(solution)/shard_map/ppermute | solution.py:112
  152.0 12.6 %collective-permute-start.19 = (bf16[128,512]{1,0:T(8,128)(2,1)S(1)}, bf16[128,512]{1,0:T(8,128)(2,1)S(1)}, u32[]{:S(2)}, u32[]{:S(2)}) collective-permute-start(bf16[128,512]{1,0:T(8,128)(2,1)S(1)} %get-tuple-element.36), channel_id=1, source_target_pairs={{0,384},{2,386},{4,388},{6,390},{8,392},{10,394},{12,396},{14,398}... | collective-permute-start | bytes 393224 | tf_op jit(solution)/shard_map/ppermute | solution.py:112
  158.9 13.0 %copy-start.36 = (bf16[128,512]{1,0:T(8,128)(2,1)S(1)}, bf16[128,512]{1,0:T(8,128)(2,1)}, u32[]{:S(2)}) copy-start(bf16[128,512]{1,0:T(8,128)(2,1)} %get-tuple-element.41) | copy-start | bytes 393220
  158.9 50.8 %copy-start.5 = (bf16[128,512]{1,0:T(8,128)(2,1)}, bf16[128,512]{1,0:T(8,128)(2,1)S(1)}, u32[]{:S(2)}) copy-start(bf16[128,512]{1,0:T(8,128)(2,1)S(1)} %collective-permute-done.21.refs_27_) | copy-start | bytes 393220
  158.9 10.7 %collective-permute-start.18 = (bf16[128,512]{1,0:T(8,128)(2,1)S(1)}, bf16[128,512]{1,0:T(8,128)(2,1)S(1)}, u32[]{:S(2)}, u32[]{:S(2)}) collective-permute-start(bf16[128,512]{1,0:T(8,128)(2,1)S(1)} %get-tuple-element.37), channel_id=1, source_target_pairs={{1,321},{3,323},{5,325},{7,327},{9,329},{11,331},{13,333},{15,335}... | collective-permute-start | bytes 393224 | tf_op jit(solution)/shard_map/ppermute | solution.py:112
  160.4 49.3 %copy-start.7 = (bf16[128,512]{1,0:T(8,128)(2,1)}, bf16[128,512]{1,0:T(8,128)(2,1)S(1)}, u32[]{:S(2)}) copy-start(bf16[128,512]{1,0:T(8,128)(2,1)S(1)} %collective-permute-done.20.refs_25_) | copy-start | bytes 393220
  160.4 11.5 %collective-permute-start.17 = (bf16[128,512]{1,0:T(8,128)(2,1)S(1)}, bf16[128,512]{1,0:T(8,128)(2,1)S(1)}, u32[]{:S(2)}, u32[]{:S(2)}) collective-permute-start(bf16[128,512]{1,0:T(8,128)(2,1)S(1)} %get-tuple-element.38), channel_id=1, source_target_pairs={{0,256},{2,258},{4,260},{6,262},{8,264},{10,266},{12,268},{14,270}... | collective-permute-start | bytes 393224 | tf_op jit(solution)/shard_map/ppermute | solution.py:112
  164.6 45.1 %copy-start.9 = (bf16[128,512]{1,0:T(8,128)(2,1)}, bf16[128,512]{1,0:T(8,128)(2,1)S(1)}, u32[]{:S(2)}) copy-start(bf16[128,512]{1,0:T(8,128)(2,1)S(1)} %collective-permute-done.19.refs_24_) | copy-start | bytes 393220
  164.6 10.5 %collective-permute-start.16 = (bf16[128,512]{1,0:T(8,128)(2,1)}, bf16[128,512]{1,0:T(8,128)(2,1)S(1)}, u32[]{:S(2)}, u32[]{:S(2)}) collective-permute-start(bf16[128,512]{1,0:T(8,128)(2,1)} %get-tuple-element.39), channel_id=1, source_target_pairs={{1,193},{3,195},{5,197},{7,199},{9,201},{11,203},{13,205},{15,207}... | collective-permute-start | bytes 393224 | tf_op jit(solution)/shard_map/ppermute | solution.py:112
  169.6 40.1 %copy-start.11 = (bf16[128,512]{1,0:T(8,128)(2,1)}, bf16[128,512]{1,0:T(8,128)(2,1)S(1)}, u32[]{:S(2)}) copy-start(bf16[128,512]{1,0:T(8,128)(2,1)S(1)} %collective-permute-done.18.refs_23_) | copy-start | bytes 393220
  169.6 9.2 %collective-permute-start.15 = (bf16[128,512]{1,0:T(8,128)(2,1)}, bf16[128,512]{1,0:T(8,128)(2,1)S(1)}, u32[]{:S(2)}, u32[]{:S(2)}) collective-permute-start(bf16[128,512]{1,0:T(8,128)(2,1)} %get-tuple-element.40), channel_id=1, source_target_pairs={{0,128},{2,130},{4,132},{6,134},{8,136},{10,138},{12,140},{14,142}... | collective-permute-start | bytes 393224 | tf_op jit(solution)/shard_map/ppermute | solution.py:112
  171.9 37.9 %copy-start.13 = (bf16[128,512]{1,0:T(8,128)(2,1)}, bf16[128,512]{1,0:T(8,128)(2,1)S(1)}, u32[]{:S(2)}) copy-start(bf16[128,512]{1,0:T(8,128)(2,1)S(1)} %collective-permute-done.17.refs_22_) | copy-start | bytes 393220
  171.9 13.7 %collective-permute-start.14 = (bf16[128,512]{1,0:T(8,128)(2,1)S(1)}, bf16[128,512]{1,0:T(8,128)(2,1)S(1)}, u32[]{:S(2)}, u32[]{:S(2)}) collective-permute-start(bf16[128,512]{1,0:T(8,128)(2,1)S(1)} %copy-done.36), channel_id=1, source_target_pairs={{1,65},{3,67},{5,69},{7,71},{9,73},{11,75},{13,77},{15,79},{17,81}... | collective-permute-start | bytes 393224 | tf_op jit(solution)/shard_map/ppermute | solution.py:112
  175.0 34.7 %copy-start.15 = (bf16[128,512]{1,0:T(8,128)(2,1)}, bf16[128,512]{1,0:T(8,128)(2,1)S(1)}, u32[]{:S(2)}) copy-start(bf16[128,512]{1,0:T(8,128)(2,1)S(1)} %collective-permute-done.16.refs_21_) | copy-start | bytes 393220
  175.0 12.5 %collective-permute-start.13 = (bf16[128,512]{1,0:T(8,128)(2,1)S(1)}, bf16[128,512]{1,0:T(8,128)(2,1)S(1)}, u32[]{:S(2)}, u32[]{:S(2)}) collective-permute-start(bf16[128,512]{1,0:T(8,128)(2,1)S(1)} %get-tuple-element.43), channel_id=1, source_target_pairs={{1,449},{3,451},{5,453},{7,455},{9,457},{11,459},{13,461},{15,463}... | collective-permute-start | bytes 393224 | tf_op jit(solution)/shard_map/ppermute | solution.py:112
  179.4 13.6 %collective-permute-start.12 = (bf16[128,512]{1,0:T(8,128)(2,1)}, bf16[128,512]{1,0:T(8,128)(2,1)S(1)}, u32[]{:S(2)}, u32[]{:S(2)}) collective-permute-start(bf16[128,512]{1,0:T(8,128)(2,1)} %get-tuple-element.44), channel_id=1, source_target_pairs={{0,384},{2,386},{4,388},{6,390},{8,392},{10,394},{12,396},{14,398}... | collective-permute-start | bytes 393224 | tf_op jit(solution)/shard_map/ppermute | solution.py:112
  186.3 9.6 %collective-permute-start.11 = (bf16[128,512]{1,0:T(8,128)(2,1)}, bf16[128,512]{1,0:T(8,128)(2,1)S(1)}, u32[]{:S(2)}, u32[]{:S(2)}) collective-permute-start(bf16[128,512]{1,0:T(8,128)(2,1)} %get-tuple-element.45), channel_id=1, source_target_pairs={{1,321},{3,323},{5,325},{7,327},{9,329},{11,331},{13,333},{15,335}... | collective-permute-start | bytes 393224 | tf_op jit(solution)/shard_map/ppermute | solution.py:112
  188.2 13.1 %collective-permute-start.10 = (bf16[128,512]{1,0:T(8,128)(2,1)}, bf16[128,512]{1,0:T(8,128)(2,1)}, u32[]{:S(2)}, u32[]{:S(2)}) collective-permute-start(bf16[128,512]{1,0:T(8,128)(2,1)} %get-tuple-element.46), channel_id=1, source_target_pairs={{0,256},{2,258},{4,260},{6,262},{8,264},{10,266},{12,268},{14,270}... | collective-permute-start | bytes 393224 | tf_op jit(solution)/shard_map/ppermute | solution.py:112
  193.7 11.2 %collective-permute-start.9 = (bf16[128,512]{1,0:T(8,128)(2,1)}, bf16[128,512]{1,0:T(8,128)(2,1)S(1)}, u32[]{:S(2)}, u32[]{:S(2)}) collective-permute-start(bf16[128,512]{1,0:T(8,128)(2,1)} %get-tuple-element.47), channel_id=1, source_target_pairs={{1,193},{3,195},{5,197},{7,199},{9,201},{11,203},{13,205},{15,207}... | collective-permute-start | bytes 393224 | tf_op jit(solution)/shard_map/ppermute | solution.py:112
  196.5 9.4 %collective-permute-start.8 = (bf16[128,512]{1,0:T(8,128)(2,1)}, bf16[128,512]{1,0:T(8,128)(2,1)S(1)}, u32[]{:S(2)}, u32[]{:S(2)}) collective-permute-start(bf16[128,512]{1,0:T(8,128)(2,1)} %get-tuple-element.48), channel_id=1, source_target_pairs={{0,128},{2,130},{4,132},{6,134},{8,136},{10,138},{12,140},{14,142}... | collective-permute-start | bytes 393224 | tf_op jit(solution)/shard_map/ppermute | solution.py:112
  201.3 8.4 %collective-permute-start.7 = (bf16[128,512]{1,0:T(8,128)(2,1)}, bf16[128,512]{1,0:T(8,128)(2,1)}, u32[]{:S(2)}, u32[]{:S(2)}) collective-permute-start(bf16[128,512]{1,0:T(8,128)(2,1)} %get-tuple-element.49), channel_id=1, source_target_pairs={{1,65},{3,67},{5,69},{7,71},{9,73},{11,75},{13,77},{15,79},{17,81}... | collective-permute-start | bytes 393224 | tf_op jit(solution)/shard_map/ppermute | solution.py:112
  237.8 13.6 %collective-permute-start.34 = (bf16[128,512]{1,0:T(8,128)(2,1)S(1)}, bf16[128,512]{1,0:T(8,128)(2,1)S(1)}, u32[]{:S(2)}, u32[]{:S(2)}) collective-permute-start(bf16[128,512]{1,0:T(8,128)(2,1)S(1)} %get-tuple-element.11), channel_id=1, source_target_pairs={{0,448},{2,450},{4,452},{6,454},{8,456},{10,458},{12,460},{14,462}... | collective-permute-start | bytes 393224 | tf_op jit(solution)/shard_map/ppermute | solution.py:121
  240.7 12.1 %collective-permute-start.33 = (bf16[128,512]{1,0:T(8,128)(2,1)S(1)}, bf16[128,512]{1,0:T(8,128)(2,1)S(1)}, u32[]{:S(2)}, u32[]{:S(2)}) collective-permute-start(bf16[128,512]{1,0:T(8,128)(2,1)S(1)} %get-tuple-element.12), channel_id=1, source_target_pairs={{0,384},{2,386},{4,388},{6,390},{8,392},{10,394},{12,396},{14,398}... | collective-permute-start | bytes 393224 | tf_op jit(solution)/shard_map/ppermute | solution.py:121
  243.1 14.8 %collective-permute-start.28 = (bf16[128,512]{1,0:T(8,128)(2,1)S(1)}, bf16[128,512]{1,0:T(8,128)(2,1)S(1)}, u32[]{:S(2)}, u32[]{:S(2)}) collective-permute-start(bf16[128,512]{1,0:T(8,128)(2,1)S(1)} %get-tuple-element.10), channel_id=1, source_target_pairs={{0,64},{2,66},{4,68},{6,70},{8,72},{10,74},{12,76},{14,78},{16,80}... | collective-permute-start | bytes 393224 | tf_op jit(solution)/shard_map/ppermute | solution.py:121
  244.4 12.2 %collective-permute-start.32 = (bf16[128,512]{1,0:T(8,128)(2,1)S(1)}, bf16[128,512]{1,0:T(8,128)(2,1)S(1)}, u32[]{:S(2)}, u32[]{:S(2)}) collective-permute-start(bf16[128,512]{1,0:T(8,128)(2,1)S(1)} %get-tuple-element.13), channel_id=1, source_target_pairs={{0,320},{2,322},{4,324},{6,326},{8,328},{10,330},{12,332},{14,334}... | collective-permute-start | bytes 393224 | tf_op jit(solution)/shard_map/ppermute | solution.py:121
  245.7 12.2 %collective-permute-start.31 = (bf16[128,512]{1,0:T(8,128)(2,1)S(1)}, bf16[128,512]{1,0:T(8,128)(2,1)S(1)}, u32[]{:S(2)}, u32[]{:S(2)}) collective-permute-start(bf16[128,512]{1,0:T(8,128)(2,1)S(1)} %get-tuple-element.14), channel_id=1, source_target_pairs={{0,256},{2,258},{4,260},{6,262},{8,264},{10,266},{12,268},{14,270}... | collective-permute-start | bytes 393224 | tf_op jit(solution)/shard_map/ppermute | solution.py:121
  251.4 6.6 %collective-permute-start.30 = (bf16[128,512]{1,0:T(8,128)(2,1)S(1)}, bf16[128,512]{1,0:T(8,128)(2,1)S(1)}, u32[]{:S(2)}, u32[]{:S(2)}) collective-permute-start(bf16[128,512]{1,0:T(8,128)(2,1)S(1)} %get-tuple-element.15), channel_id=1, source_target_pairs={{0,192},{2,194},{4,196},{6,198},{8,200},{10,202},{12,204},{14,206}... | collective-permute-start | bytes 393224 | tf_op jit(solution)/shard_map/ppermute | solution.py:121
  252.7 10.6 %collective-permute-start.29 = (bf16[128,512]{1,0:T(8,128)(2,1)S(1)}, bf16[128,512]{1,0:T(8,128)(2,1)S(1)}, u32[]{:S(2)}, u32[]{:S(2)}) collective-permute-start(bf16[128,512]{1,0:T(8,128)(2,1)S(1)} %get-tuple-element.16), channel_id=1, source_target_pairs={{0,128},{2,130},{4,132},{6,134},{8,136},{10,138},{12,140},{14,142}... | collective-permute-start | bytes 393224 | tf_op jit(solution)/shard_map/ppermute | solution.py:121
  (29 other events, 60.0 us)

commit v2 on v0

v2 whole, which is shorter than its diff:
```python
import jax
import jax.numpy as jnp
import numpy as np
from jax import lax
from jax.experimental import pallas as pl
from jax.experimental.pallas import tpu as pltpu
from jax.sharding import Mesh, PartitionSpec as P

HALVES = 2
STAGES = 4
CORES = 2
SEGMENT = ("half", "stage")
DOM = ("pair", "core")
PIECES = ((0, 1), (2,))
ANYWHERE = pl.BlockSpec(memory_space=pl.ANY)
VMEM = pl.BlockSpec(memory_space=pltpu.VMEM)


def tile_of(slot):
    mirror = lax.axis_index("half") * (STAGES - 1)
    return lax.axis_index("stage") ^ mirror ^ slot


def exchange(block, slot):
    if slot == 0:
        return block
    return lax.ppermute(block, "stage", [(u, u ^ slot) for u in range(STAGES)])


def pick_kernel(levels, wanted_ref, history_ref, out_ref):
    rows = history_ref.shape[1]
    receivers, _, slots, width = out_ref.shape
    wanted = wanted_ref[...]
    column = lax.broadcasted_iota(jnp.int32, (receivers * slots, rows), 1)
    pick = jnp.where(wanted == column, 1.0, 0.0).astype(jnp.bfloat16)
    for place, i in enumerate(levels):
        got = jnp.dot(pick, history_ref[i], preferred_element_type=jnp.float32)
        out_ref[:, place] = got.astype(jnp.bfloat16).reshape(receivers, slots, width)


def pick_rows(levels, wanted, history, parts, slots):
    width = history.shape[2]
    step = 16
    return pl.pallas_call(
        lambda *refs: pick_kernel(levels, *refs),
        out_shape=jax.ShapeDtypeStruct((parts, len(levels), slots, width), jnp.bfloat16),
        grid=(parts // step,),
        in_specs=[
            pl.BlockSpec((step * slots, 1), lambda g: (g, 0)),
            pl.BlockSpec(history.shape, lambda g: (0, 0, 0)),
        ],
        out_specs=pl.BlockSpec((step, len(levels), slots, width), lambda g: (g, 0, 0, 0)),
        compiler_params=pltpu.CompilerParams(vmem_limit_bytes=24 * 1024 * 1024),
        cost_estimate=pl.CostEstimate(
            flops=2 * len(levels) * parts * slots * history.shape[1] * width,
            bytes_accessed=2 * (len(levels) * parts * slots * width + history.size),
            transcendentals=0,
        ),
    )(wanted, history)


def halo_kernel(levels, arrived_ref, spread_ref, features_ref, *out_refs):
    parts, _, slots, width = arrived_ref.shape
    tiles, rows, _ = spread_ref.shape
    spread = jnp.concatenate([spread_ref[tile_of(r)] for r in range(tiles)], axis=0)
    for place in range(levels):
        halo = arrived_ref[:, place].reshape(parts * slots, width)
        summed = jnp.dot(spread, halo, preferred_element_type=jnp.float32)
        for r in range(tiles):
            start = 0.1 * features_ref[tile_of(r)].astype(jnp.float32)
            part = 0.9 * summed[r * rows : (r + 1) * rows] + start
            out_refs[r][place] = part.astype(jnp.bfloat16)


def halo_sums(arrived, spread, features):
    parts, levels, slots, width = arrived.shape
    tiles, rows, halo_rows = spread.shape
    return pl.pallas_call(
        lambda *refs: halo_kernel(levels, *refs),
        out_shape=[jax.ShapeDtypeStruct((levels, rows, width), jnp.bfloat16)] * tiles,
        in_specs=[VMEM] * 3,
        out_specs=[VMEM] * tiles,
        compiler_params=pltpu.CompilerParams(vmem_limit_bytes=24 * 1024 * 1024),
        cost_estimate=pl.CostEstimate(
            flops=2 * levels * tiles * rows * halo_rows * width,
            bytes_accessed=2 * (arrived.size + spread.size + features.size * (1 + levels)),
            transcendentals=0,
        ),
    )(arrived, spread, features)


def chain_kernel(which, betas, x_ref, a_ref, w_ref, *refs):
    stages, cores, levels, depth, width = w_ref.shape
    pieces = len(PIECES)
    h_refs = refs[: pieces * stages]
    refs = refs[pieces * stages :]
    if which > 0:
        before_refs, refs = refs[:stages], refs[stages:]
        out_refs, refs = refs[:stages], refs[stages:]
    else:
        out_refs, last_ref, refs = refs[:stages], refs[stages], refs[stages + 1 :]
    w_buf, w_sem, h_sem = refs[:3]
    h_bufs = refs[3:]
    half = lax.axis_index("half")
    stage = lax.axis_index("stage")

    @pl.when(half == which)
    def _():
        def w_copy(s, c):
            return pltpu.make_async_copy(
                w_ref.at[s, c], w_buf.at[s, :, pl.ds(c * depth, depth)], w_sem.at[s, c]
            )

        def h_copy(p, r, s):
            return pltpu.make_async_copy(
                h_refs[p * stages + r], h_bufs[p].at[s], h_sem.at[p, s]
            )

        for r in range(stages):
            for p in range(pieces):
                h_copy(p, r, stage ^ r).start()
        for s in range(stages):
            for c in range(cores):
                w_copy(s, c).start()

        a = a_ref[...]
        x = x_ref[...]
        for s in range(stages):
            for p in range(pieces):
                h_copy(p, 0, s).wait()
            for c in range(cores):
                w_copy(s, c).wait()
            for p, chosen in enumerate(PIECES):
                for place, i in enumerate(chosen):
                    beta = betas[(which * stages + s) * levels + i]
                    summed = jnp.dot(a, x, preferred_element_type=jnp.float32)
                    support = 0.9 * summed + h_bufs[p][s, place].astype(jnp.float32)
                    branch = jnp.dot(
                        support.astype(jnp.bfloat16),
                        w_buf[s, i],
                        preferred_element_type=jnp.float32,
                    )
                    mixed = (1.0 - beta) * support + beta * branch
                    x = jnp.maximum(mixed, 0.0).astype(jnp.bfloat16)
            for r in range(stages):

                @pl.when(stage ^ s == r)
                def _():
                    out_refs[r][...] = x

        if which == 0:
            last_ref[...] = x

    @pl.when(half != which)
    def _():
        if which == 0:
            last_ref[...] = jnp.zeros_like(last_ref)
        for r in range(stages):
            out_refs[r][...] = before_refs[r][...] if which > 0 else jnp.zeros_like(out_refs[r])


def chain(which, x, a, weights, halos, before=()):
    stages, cores, levels, depth, width = weights.shape
    rows = x.shape[0]
    order = np.arange(HALVES * stages * levels, dtype=np.float32)
    betas = [float(b) for b in np.log1p(np.float32(1.0) / (order + np.float32(1.0)))]
    flat = [h for piece in halos for h in piece]
    outs = stages if before else stages + 1
    return pl.pallas_call(
        lambda *refs: chain_kernel(which, betas, *refs),
        out_shape=[jax.ShapeDtypeStruct((rows, width), jnp.bfloat16)] * outs,
        in_specs=[VMEM, VMEM, ANYWHERE] + [ANYWHERE] * len(flat) + [VMEM] * len(before),
        out_specs=[VMEM] * outs,
        scratch_shapes=[
            pltpu.VMEM((stages, levels, cores * depth, width), jnp.bfloat16),
            pltpu.SemaphoreType.DMA((stages, cores)),
            pltpu.SemaphoreType.DMA((len(halos), stages)),
        ]
        + [pltpu.VMEM((stages,) + piece[0].shape, jnp.bfloat16) for piece in halos],
        compiler_params=pltpu.CompilerParams(vmem_limit_bytes=60 * 1024 * 1024),
        cost_estimate=pl.CostEstimate(
            flops=2 * stages * levels * rows * width * (width + rows),
            bytes_accessed=2 * stages * levels * width * (width + rows),
            transcendentals=0,
        ),
    )(x, a, weights, *flat, *before)


def place_kernel(*refs):
    in_refs, out_ref, sem = refs[:-2], refs[-2], refs[-1]
    copies = [
        pltpu.make_async_copy(ref, out_ref.at[0, tile_of(r)], sem.at[r])
        for r, ref in enumerate(in_refs)
    ]
    for copy in copies:
        copy.start()
    for copy in copies:
        copy.wait()


def place(tiles):
    rows, width = tiles[0].shape
    return pl.pallas_call(
        place_kernel,
        out_shape=jax.ShapeDtypeStruct((1, len(tiles), rows, width), jnp.bfloat16),
        in_specs=[ANYWHERE] * len(tiles),
        out_specs=ANYWHERE,
        scratch_shapes=[pltpu.SemaphoreType.DMA((len(tiles),))],
    )(*tiles)


def local(features, history, weights, send_rows, send_count, adj_src, adj_blocks):
    rows_dev, width = features.shape
    levels = weights.shape[0]
    tile_rows = adj_blocks.shape[2]
    parts, slots = send_rows.shape[1:]
    halo_rows = parts * slots
    halo_tiles = halo_rows // tile_rows
    core = lax.axis_index("core")
    tiles = features.reshape(STAGES, tile_rows, width)

    depth = width // CORES
    own = lax.dynamic_slice_in_dim(weights, core * depth, depth, 1)
    group = lax.all_gather(own, ("stage", "core")).reshape(STAGES, CORES, levels, depth, width)

    live = jnp.arange(slots)[None, :] < send_count[0][:, None]
    wanted = jnp.where(live, send_rows[0], -1).reshape(halo_rows, 1)

    spread = sum(
        jnp.where(
            (adj_src[:, k, None] - 1 == jnp.arange(halo_tiles)[None, :])[:, None, :, None],
            adj_blocks[:, k, :, None, :],
            jnp.zeros((), jnp.bfloat16),
        )
        for k in range(1, adj_src.shape[1])
    ).reshape(STAGES, tile_rows, halo_rows)

    halos = []
    arrived = None
    for chosen in PIECES:
        outgoing = pick_rows(chosen, wanted, history, parts, slots)
        if arrived is not None:
            outgoing, arrived = lax.optimization_barrier((outgoing, arrived))
        following = lax.all_to_all(outgoing, DOM, split_axis=0, concat_axis=0, tiled=True)
        if arrived is not None:
            sums = halo_sums(arrived, spread, tiles)
            halos.append([exchange(block, r) for r, block in enumerate(sums)])
        arrived = following
    sums = halo_sums(arrived, spread, tiles)
    halos.append([exchange(block, r) for r, block in enumerate(sums)])

    own_tile = tile_of(0)
    x = lax.dynamic_index_in_dim(tiles, own_tile, 0, keepdims=False)
    a = lax.dynamic_index_in_dim(adj_blocks[:, 0], own_tile, 0, keepdims=False)
    *first, last = chain(0, x, a, group, halos)
    mirror = [(s, HALVES * STAGES - 1 - s) for s in range(STAGES)]
    done = chain(1, lax.ppermute(last, SEGMENT, mirror), a, group, halos, first)
    fresh = place([exchange(block, r) for r, block in enumerate(done)])
    return fresh.reshape(1, rows_dev, width)


def solution(mesh):
    segments, parts = mesh.devices.shape
    devices = mesh.devices.reshape(HALVES, segments // HALVES, parts // CORES, CORES)
    fine = Mesh(devices, SEGMENT + DOM)
    placed = (
        P(DOM, None),
        P(SEGMENT, DOM, None),
        P(SEGMENT, None, None),
        P(DOM, None, None),
        P(DOM, None),
        P(DOM, None),
        P(DOM, None, None, None),
    )
    return jax.shard_map(
        local, mesh=fine, in_specs=placed, out_specs=P(SEGMENT, DOM, None), check_vma=False
    )
```

time: 455 us -> 218 us (0.48); the launches traced: 446 us -> 214 us
  matrix products: 119 us -> 0 us
  local copies, waits for them, and re-layouts: 114 us -> 34.1 us
  other arithmetic: 53.8 us -> 5.1 us
  Pallas kernels: 0 us -> 34.4 us
  waiting for transfers between devices: 92.4 us -> 72.7 us
  between operations: 2.84 us -> 13.8 us
  starting transfers between devices: 63.1 us -> 54.1 us
    dot_general x66 -> x0, matrix products: 119 us -> none  [the longest x33 71 us: local(): jnp.dot(support.astype(jnp.bfloat16), weights[layer_pos], preferred_eleme...]
    gather x34 -> x0, local copies, waits for them, and re-layouts: 109 us -> none  [the longest x33 91.4 us: local(): sources[source_ids]]
    concatenate x33 -> x0, other arithmetic: 38 us -> none  [local(): sources = jnp.concatenate([local_tiles, halo_tiles[layer_pos]], axis=0)]
    pallas_call x0 -> x7, Pallas kernels: none -> 34.4 us  [the longest x1 17 us: place(): pl.pallas_call(place_kernel, out_shape=jax.ShapeDtypeStruct((1, len(tiles...]
    all_to_all x1 -> x2, waiting for transfers between devices: 67.7 us -> 44.4 us  [local(): lax.all_to_all(outgoing, DOM, split_axis=0, concat_axis=0, tiled=True)]
    broadcast_in_dim x1 -> x11, local copies, waits for them, and re-layouts: 0.83 us -> 17.9 us  [local(): jnp.where((adj_src[:, k, None] - 1 == jnp.arange(halo_tiles)[None, :])[:,...]
    ppermute x10, starting transfers between devices: 51.8 us -> 34.7 us  [the longest x9 32.5 us: exchange(): return lax.ppermute(block, 'stage', [(u, u ^ slot) for u in range(STAGES)])]
    reshape x11 -> x0, other arithmetic: 10.3 us -> none  [local(): local_tiles = hidden.reshape(batch_tiles, tile_rows, feature_width)]
  transfers between devices with their start and end apart: 11 -> 13, of which waited for: 11 -> 6; matrix products, arithmetic and copies ran while one was open for 1% -> 13% of each run, Pallas kernels for 0% -> 4%
where the time goes in v2:
time: 218 us; the launch traced here: 214 us
  waiting for transfers between devices  72.7 us (33%)
  starting transfers between devices  54.1 us (25%)
  Pallas kernels  34.4 us (16%)
  local copies, waits for them, and re-layouts  34.1 us (16%)
  between operations  13.8 us (6%)
  other arithmetic  5.1 us (2%)
    all_to_all x2, waiting for transfers between devices, local(): lax.all_to_all(outgoing, DOM, split_axis=0, concat_axis=0, tiled=True)  44.4 us
    ppermute x9, starting transfers between devices, exchange(): return lax.ppermute(block, 'stage', [(u, u ^ slot) for u in range(STAGES)])  32.5 us
    ppermute x9, waiting for transfers between devices, exchange(): return lax.ppermute(block, 'stage', [(u, u ^ slot) for u in range(STAGES)])  23.6 us
    all_to_all x2, starting transfers between devices, local(): lax.all_to_all(outgoing, DOM, split_axis=0, concat_axis=0, tiled=True)  19.3 us
    broadcast_in_dim x11, local copies, waits for them, and re-layouts, local(): jnp.where((adj_src[:, k, None] - 1 == jnp.arange(halo_tiles)[None, :])[:,...  17.9 us
    pallas_call x1, Pallas kernels, place(): pl.pallas_call(place_kernel, out_shape=jax.ShapeDtypeStruct((1, len(tiles...  17 us
    unnamed x65, local copies, waits for them, and re-layouts  11.7 us
    pallas_call x2, Pallas kernels, chain(): pl.pallas_call(lambda *refs: chain_kernel(which, betas, *refs), out_shape...  9.76 us
  transfers between devices with their start and end apart: 13, of which 6 were waited for; matrix products, arithmetic and copies ran while one was open for 13% of the time, Pallas kernels for 4%

profile of v2, /device:TPU:6, one launch (start us, length us, event | category | flops | bytes accessed | tf_op | source)
XLA Modules:
  0.0 214.0 jit_solution(2261207091538605213)
XLA Ops:
  6.6 1.4 copy-done
  7.9 0.9 constant_dynamic-slice_fusion
  9.0 1.1 squeeze.15
  10.5 1.1 broadcast_select_fusion.refs_0_
  11.6 2.0 shard_map.74
  13.6 1.4 copy-done.1
  15.0 0.8 copy-done.3
  15.8 11.2 %all-to-all-start = ((bf16[64,2,16,512]{3,2,1,0:T(8,128)(2,1)}), bf16[64,2,16,512]{3,2,1,0:T(8,128)(2,1)}, u32[]{:S(2)}, u32[]{:S(2)}) async-start(bf16[64,2,16,512]{3,2,1,0:T(8,128)(2,1)} %copy-done.1), calls=%async_computation | async-start | bytes 4194304 | tf_op jit(solution)/shard_map/all_to_all | solution.py:244
  27.0 0.7 add_reduce_fusion.4
  28.0 1.1 copy-done.4
  29.1 1.4 shard_map.73
  30.5 1.0 copy-done.5
  31.4 44.4 %all-to-all-done.refs_0_ = bf16[64,2,16,512]{3,2,1,0:T(8,128)(2,1)} async-done(((bf16[64,2,16,512]{3,2,1,0:T(8,128)(2,1)}), bf16[64,2,16,512]{3,2,1,0:T(8,128)(2,1)}, u32[]{:S(2)}, u32[]{:S(2)}) %all-to-all-start) | async-done | bytes 2097184 | tf_op jit(solution)/shard_map/all_to_all | solution.py:244
  75.9 8.1 %all-to-all-start.1 = ((bf16[64,1,16,512]{3,2,1,0:T(8,128)(2,1)}), bf16[64,1,16,512]{3,2,1,0:T(8,128)(2,1)S(1)}, u32[]{:S(2)}, u32[]{:S(2)}) async-start(bf16[64,1,16,512]{3,2,1,0:T(8,128)(2,1)} %copy-done.5), calls=%async_computation.1 | async-start | bytes 2097152 | tf_op jit(solution)/shard_map/all_to_all | solution.py:244
  84.3 0.8 slice_bitcast_fusion.4
  85.1 1.1 broadcast_in_dim.124
  86.2 2.3 %broadcast_in_dim.125 = bf16[4,128,1024]{2,1,0:T(8,128)(2,1)} reshape(bf16[4,128,8,128]{3,2,1,0:T(8,128)(2,1)} %broadcast_in_dim.124) | data formatting | bytes 2097152 | tf_op jit(solution)/shard_map/jit(_where)/broadcast_in_dim | solution.py:230
  88.5 1.2 broadcast_in_dim.131
  89.6 2.3 %broadcast_in_dim.132 = bf16[4,128,1024]{2,1,0:T(8,128)(2,1)} reshape(bf16[4,128,8,128]{3,2,1,0:T(8,128)(2,1)} %broadcast_in_dim.131) | data formatting | bytes 2097152 | tf_op jit(solution)/shard_map/jit(_where)/broadcast_in_dim | solution.py:230
  91.9 1.1 broadcast_in_dim.137
  93.1 2.3 %broadcast_in_dim.138 = bf16[4,128,1024]{2,1,0:T(8,128)(2,1)} reshape(bf16[4,128,8,128]{3,2,1,0:T(8,128)(2,1)} %broadcast_in_dim.137) | data formatting | bytes 2097152 | tf_op jit(solution)/shard_map/jit(_where)/broadcast_in_dim | solution.py:230
  95.4 1.1 broadcast_in_dim.143
  96.5 2.3 %broadcast_in_dim.144 = bf16[4,128,1024]{2,1,0:T(8,128)(2,1)} reshape(bf16[4,128,8,128]{3,2,1,0:T(8,128)(2,1)} %broadcast_in_dim.143) | data formatting | bytes 2097152 | tf_op jit(solution)/shard_map/jit(_where)/broadcast_in_dim | solution.py:230
  98.8 1.1 broadcast_in_dim.149
  99.9 2.3 %broadcast_in_dim.150 = bf16[4,128,1024]{2,1,0:T(8,128)(2,1)} reshape(bf16[4,128,8,128]{3,2,1,0:T(8,128)(2,1)} %broadcast_in_dim.149) | data formatting | bytes 2097152 | tf_op jit(solution)/shard_map/jit(_where)/broadcast_in_dim | solution.py:230
  102.4 3.0 %select_add_fusion.refs_1_ = bf16[4,128,1024]{2,1,0:T(8,128)(2,1)S(1)} fusion(bf16[4,128,1024]{2,1,0:T(8,128)(2,1)} %broadcast_in_dim.150, bf16[4,128,1024]{2,1,0:T(8,128)(2,1)} %broadcast_in_dim.144, bf16[4,128,1024]{2,1,0:T(8,128)(2,1)} %broadcast_in_dim.138, bf16[4,128,1024]{2,1,0:T(8,128)(2,1)} %broadcast_in_dim.132, ...), kind=kLoop, calls=%fused_computation | loop fusion | flops 4718592 | bytes 6311936 | tf_op jit(solution)/shard_map/add | solution.py:229
  105.4 3.5 %shard_map.75 = (bf16[2,128,512]{2,1,0:T(8,128)(2,1)S(1)}, bf16[2,128,512]{2,1,0:T(8,128)(2,1)}, bf16[2,128,512]{2,1,0:T(8,128)(2,1)S(1)}, bf16[2,128,512]{2,1,0:T(8,128)(2,1)S(1)}) custom-call(bf16[64,2,16,512]{3,2,1,0:T(8,128)(2,1)} %all-to-all-done.refs_0_, bf16[4,128,1024]{2,1,0:T(8,128)(2,1)S(1)} %select_add_fusion.refs_1_, ...), custom_call_target="tpu_custom_call" | custom-call | flops 1073741824 | bytes 4718592 | tf_op jit(solution)/shard_map/pallas_call | solution.py:78
  108.9 1.0 copy-done.6
  111.3 4.2 %collective-permute-start = (bf16[2,128,512]{2,1,0:T(8,128)(2,1)}, bf16[2,128,512]{2,1,0:T(8,128)(2,1)}, u32[]{:S(2)}, u32[]{:S(2)}) collective-permute-start(bf16[2,128,512]{2,1,0:T(8,128)(2,1)} %get-tuple-element.26), channel_id=1, source_target_pairs={{0,64},{64,0},{128,192},{192,128},{1,65},{65,1},{129,193},{193,129... | collective-permute-start | bytes 786440 | tf_op jit(solution)/shard_map/ppermute | solution.py:27
  115.5 6.1 %collective-permute-start.1 = (bf16[2,128,512]{2,1,0:T(8,128)(2,1)}, bf16[2,128,512]{2,1,0:T(8,128)(2,1)}, u32[]{:S(2)}, u32[]{:S(2)}) collective-permute-start(bf16[2,128,512]{2,1,0:T(8,128)(2,1)} %copy-done.11), channel_id=1, source_target_pairs={{0,128},{64,192},{128,0},{192,64},{1,129},{65,193},{129,1},{193,65... | collective-permute-start | bytes 786440 | tf_op jit(solution)/shard_map/ppermute | solution.py:27
  121.5 1.9 collective-permute-start.2
  123.5 1.2 copy-done.7
  125.4 2.5 %collective-permute-start.3 = (bf16[1,128,512]{2,1,0:T(8,128)(2,1)S(1)}, bf16[1,128,512]{2,1,0:T(8,128)(2,1)S(1)}, u32[]{:S(2)}, u32[]{:S(2)}) collective-permute-start(bf16[1,128,512]{2,1,0:T(8,128)(2,1)S(1)} %get-tuple-element.31), channel_id=1, source_target_pairs={{0,64},{64,0},{128,192},{192,128},{1,65},{65,1},{129,193},{193,129... | collective-permute-start | bytes 393224 | tf_op jit(solution)/shard_map/ppermute | solution.py:27
  127.9 5.7 %collective-permute-start.4 = (bf16[1,128,512]{2,1,0:T(8,128)(2,1)S(1)}, bf16[1,128,512]{2,1,0:T(8,128)(2,1)S(1)}, u32[]{:S(2)}, u32[]{:S(2)}) collective-permute-start(bf16[1,128,512]{2,1,0:T(8,128)(2,1)S(1)} %get-tuple-element.32), channel_id=1, source_target_pairs={{0,128},{64,192},{128,0},{192,64},{1,129},{65,193},{129,1},{193,65... | collective-permute-start | bytes 393224 | tf_op jit(solution)/shard_map/ppermute | solution.py:27
  133.7 1.9 collective-permute-start.5
  135.6 1.4 dynamic-slice_bitcast_fusion.1.refs_1_
  137.6 8.3 %collective-permute-done.1.refs_5_ = bf16[2,128,512]{2,1,0:T(8,128)(2,1)} collective-permute-done((bf16[2,128,512]{2,1,0:T(8,128)(2,1)}, bf16[2,128,512]{2,1,0:T(8,128)(2,1)}, u32[]{:S(2)}, u32[]{:S(2)}) %collective-permute-start.1) | collective-permute-done | bytes 262176 | tf_op jit(solution)/shard_map/ppermute | solution.py:27
  145.9 8.3 %collective-permute-done.4.refs_9_ = bf16[1,128,512]{2,1,0:T(8,128)(2,1)S(1)} collective-permute-done((bf16[1,128,512]{2,1,0:T(8,128)(2,1)S(1)}, bf16[1,128,512]{2,1,0:T(8,128)(2,1)S(1)}, u32[]{:S(2)}, u32[]{:S(2)}) %collective-permute-start.4) | collective-permute-done | bytes 131104 | tf_op jit(solution)/shard_map/ppermute | solution.py:27
  154.9 7.6 %shard_map.77 = (bf16[128,512]{1,0:T(8,128)(2,1)}, bf16[128,512]{1,0:T(8,128)(2,1)}, bf16[128,512]{1,0:T(8,128)(2,1)}, bf16[128,512]{1,0:T(8,128)(2,1)}, bf16[128,512]{1,0:T(8,128)(2,1)}) custom-call(bf16[128,512]{1,0:T(8,128)(2,1)} %dynamic-slice_bitcast_fusion.refs_0_, bf16[128,128]{1,0:T(8,128)(2,1)} %dynamic-slice_bitcast_fusion.1.refs_1_, ...), custom_call_target="tpu_custom_call" | custom-call | flops 1006632960 | bytes 7864320 | tf_op jit(solution)/shard_map/pallas_call | solution.py:169
  162.5 2.2 %collective-permute-start.6 = (bf16[128,512]{1,0:T(8,128)(2,1)}, bf16[128,512]{1,0:T(8,128)(2,1)S(1)}, u32[]{:S(2)}, u32[]{:S(2)}) collective-permute-start(bf16[128,512]{1,0:T(8,128)(2,1)} %get-tuple-element.34), channel_id=1, source_target_pairs={{0,448},{64,384},{128,320},{192,256},{1,449},{65,385},{129,321},{1... | collective-permute-start | bytes 393224 | tf_op jit(solution)/shard_map/ppermute | solution.py:257
  164.8 4.6 %collective-permute-done.6.refs_0_ = bf16[128,512]{1,0:T(8,128)(2,1)S(1)} collective-permute-done((bf16[128,512]{1,0:T(8,128)(2,1)}, bf16[128,512]{1,0:T(8,128)(2,1)S(1)}, u32[]{:S(2)}, u32[]{:S(2)}) %collective-permute-start.6) | collective-permute-done | bytes 131104 | tf_op jit(solution)/shard_map/ppermute | solution.py:257
  170.0 2.2 %shard_map.78 = (bf16[128,512]{1,0:T(8,128)(2,1)}, bf16[128,512]{1,0:T(8,128)(2,1)}, bf16[128,512]{1,0:T(8,128)(2,1)}, bf16[128,512]{1,0:T(8,128)(2,1)}) custom-call(bf16[128,512]{1,0:T(8,128)(2,1)} %copy-done.19, bf16[128,128]{1,0:T(8,128)(2,1)} %dynamic-slice_bitcast_fusion.1.refs_1_, bf16[4,2,3,256,512]{4,3,2,1,0:T(8,128)(2,1)} %bitcast.57, ...), custom_call_target="tpu_custom_call" | custom-call | flops 1006632960 | bytes 7864320 | tf_op jit(solution)/shard_map/pallas_call | solution.py:169
  172.2 3.3 %collective-permute-start.7 = (bf16[128,512]{1,0:T(8,128)(2,1)}, bf16[128,512]{1,0:T(8,128)(2,1)S(1)}, u32[]{:S(2)}, u32[]{:S(2)}) collective-permute-start(bf16[128,512]{1,0:T(8,128)(2,1)} %get-tuple-element.40), channel_id=1, source_target_pairs={{0,64},{64,0},{128,192},{192,128},{1,65},{65,1},{129,193},{193,129... | collective-permute-start | bytes 393224 | tf_op jit(solution)/shard_map/ppermute | solution.py:27
  175.5 5.0 %collective-permute-start.8 = (bf16[128,512]{1,0:T(8,128)(2,1)}, bf16[128,512]{1,0:T(8,128)(2,1)S(1)}, u32[]{:S(2)}, u32[]{:S(2)}) collective-permute-start(bf16[128,512]{1,0:T(8,128)(2,1)} %get-tuple-element.41), channel_id=1, source_target_pairs={{0,128},{64,192},{128,0},{192,64},{1,129},{65,193},{129,1},{193,65... | collective-permute-start | bytes 393224 | tf_op jit(solution)/shard_map/ppermute | solution.py:27
  180.5 1.9 collective-permute-start.9
  182.5 5.2 %collective-permute-done.8.refs_2_ = bf16[128,512]{1,0:T(8,128)(2,1)S(1)} collective-permute-done((bf16[128,512]{1,0:T(8,128)(2,1)}, bf16[128,512]{1,0:T(8,128)(2,1)S(1)}, u32[]{:S(2)}, u32[]{:S(2)}) %collective-permute-start.8) | collective-permute-done | bytes 131104 | tf_op jit(solution)/shard_map/ppermute | solution.py:27
  187.6 1.9 collective-permute-done.9.refs_3_
  190.1 17.0 %shard_map.79 = bf16[1,4,128,512]{3,2,1,0:T(8,128)(2,1)} custom-call(bf16[128,512]{1,0:T(8,128)(2,1)} %get-tuple-element.39.refs_0_, bf16[128,512]{1,0:T(8,128)(2,1)} %copy-done.20, bf16[128,512]{1,0:T(8,128)(2,1)} %copy-done.21, bf16[128,512]{1,0:T(8,128)(2,1)} %copy-done.22), custom_call_target="tpu_custom_call" | custom-call | tf_op jit(solution)/shard_map/pallas_call | solution.py:203
  (74 shorter events, 6.0 us)
Async XLA Ops:
  6.5 1.4 copy-start
  6.5 2.4 %copy-start.24 = (s32[1,64,16]{1,2,0:T(8,128)S(1)}, s32[1,64,16]{1,2,0:T(8,128)}, u32[]{:S(2)}) copy-start(s32[1,64,16]{1,2,0:T(8,128)} %param.10) | copy-start | bytes 12292
  6.5 3.6 %copy-start.25 = (s32[1,64]{1,0:T(1,128)S(1)}, s32[1,64]{1,0:T(1,128)}, u32[]{:S(2)}) copy-start(s32[1,64]{1,0:T(1,128)} %param.11) | copy-start | bytes 772
  6.5 147.7 %all-gather.3.cloned.1.call-start = ((), (), s32[]{:S(2)}) async-start(), calls=%async_computation.2 | async-start | bytes 7077888 | tf_op jit(solution)/shard_map/all_gather | solution.py:224
  7.9 3.7 %copy-start.2 = (bf16[3,512,512]{2,1,0:T(8,128)(2,1)S(1)}, bf16[3,512,512]{2,1,0:T(8,128)(2,1)}, u32[]{:S(2)}) copy-start(bf16[3,512,512]{2,1,0:T(8,128)(2,1)} %refs_1_.3) | copy-start | bytes 4718596
  13.6 1.4 copy-start.1
  15.0 0.8 copy-start.3
  15.8 11.2 %copy-start.23 = (s32[4,6]{1,0:T(4,128)S(1)}, s32[4,6]{1,0:T(4,128)}, u32[]{:S(2)}) copy-start(s32[4,6]{1,0:T(4,128)} %param.12) | copy-start | bytes 292
  15.8 60.1 %all-to-all-start = ((bf16[64,2,16,512]{3,2,1,0:T(8,128)(2,1)}), bf16[64,2,16,512]{3,2,1,0:T(8,128)(2,1)}, u32[]{:S(2)}, u32[]{:S(2)}) async-start(bf16[64,2,16,512]{3,2,1,0:T(8,128)(2,1)} %copy-done.1), calls=%async_computation | async-start | bytes 4194304 | tf_op jit(solution)/shard_map/all_to_all | solution.py:244
  28.0 1.1 copy-start.4
  30.5 1.0 copy-start.5
  31.4 52.8 %copy-start.12 = (bf16[4,6,128,128]{3,2,1,0:T(8,128)(2,1)S(1)}, bf16[4,6,128,128]{3,2,1,0:T(8,128)(2,1)}, u32[]{:S(2)}) copy-start(bf16[4,6,128,128]{3,2,1,0:T(8,128)(2,1)} %param.13) | copy-start | bytes 2359300
  75.9 47.6 %all-to-all-start.1 = ((bf16[64,1,16,512]{3,2,1,0:T(8,128)(2,1)}), bf16[64,1,16,512]{3,2,1,0:T(8,128)(2,1)S(1)}, u32[]{:S(2)}, u32[]{:S(2)}) async-start(bf16[64,1,16,512]{3,2,1,0:T(8,128)(2,1)} %copy-done.5), calls=%async_computation.1 | async-start | bytes 2097152 | tf_op jit(solution)/shard_map/all_to_all | solution.py:244
  85.1 3.4 %copy-start.18 = (bf16[4,128,128]{2,1,0:T(8,128)(2,1)S(1)}, bf16[4,128,128]{2,1,0:T(8,128)(2,1)}, u32[]{:S(2)}) copy-start(bf16[4,128,128]{2,1,0:T(8,128)(2,1)} %get-tuple-element.50) | copy-start | bytes 393220
  88.5 3.5 %copy-start.17 = (bf16[4,128,128]{2,1,0:T(8,128)(2,1)S(1)}, bf16[4,128,128]{2,1,0:T(8,128)(2,1)}, u32[]{:S(2)}) copy-start(bf16[4,128,128]{2,1,0:T(8,128)(2,1)} %get-tuple-element.49) | copy-start | bytes 393220
  91.9 3.4 %copy-start.16 = (bf16[4,128,128]{2,1,0:T(8,128)(2,1)S(1)}, bf16[4,128,128]{2,1,0:T(8,128)(2,1)}, u32[]{:S(2)}) copy-start(bf16[4,128,128]{2,1,0:T(8,128)(2,1)} %get-tuple-element.53) | copy-start | bytes 393220
  98.8 3.4 %copy-start.26 = (s32[4]{0:T(128)S(1)}, s32[4]{0:T(128)}, u32[]{:S(2)}) copy-start(s32[4]{0:T(128)} %get-tuple-element.43) | copy-start | bytes 52
  102.4 3.0 %copy-start.9 = (bf16[512,512]{1,0:T(8,128)(2,1)S(1)}, bf16[512,512]{1,0:T(8,128)(2,1)}, u32[]{:S(2)}) copy-start(bf16[512,512]{1,0:T(8,128)(2,1)} %param.7) | copy-start | bytes 1572868
  108.9 1.0 copy-start.6
  109.8 0.7 copy-start.8
  110.6 0.7 copy-start.11
  111.3 22.4 %collective-permute-start = (bf16[2,128,512]{2,1,0:T(8,128)(2,1)}, bf16[2,128,512]{2,1,0:T(8,128)(2,1)}, u32[]{:S(2)}, u32[]{:S(2)}) collective-permute-start(bf16[2,128,512]{2,1,0:T(8,128)(2,1)} %get-tuple-element.26), channel_id=1, source_target_pairs={{0,64},{64,0},{128,192},{192,128},{1,65},{65,1},{129,193},{193,129... | collective-permute-start | bytes 786440 | tf_op jit(solution)/shard_map/ppermute | solution.py:27
  115.5 30.4 %collective-permute-start.1 = (bf16[2,128,512]{2,1,0:T(8,128)(2,1)}, bf16[2,128,512]{2,1,0:T(8,128)(2,1)}, u32[]{:S(2)}, u32[]{:S(2)}) collective-permute-start(bf16[2,128,512]{2,1,0:T(8,128)(2,1)} %copy-done.11), channel_id=1, source_target_pairs={{0,128},{64,192},{128,0},{192,64},{1,129},{65,193},{129,1},{193,65... | collective-permute-start | bytes 786440 | tf_op jit(solution)/shard_map/ppermute | solution.py:27
  121.5 24.3 %collective-permute-start.2 = (bf16[2,128,512]{2,1,0:T(8,128)(2,1)S(1)}, bf16[2,128,512]{2,1,0:T(8,128)(2,1)}, u32[]{:S(2)}, u32[]{:S(2)}) collective-permute-start(bf16[2,128,512]{2,1,0:T(8,128)(2,1)S(1)} %get-tuple-element.28), channel_id=1, source_target_pairs={{0,192},{64,128},{128,64},{192,0},{1,193},{65,129},{129,65},{193,1... | collective-permute-start | bytes 786440 | tf_op jit(solution)/shard_map/ppermute | solution.py:27
  123.5 1.2 copy-start.7
  125.4 12.2 %copy-start.10 = (bf16[1,128,512]{2,1,0:T(8,128)(2,1)}, bf16[1,128,512]{2,1,0:T(8,128)(2,1)S(1)}, u32[]{:S(2)}) copy-start(bf16[1,128,512]{2,1,0:T(8,128)(2,1)S(1)} %get-tuple-element.30.refs_7_) | copy-start | bytes 393220
  125.4 20.4 %collective-permute-start.3 = (bf16[1,128,512]{2,1,0:T(8,128)(2,1)S(1)}, bf16[1,128,512]{2,1,0:T(8,128)(2,1)S(1)}, u32[]{:S(2)}, u32[]{:S(2)}) collective-permute-start(bf16[1,128,512]{2,1,0:T(8,128)(2,1)S(1)} %get-tuple-element.31), channel_id=1, source_target_pairs={{0,64},{64,0},{128,192},{192,128},{1,65},{65,1},{129,193},{193,129... | collective-permute-start | bytes 393224 | tf_op jit(solution)/shard_map/ppermute | solution.py:27
  127.9 26.3 %collective-permute-start.4 = (bf16[1,128,512]{2,1,0:T(8,128)(2,1)S(1)}, bf16[1,128,512]{2,1,0:T(8,128)(2,1)S(1)}, u32[]{:S(2)}, u32[]{:S(2)}) collective-permute-start(bf16[1,128,512]{2,1,0:T(8,128)(2,1)S(1)} %get-tuple-element.32), channel_id=1, source_target_pairs={{0,128},{64,192},{128,0},{192,64},{1,129},{65,193},{129,1},{193,65... | collective-permute-start | bytes 393224 | tf_op jit(solution)/shard_map/ppermute | solution.py:27
  133.7 20.5 %collective-permute-start.5 = (bf16[1,128,512]{2,1,0:T(8,128)(2,1)S(1)}, bf16[1,128,512]{2,1,0:T(8,128)(2,1)S(1)}, u32[]{:S(2)}, u32[]{:S(2)}) collective-permute-start(bf16[1,128,512]{2,1,0:T(8,128)(2,1)S(1)} %get-tuple-element.33), channel_id=1, source_target_pairs={{0,192},{64,128},{128,64},{192,0},{1,193},{65,129},{129,65},{193,1... | collective-permute-start | bytes 393224 | tf_op jit(solution)/shard_map/ppermute | solution.py:27
  145.9 8.3 %copy-start.13 = (bf16[1,128,512]{2,1,0:T(8,128)(2,1)}, bf16[1,128,512]{2,1,0:T(8,128)(2,1)S(1)}, u32[]{:S(2)}) copy-start(bf16[1,128,512]{2,1,0:T(8,128)(2,1)S(1)} %collective-permute-done.3.refs_8_) | copy-start | bytes 393220
  154.2 0.7 copy-start.14
  154.2 0.7 copy-start.15
  162.5 6.8 %collective-permute-start.6 = (bf16[128,512]{1,0:T(8,128)(2,1)}, bf16[128,512]{1,0:T(8,128)(2,1)S(1)}, u32[]{:S(2)}, u32[]{:S(2)}) collective-permute-start(bf16[128,512]{1,0:T(8,128)(2,1)} %get-tuple-element.34), channel_id=1, source_target_pairs={{0,448},{64,384},{128,320},{192,256},{1,449},{65,385},{129,321},{1... | collective-permute-start | bytes 393224 | tf_op jit(solution)/shard_map/ppermute | solution.py:257
  169.4 0.7 copy-start.19
  172.2 10.3 %collective-permute-start.7 = (bf16[128,512]{1,0:T(8,128)(2,1)}, bf16[128,512]{1,0:T(8,128)(2,1)S(1)}, u32[]{:S(2)}, u32[]{:S(2)}) collective-permute-start(bf16[128,512]{1,0:T(8,128)(2,1)} %get-tuple-element.40), channel_id=1, source_target_pairs={{0,64},{64,0},{128,192},{192,128},{1,65},{65,1},{129,193},{193,129... | collective-permute-start | bytes 393224 | tf_op jit(solution)/shard_map/ppermute | solution.py:27
  175.5 12.2 %collective-permute-start.8 = (bf16[128,512]{1,0:T(8,128)(2,1)}, bf16[128,512]{1,0:T(8,128)(2,1)S(1)}, u32[]{:S(2)}, u32[]{:S(2)}) collective-permute-start(bf16[128,512]{1,0:T(8,128)(2,1)} %get-tuple-element.41), channel_id=1, source_target_pairs={{0,128},{64,192},{128,0},{192,64},{1,129},{65,193},{129,1},{193,65... | collective-permute-start | bytes 393224 | tf_op jit(solution)/shard_map/ppermute | solution.py:27
  180.5 9.0 %collective-permute-start.9 = (bf16[128,512]{1,0:T(8,128)(2,1)}, bf16[128,512]{1,0:T(8,128)(2,1)S(1)}, u32[]{:S(2)}, u32[]{:S(2)}) collective-permute-start(bf16[128,512]{1,0:T(8,128)(2,1)} %get-tuple-element.42), channel_id=1, source_target_pairs={{0,192},{64,128},{128,64},{192,0},{1,193},{65,129},{129,65},{193,1... | collective-permute-start | bytes 393224 | tf_op jit(solution)/shard_map/ppermute | solution.py:27
  182.5 7.0 %copy-start.20 = (bf16[128,512]{1,0:T(8,128)(2,1)}, bf16[128,512]{1,0:T(8,128)(2,1)S(1)}, u32[]{:S(2)}) copy-start(bf16[128,512]{1,0:T(8,128)(2,1)S(1)} %collective-permute-done.7.refs_1_) | copy-start | bytes 393220
  187.6 1.9 copy-start.21
  189.5 0.7 copy-start.22
Sparse Core Ops, SparseCore 0:
  9.4 82.0 all-gather.2

commit v3 on v2

v3 whole, which is shorter than its diff:
```python
import jax
import jax.numpy as jnp
import numpy as np
from jax import lax
from jax.experimental import pallas as pl
from jax.experimental.pallas import tpu as pltpu
from jax.sharding import Mesh, PartitionSpec as P

HALVES = 2
STAGES = 4
CORES = 2
SEGMENT = ("half", "stage")
DOM = ("pair", "core")
PIECES = ((0, 1), (2,))
ANYWHERE = pl.BlockSpec(memory_space=pl.ANY)
VMEM = pl.BlockSpec(memory_space=pltpu.VMEM)
GRANT = pltpu.CompilerParams(vmem_limit_bytes=60 * 1024 * 1024)
SMALL = pltpu.CompilerParams(vmem_limit_bytes=24 * 1024 * 1024)


def tile_of(slot):
    mirror = lax.axis_index("half") * (STAGES - 1)
    return lax.axis_index("stage") ^ mirror ^ slot


def exchange(block, slot):
    if slot == 0:
        return block
    return lax.ppermute(block, "stage", [(u, u ^ slot) for u in range(STAGES)])


def spread_kernel(source_ref, blocks_ref, features_ref, out_ref, own_a_ref, own_x_ref):
    tiles, picked, rows, _ = blocks_ref.shape
    own_a_ref[...] = blocks_ref[tile_of(0), 0]
    own_x_ref[...] = features_ref[tile_of(0)]
    out_ref[...] = jnp.zeros_like(out_ref)
    for t in range(tiles):
        for k in range(1, picked):
            first = pl.multiple_of((source_ref[t, k] - 1) * rows, rows)
            out_ref[t, :, pl.ds(first, rows)] = blocks_ref[t, k]


def spread_blocks(adj_src, adj_blocks, features, halo_rows):
    tiles, _, rows, _ = adj_blocks.shape
    width = features.shape[2]
    return pl.pallas_call(
        spread_kernel,
        out_shape=[
            jax.ShapeDtypeStruct((tiles, rows, halo_rows), jnp.bfloat16),
            jax.ShapeDtypeStruct((rows, rows), jnp.bfloat16),
            jax.ShapeDtypeStruct((rows, width), jnp.bfloat16),
        ],
        in_specs=[pl.BlockSpec(memory_space=pltpu.SMEM), VMEM, VMEM],
        out_specs=[VMEM] * 3,
        compiler_params=GRANT,
    )(adj_src, adj_blocks, features)


def pick_kernel(rows_ref, count_ref, history_ref, out_ref):
    receivers, levels, slots, width = out_ref.shape
    rows = history_ref.shape[1]
    slot = lax.broadcasted_iota(jnp.int32, (slots, receivers), 0)
    wanted = jnp.where(slot < count_ref[0], rows_ref[0], -1)
    column = lax.broadcasted_iota(jnp.int32, (slots, rows), 1)
    picks = [
        jnp.where(wanted[:, p : p + 1] == column, 1.0, 0.0).astype(jnp.bfloat16)
        for p in range(receivers)
    ]
    pick = jnp.concatenate(picks, axis=0)
    for place in range(levels):
        got = jnp.dot(pick, history_ref[place], preferred_element_type=jnp.float32)
        out_ref[:, place] = got.astype(jnp.bfloat16).reshape(receivers, slots, width)


def pick_rows(levels, send_rows, send_count, history):
    parts, slots = send_rows.shape[1:]
    _, rows, width = history.shape
    step = 16
    steps = parts // step
    by_slot = send_rows.reshape(steps, step, slots).swapaxes(1, 2)
    return pl.pallas_call(
        pick_kernel,
        out_shape=jax.ShapeDtypeStruct((parts, len(levels), slots, width), jnp.bfloat16),
        grid=(steps,),
        in_specs=[
            pl.BlockSpec((1, slots, step), lambda g: (g, 0, 0)),
            pl.BlockSpec((1, 1, step), lambda g: (g, 0, 0)),
            pl.BlockSpec(
                (len(levels), rows, width), lambda g: (levels[0] // len(levels), 0, 0)
            ),
        ],
        out_specs=pl.BlockSpec((step, len(levels), slots, width), lambda g: (g, 0, 0, 0)),
        compiler_params=GRANT,
        cost_estimate=pl.CostEstimate(
            flops=2 * len(levels) * parts * slots * rows * width,
            bytes_accessed=2 * len(levels) * (parts * slots + rows) * width,
            transcendentals=0,
        ),
    )(by_slot, send_count.reshape(steps, 1, step), history)


def halo_kernel(levels, arrived_ref, spread_ref, features_ref, *out_refs):
    parts, _, slots, width = arrived_ref.shape
    tiles, rows, _ = spread_ref.shape
    spread = jnp.concatenate([spread_ref[tile_of(r)] for r in range(tiles)], axis=0)
    for place in range(levels):
        halo = arrived_ref[:, place].reshape(parts * slots, width)
        summed = jnp.dot(spread, halo, preferred_element_type=jnp.float32)
        for r in range(tiles):
            start = 0.1 * features_ref[tile_of(r)].astype(jnp.float32)
            part = 0.9 * summed[r * rows : (r + 1) * rows] + start
            out_refs[r][place] = part.astype(jnp.bfloat16)


def halo_sums(arrived, spread, features, grant):
    parts, levels, slots, width = arrived.shape
    tiles, rows, halo_rows = spread.shape
    return pl.pallas_call(
        lambda *refs: halo_kernel(levels, *refs),
        out_shape=[jax.ShapeDtypeStruct((levels, rows, width), jnp.bfloat16)] * tiles,
        in_specs=[VMEM] * 3,
        out_specs=[VMEM] * tiles,
        compiler_params=grant,
        cost_estimate=pl.CostEstimate(
            flops=2 * levels * tiles * rows * halo_rows * width,
            bytes_accessed=2 * (arrived.size + spread.size + features.size * (1 + levels)),
            transcendentals=0,
        ),
    )(arrived, spread, features)


def chain_kernel(which, betas, x_ref, a_ref, w_ref, *refs):
    stages, cores, levels, depth, _ = w_ref.shape
    pieces = len(PIECES)
    h_refs = [refs[p * stages : (p + 1) * stages] for p in range(pieces)]
    refs = refs[pieces * stages :]
    if which > 0:
        before_refs, refs = refs[:stages], refs[stages:]
    out_refs = refs[:stages]
    h_bufs = refs[-pieces:]
    half = lax.axis_index("half")
    stage = lax.axis_index("stage")

    @pl.when(half == which)
    def _():
        for p in range(pieces):
            for r in range(stages):
                h_bufs[p][stage ^ r] = h_refs[p][r][...]
        a = a_ref[...]
        x = x_ref[...]
        for s in range(stages):
            for p, chosen in enumerate(PIECES):
                for place, i in enumerate(chosen):
                    beta = betas[(which * stages + s) * levels + i]
                    summed = jnp.dot(a, x, preferred_element_type=jnp.float32)
                    support = 0.9 * summed + h_bufs[p][s, place].astype(jnp.float32)
                    rounded = support.astype(jnp.bfloat16)
                    branch = sum(
                        jnp.dot(
                            rounded[:, c * depth : (c + 1) * depth],
                            w_ref[s, c, i],
                            preferred_element_type=jnp.float32,
                        )
                        for c in range(cores)
                    )
                    mixed = (1.0 - beta) * support + beta * branch
                    x = jnp.maximum(mixed, 0.0).astype(jnp.bfloat16)
            for r in range(stages):

                @pl.when(stage ^ s == r)
                def _():
                    out_refs[r][...] = x

        if which == 0:
            refs[stages][...] = x

    if which > 0:

        @pl.when(half != which)
        def _():
            for r in range(stages):
                out_refs[r][...] = before_refs[r][...]


def chain(which, x, a, weights, halos, before=()):
    stages, _, levels, _, width = weights.shape
    rows = x.shape[0]
    order = np.arange(HALVES * stages * levels, dtype=np.float32)
    betas = [float(b) for b in np.log1p(np.float32(1.0) / (order + np.float32(1.0)))]
    flat = [h for piece in halos for h in piece]
    outs = stages if before else stages + 1
    return pl.pallas_call(
        lambda *refs: chain_kernel(which, betas, *refs),
        out_shape=[jax.ShapeDtypeStruct((rows, width), jnp.bfloat16)] * outs,
        in_specs=[VMEM] * (3 + len(flat) + len(before)),
        out_specs=[VMEM] * outs,
        scratch_shapes=[
            pltpu.VMEM((stages,) + piece[0].shape, jnp.bfloat16) for piece in halos
        ],
        compiler_params=SMALL,
        cost_estimate=pl.CostEstimate(
            flops=2 * stages * levels * rows * width * (width + rows),
            bytes_accessed=2 * stages * levels * width * (width + rows),
            transcendentals=0,
        ),
    )(x, a, weights, *flat, *before)


def place_kernel(*refs):
    in_refs, out_ref = refs[:-1], refs[-1]
    for r, ref in enumerate(in_refs):
        out_ref[0, tile_of(r)] = ref[...]


def place(tiles):
    rows, width = tiles[0].shape
    return pl.pallas_call(
        place_kernel,
        out_shape=jax.ShapeDtypeStruct((1, len(tiles), rows, width), jnp.bfloat16),
        in_specs=[VMEM] * len(tiles),
        out_specs=VMEM,
        compiler_params=SMALL,
    )(*tiles)


def local(features, history, weights, send_rows, send_count, adj_src, adj_blocks):
    rows_dev, width = features.shape
    levels = weights.shape[0]
    tile_rows = adj_blocks.shape[2]
    parts, slots = send_rows.shape[1:]
    halo_rows = parts * slots
    core = lax.axis_index("core")
    tiles = features.reshape(STAGES, tile_rows, width)

    outgoing = pick_rows(PIECES[0], send_rows, send_count, history)
    outgoing, history, adj_blocks = lax.optimization_barrier((outgoing, history, adj_blocks))
    spread, own_a, own_x = spread_blocks(adj_src, adj_blocks, tiles, halo_rows)
    spread, weights = lax.optimization_barrier((spread, weights))

    depth = width // CORES
    own = lax.dynamic_slice_in_dim(weights, core * depth, depth, 1)
    group = lax.all_gather(own, ("stage", "core")).reshape(STAGES, CORES, levels, depth, width)

    halos = []
    for following in PIECES[1:] + (None,):
        arrived = lax.all_to_all(outgoing, DOM, split_axis=0, concat_axis=0, tiled=True)
        if following is not None:
            outgoing = pick_rows(following, send_rows, send_count, history)
            arrived, outgoing, spread = lax.optimization_barrier((arrived, outgoing, spread))
        sums = halo_sums(arrived, spread, tiles, SMALL)
        if following is None:
            sums, group = lax.optimization_barrier((sums, group))
        halos.append([exchange(block, r) for r, block in enumerate(sums)])

    *first, last = chain(0, own_x, own_a, group, halos)
    mirror = [(s, HALVES * STAGES - 1 - s) for s in range(STAGES)]
    done = chain(1, lax.ppermute(last, SEGMENT, mirror), own_a, group, halos, first)
    fresh = place([exchange(block, r) for r, block in enumerate(done)])
    return fresh.reshape(1, rows_dev, width)


def solution(mesh):
    segments, parts = mesh.devices.shape
    devices = mesh.devices.reshape(HALVES, segments // HALVES, parts // CORES, CORES)
    fine = Mesh(devices, SEGMENT + DOM)
    placed = (
        P(DOM, None),
        P(SEGMENT, DOM, None),
        P(SEGMENT, None, None),
        P(DOM, None, None),
        P(DOM, None),
        P(DOM, None),
        P(DOM, None, None, None),
    )
    return jax.shard_map(
        local, mesh=fine, in_specs=placed, out_specs=P(SEGMENT, DOM, None), check_vma=False
    )
```

time: 218 us -> 186 us (0.85)
  the two profiles are of different devices: /device:TPU:6 before, /device:TPU:322 now
where the time goes in v3:
time: 186 us; the launch traced here: 185 us
  waiting for transfers between devices  87.3 us (47%)
  starting transfers between devices  47.5 us (26%)
  Pallas kernels  22.9 us (12%)
  between operations  13.6 us (7%)
  local copies, waits for them, and re-layouts  12.5 us (7%)
    all_to_all x2, waiting for transfers between devices, local(): lax.all_to_all(outgoing, DOM, split_axis=0, concat_axis=0, tiled=True)  58.5 us
    ppermute x9, starting transfers between devices, exchange(): return lax.ppermute(block, 'stage', [(u, u ^ slot) for u in range(STAGES)])  27.6 us
    ppermute x9, waiting for transfers between devices, exchange(): return lax.ppermute(block, 'stage', [(u, u ^ slot) for u in range(STAGES)])  19.6 us
    all_to_all x2, starting transfers between devices, local(): lax.all_to_all(outgoing, DOM, split_axis=0, concat_axis=0, tiled=True)  18.4 us
    unnamed x23, local copies, waits for them, and re-layouts  9.41 us
    ppermute x1, waiting for transfers between devices, local(): lax.ppermute(last, SEGMENT, mirror)  9.12 us
    pallas_call x2, Pallas kernels, pick_rows(): pl.pallas_call(pick_kernel, out_shape=jax.ShapeDtypeStruct((parts, len(le...  8.51 us
    pallas_call x2, Pallas kernels, chain(): pl.pallas_call(lambda *refs: chain_kernel(which, betas, *refs), out_shape...  6.57 us
  transfers between devices with their start and end apart: 13, of which 7 were waited for; matrix products, arithmetic and copies ran while one was open for 0% of the time, Pallas kernels for 4%

profile of v3, /device:TPU:322, one launch (start us, length us, event | category | flops | bytes accessed | tf_op | source)
XLA Modules:
  0.0 185.1 jit_solution(2827470098491799435)
XLA Ops:
  6.5 0.5 broadcast.3
  7.1 1.3 reduce.3
  8.4 0.7 reshape.18
  9.0 0.8 reshape.17
  9.8 0.6 copy.17
  10.4 4.6 %shard_map.73 = bf16[64,2,16,512]{3,2,1,0:T(8,128)(2,1)} custom-call(s32[4,16,16]{2,1,0:T(8,128)} %bitcast.14, s32[4,1,16]{2,1,0:T(1,128)} %bitcast.16, bf16[3,512,512]{2,1,0:T(8,128)(2,1)} %history_ref.2), custom_call_target="tpu_custom_call" | custom-call | flops 1073741824 | bytes 3145728 | tf_op jit(solution)/shard_map/pallas_call | solution.py:81
  15.0 2.6 %shard_map.74 = (bf16[4,128,1024]{2,1,0:T(8,128)(2,1)}, bf16[128,128]{1,0:T(8,128)(2,1)}, bf16[128,512]{1,0:T(8,128)(2,1)}) custom-call(s32[4,6]{1,0:T(4,128)} %source_ref.1, bf16[4,6,128,128]{3,2,1,0:T(8,128)(2,1)} %blocks_ref, bf16[4,128,512]{2,1,0:T(8,128)(2,1)} %bitcast.11), custom_call_target="tpu_custom_call" | custom-call | tf_op jit(solution)/shard_map/pallas_call | solution.py:46
  17.6 1.0 constant_dynamic-slice_fusion
  18.6 0.0 all-gather.3.cloned.1.call-update
  18.6 10.9 %all-to-all-start = ((bf16[64,2,16,512]{3,2,1,0:T(8,128)(2,1)}), bf16[64,2,16,512]{3,2,1,0:T(8,128)(2,1)}, u32[]{:S(2)}, u32[]{:S(2)}) async-start(bf16[64,2,16,512]{3,2,1,0:T(8,128)(2,1)} %shard_map.73), calls=%async_computation | async-start | bytes 4194304 | tf_op jit(solution)/shard_map/all_to_all | solution.py:246
  29.5 0.0 copy-start.3
  29.5 3.9 %shard_map.75 = bf16[64,1,16,512]{3,2,1,0:T(8,128)(2,1)} custom-call(s32[4,16,16]{2,1,0:T(8,128)} %bitcast.15, s32[4,1,16]{2,1,0:T(1,128)} %bitcast.17, bf16[3,512,512]{2,1,0:T(8,128)(2,1)} %history_ref.2), custom_call_target="tpu_custom_call" | custom-call | flops 536870912 | bytes 1572864 | tf_op jit(solution)/shard_map/pallas_call | solution.py:81
  33.4 45.5 %all-to-all-done.refs_0_ = bf16[64,2,16,512]{3,2,1,0:T(8,128)(2,1)} async-done(((bf16[64,2,16,512]{3,2,1,0:T(8,128)(2,1)}), bf16[64,2,16,512]{3,2,1,0:T(8,128)(2,1)}, u32[]{:S(2)}, u32[]{:S(2)}) %all-to-all-start) | async-done | bytes 2097184 | tf_op jit(solution)/shard_map/all_to_all | solution.py:246
  78.9 7.5 %all-to-all-start.1 = ((bf16[64,1,16,512]{3,2,1,0:T(8,128)(2,1)}), bf16[64,1,16,512]{3,2,1,0:T(8,128)(2,1)S(1)}, u32[]{:S(2)}, u32[]{:S(2)}) async-start(bf16[64,1,16,512]{3,2,1,0:T(8,128)(2,1)} %shard_map.75), calls=%async_computation.1 | async-start | bytes 2097152 | tf_op jit(solution)/shard_map/all_to_all | solution.py:246
  86.5 1.2 copy-done.4
  87.7 3.7 %shard_map.77 = (bf16[2,128,512]{2,1,0:T(8,128)(2,1)S(1)}, bf16[2,128,512]{2,1,0:T(8,128)(2,1)}, bf16[2,128,512]{2,1,0:T(8,128)(2,1)}, bf16[2,128,512]{2,1,0:T(8,128)(2,1)}) custom-call(bf16[64,2,16,512]{3,2,1,0:T(8,128)(2,1)} %all-to-all-done.refs_0_, bf16[4,128,1024]{2,1,0:T(8,128)(2,1)S(1)} %copy-done.4, bf16[4,128,512]{2,1,0:T(8,128)(2,1)S(1)} %bitcast.12), custom_call_target="tpu_custom_call" | custom-call | flops 1073741824 | bytes 4718592 | tf_op jit(solution)/shard_map/pallas_call | solution.py:118
  91.4 2.5 %collective-permute-start = (bf16[2,128,512]{2,1,0:T(8,128)(2,1)}, bf16[2,128,512]{2,1,0:T(8,128)(2,1)}, u32[]{:S(2)}, u32[]{:S(2)}) collective-permute-start(bf16[2,128,512]{2,1,0:T(8,128)(2,1)} %get-tuple-element.55), channel_id=1, source_target_pairs={{0,64},{64,0},{128,192},{192,128},{1,65},{65,1},{129,193},{193,129... | collective-permute-start | bytes 786440 | tf_op jit(solution)/shard_map/ppermute | solution.py:29
  93.9 4.3 %collective-permute-start.1 = (bf16[2,128,512]{2,1,0:T(8,128)(2,1)}, bf16[2,128,512]{2,1,0:T(8,128)(2,1)}, u32[]{:S(2)}, u32[]{:S(2)}) collective-permute-start(bf16[2,128,512]{2,1,0:T(8,128)(2,1)} %get-tuple-element.56), channel_id=1, source_target_pairs={{0,128},{64,192},{128,0},{192,64},{1,129},{65,193},{129,1},{193,65... | collective-permute-start | bytes 786440 | tf_op jit(solution)/shard_map/ppermute | solution.py:29
  98.1 2.5 %collective-permute-start.2 = (bf16[2,128,512]{2,1,0:T(8,128)(2,1)}, bf16[2,128,512]{2,1,0:T(8,128)(2,1)}, u32[]{:S(2)}, u32[]{:S(2)}) collective-permute-start(bf16[2,128,512]{2,1,0:T(8,128)(2,1)} %get-tuple-element.57), channel_id=1, source_target_pairs={{0,192},{64,128},{128,64},{192,0},{1,193},{65,129},{129,65},{193,1... | collective-permute-start | bytes 786440 | tf_op jit(solution)/shard_map/ppermute | solution.py:29
  100.6 13.0 %all-to-all-done.1.refs_0_ = bf16[64,1,16,512]{3,2,1,0:T(8,128)(2,1)S(1)} async-done(((bf16[64,1,16,512]{3,2,1,0:T(8,128)(2,1)}), bf16[64,1,16,512]{3,2,1,0:T(8,128)(2,1)S(1)}, u32[]{:S(2)}, u32[]{:S(2)}) %all-to-all-start.1) | async-done | bytes 1048608 | tf_op jit(solution)/shard_map/all_to_all | solution.py:246
  113.6 1.2 copy-done.5
  114.8 0.7 shard_map.76
  115.6 0.6 copy-done.8
  116.2 0.7 copy-done.9
  116.9 0.7 copy-done.10
  117.5 2.4 %collective-permute-start.3 = (bf16[1,128,512]{2,1,0:T(8,128)(2,1)}, bf16[1,128,512]{2,1,0:T(8,128)(2,1)S(1)}, u32[]{:S(2)}, u32[]{:S(2)}) collective-permute-start(bf16[1,128,512]{2,1,0:T(8,128)(2,1)} %copy-done.10), channel_id=1, source_target_pairs={{0,64},{64,0},{128,192},{192,128},{1,65},{65,1},{129,193},{193,129... | collective-permute-start | bytes 393224 | tf_op jit(solution)/shard_map/ppermute | solution.py:29
  120.0 4.3 %collective-permute-start.4 = (bf16[1,128,512]{2,1,0:T(8,128)(2,1)}, bf16[1,128,512]{2,1,0:T(8,128)(2,1)S(1)}, u32[]{:S(2)}, u32[]{:S(2)}) collective-permute-start(bf16[1,128,512]{2,1,0:T(8,128)(2,1)} %copy-done.9), channel_id=1, source_target_pairs={{0,128},{64,192},{128,0},{192,64},{1,129},{65,193},{129,1},{193,65... | collective-permute-start | bytes 393224 | tf_op jit(solution)/shard_map/ppermute | solution.py:29
  124.3 0.0 collective-permute-done.refs_4_
  124.3 2.5 %collective-permute-start.5 = (bf16[1,128,512]{2,1,0:T(8,128)(2,1)}, bf16[1,128,512]{2,1,0:T(8,128)(2,1)S(1)}, u32[]{:S(2)}, u32[]{:S(2)}) collective-permute-start(bf16[1,128,512]{2,1,0:T(8,128)(2,1)} %copy-done.8), channel_id=1, source_target_pairs={{0,192},{64,128},{128,64},{192,0},{1,193},{65,129},{129,65},{193,1... | collective-permute-start | bytes 393224 | tf_op jit(solution)/shard_map/ppermute | solution.py:29
  126.8 0.0 collective-permute-done.1.refs_5_
  126.8 0.0 collective-permute-done.2.refs_6_
  126.8 0.0 collective-permute-done.3.refs_8_
  126.8 7.1 %collective-permute-done.4.refs_9_ = bf16[1,128,512]{2,1,0:T(8,128)(2,1)S(1)} collective-permute-done((bf16[1,128,512]{2,1,0:T(8,128)(2,1)}, bf16[1,128,512]{2,1,0:T(8,128)(2,1)S(1)}, u32[]{:S(2)}, u32[]{:S(2)}) %collective-permute-start.4) | collective-permute-done | bytes 131104 | tf_op jit(solution)/shard_map/ppermute | solution.py:29
  133.9 3.8 %collective-permute-done.5.refs_10_ = bf16[1,128,512]{2,1,0:T(8,128)(2,1)S(1)} collective-permute-done((bf16[1,128,512]{2,1,0:T(8,128)(2,1)}, bf16[1,128,512]{2,1,0:T(8,128)(2,1)S(1)}, u32[]{:S(2)}, u32[]{:S(2)}) %collective-permute-start.5) | collective-permute-done | bytes 131104 | tf_op jit(solution)/shard_map/ppermute | solution.py:29
  137.7 2.8 %copy-done.1 = bf16[24,256,512]{2,1,0:T(8,128)(2,1)S(1)} copy-done((bf16[24,256,512]{2,1,0:T(8,128)(2,1)S(1)}, bf16[24,256,512]{2,1,0:T(8,128)(2,1)}, u32[]{:S(2)}) %copy-start.1) | copy-done | bytes 6291480
  140.5 0.9 copy-done.6
  141.4 0.8 copy-done.7
  142.2 1.3 shard_map.78
  143.4 1.5 collective-permute-start.6
  145.0 9.1 %collective-permute-done.6.refs_0_ = bf16[128,512]{1,0:T(8,128)(2,1)S(1)} collective-permute-done((bf16[128,512]{1,0:T(8,128)(2,1)S(1)}, bf16[128,512]{1,0:T(8,128)(2,1)S(1)}, u32[]{:S(2)}, u32[]{:S(2)}) %collective-permute-start.6) | collective-permute-done | bytes 131104 | tf_op jit(solution)/shard_map/ppermute | solution.py:257
  154.1 5.3 %shard_map.79 = (bf16[128,512]{1,0:T(8,128)(2,1)S(1)}, bf16[128,512]{1,0:T(8,128)(2,1)S(1)}, bf16[128,512]{1,0:T(8,128)(2,1)S(1)}, bf16[128,512]{1,0:T(8,128)(2,1)S(1)}) custom-call(bf16[128,512]{1,0:T(8,128)(2,1)S(1)} %collective-permute-done.6.refs_0_, bf16[128,128]{1,0:T(8,128)(2,1)S(1)} %copy-done.7, bf16[4,2,3,256,512]{4,3,2,1,0:T(8,128)(2,1)S(1)} %bitcast.10, ...), custom_call_target="tpu_custom_call" | custom-call | flops 1006632960 | bytes 7864320 | tf_op jit(solution)/shard_map/pallas_call | solution.py:192
  159.4 1.9 %collective-permute-start.7 = (bf16[128,512]{1,0:T(8,128)(2,1)S(1)}, bf16[128,512]{1,0:T(8,128)(2,1)S(1)}, u32[]{:S(2)}, u32[]{:S(2)}) collective-permute-start(bf16[128,512]{1,0:T(8,128)(2,1)S(1)} %get-tuple-element.68), channel_id=1, source_target_pairs={{0,64},{64,0},{128,192},{192,128},{1,65},{65,1},{129,193},{193,129... | collective-permute-start | bytes 393224 | tf_op jit(solution)/shard_map/ppermute | solution.py:29
  161.3 4.8 %collective-permute-start.8 = (bf16[128,512]{1,0:T(8,128)(2,1)S(1)}, bf16[128,512]{1,0:T(8,128)(2,1)S(1)}, u32[]{:S(2)}, u32[]{:S(2)}) collective-permute-start(bf16[128,512]{1,0:T(8,128)(2,1)S(1)} %get-tuple-element.69), channel_id=1, source_target_pairs={{0,128},{64,192},{128,0},{192,64},{1,129},{65,193},{129,1},{193,65... | collective-permute-start | bytes 393224 | tf_op jit(solution)/shard_map/ppermute | solution.py:29
  166.1 2.5 %collective-permute-start.9 = (bf16[128,512]{1,0:T(8,128)(2,1)S(1)}, bf16[128,512]{1,0:T(8,128)(2,1)S(1)}, u32[]{:S(2)}, u32[]{:S(2)}) collective-permute-start(bf16[128,512]{1,0:T(8,128)(2,1)S(1)} %get-tuple-element.70), channel_id=1, source_target_pairs={{0,192},{64,128},{128,64},{192,0},{1,193},{65,129},{129,65},{193,1... | collective-permute-start | bytes 393224 | tf_op jit(solution)/shard_map/ppermute | solution.py:29
  168.6 0.0 collective-permute-done.7.refs_1_
  168.7 5.1 %collective-permute-done.8.refs_2_ = bf16[128,512]{1,0:T(8,128)(2,1)S(1)} collective-permute-done((bf16[128,512]{1,0:T(8,128)(2,1)S(1)}, bf16[128,512]{1,0:T(8,128)(2,1)S(1)}, u32[]{:S(2)}, u32[]{:S(2)}) %collective-permute-start.8) | collective-permute-done | bytes 131104 | tf_op jit(solution)/shard_map/ppermute | solution.py:29
  173.8 3.6 %collective-permute-done.9.refs_3_ = bf16[128,512]{1,0:T(8,128)(2,1)S(1)} collective-permute-done((bf16[128,512]{1,0:T(8,128)(2,1)S(1)}, bf16[128,512]{1,0:T(8,128)(2,1)S(1)}, u32[]{:S(2)}, u32[]{:S(2)}) %collective-permute-start.9) | collective-permute-done | bytes 131104 | tf_op jit(solution)/shard_map/ppermute | solution.py:29
  177.4 0.8 shard_map.80
  (15 shorter events, 0.0 us)
Async XLA Ops:
  6.5 11.1 %copy-start = (bf16[3,512,512]{2,1,0:T(8,128)(2,1)S(1)}, bf16[3,512,512]{2,1,0:T(8,128)(2,1)}, u32[]{:S(2)}) copy-start(bf16[3,512,512]{2,1,0:T(8,128)(2,1)} %param.9) | copy-start | bytes 4718596
  6.5 111.0 %all-gather.3.cloned.1.call-start = ((), (), s32[]{:S(2)}) async-start(), calls=%async_computation.2 | async-start | bytes 7077888 | tf_op jit(solution)/shard_map/all_gather | solution.py:242
  18.6 60.3 %all-to-all-start = ((bf16[64,2,16,512]{3,2,1,0:T(8,128)(2,1)}), bf16[64,2,16,512]{3,2,1,0:T(8,128)(2,1)}, u32[]{:S(2)}, u32[]{:S(2)}) async-start(bf16[64,2,16,512]{3,2,1,0:T(8,128)(2,1)} %shard_map.73), calls=%async_computation | async-start | bytes 4194304 | tf_op jit(solution)/shard_map/all_to_all | solution.py:246
  29.5 57.0 %copy-start.3 = (bf16[512,512]{1,0:T(8,128)(2,1)S(1)}, bf16[512,512]{1,0:T(8,128)(2,1)}, u32[]{:S(2)}) copy-start(bf16[512,512]{1,0:T(8,128)(2,1)} %param.7) | copy-start | bytes 1572868
  78.9 34.7 %all-to-all-start.1 = ((bf16[64,1,16,512]{3,2,1,0:T(8,128)(2,1)}), bf16[64,1,16,512]{3,2,1,0:T(8,128)(2,1)S(1)}, u32[]{:S(2)}, u32[]{:S(2)}) async-start(bf16[64,1,16,512]{3,2,1,0:T(8,128)(2,1)} %shard_map.75), calls=%async_computation.1 | async-start | bytes 2097152 | tf_op jit(solution)/shard_map/all_to_all | solution.py:246
  86.5 1.2 copy-start.4
  91.4 32.9 %collective-permute-start = (bf16[2,128,512]{2,1,0:T(8,128)(2,1)}, bf16[2,128,512]{2,1,0:T(8,128)(2,1)}, u32[]{:S(2)}, u32[]{:S(2)}) collective-permute-start(bf16[2,128,512]{2,1,0:T(8,128)(2,1)} %get-tuple-element.55), channel_id=1, source_target_pairs={{0,64},{64,0},{128,192},{192,128},{1,65},{65,1},{129,193},{193,129... | collective-permute-start | bytes 786440 | tf_op jit(solution)/shard_map/ppermute | solution.py:29
  93.9 32.9 %collective-permute-start.1 = (bf16[2,128,512]{2,1,0:T(8,128)(2,1)}, bf16[2,128,512]{2,1,0:T(8,128)(2,1)}, u32[]{:S(2)}, u32[]{:S(2)}) collective-permute-start(bf16[2,128,512]{2,1,0:T(8,128)(2,1)} %get-tuple-element.56), channel_id=1, source_target_pairs={{0,128},{64,192},{128,0},{192,64},{1,129},{65,193},{129,1},{193,65... | collective-permute-start | bytes 786440 | tf_op jit(solution)/shard_map/ppermute | solution.py:29
  98.1 28.7 %collective-permute-start.2 = (bf16[2,128,512]{2,1,0:T(8,128)(2,1)}, bf16[2,128,512]{2,1,0:T(8,128)(2,1)}, u32[]{:S(2)}, u32[]{:S(2)}) collective-permute-start(bf16[2,128,512]{2,1,0:T(8,128)(2,1)} %get-tuple-element.57), channel_id=1, source_target_pairs={{0,192},{64,128},{128,64},{192,0},{1,193},{65,129},{129,65},{193,1... | collective-permute-start | bytes 786440 | tf_op jit(solution)/shard_map/ppermute | solution.py:29
  113.6 1.2 copy-start.5
  115.5 0.6 copy-start.8
  116.2 0.7 copy-start.9
  116.9 0.7 copy-start.10
  117.5 9.3 %collective-permute-start.3 = (bf16[1,128,512]{2,1,0:T(8,128)(2,1)}, bf16[1,128,512]{2,1,0:T(8,128)(2,1)S(1)}, u32[]{:S(2)}, u32[]{:S(2)}) collective-permute-start(bf16[1,128,512]{2,1,0:T(8,128)(2,1)} %copy-done.10), channel_id=1, source_target_pairs={{0,64},{64,0},{128,192},{192,128},{1,65},{65,1},{129,193},{193,129... | collective-permute-start | bytes 393224 | tf_op jit(solution)/shard_map/ppermute | solution.py:29
  120.0 13.9 %collective-permute-start.4 = (bf16[1,128,512]{2,1,0:T(8,128)(2,1)}, bf16[1,128,512]{2,1,0:T(8,128)(2,1)S(1)}, u32[]{:S(2)}, u32[]{:S(2)}) collective-permute-start(bf16[1,128,512]{2,1,0:T(8,128)(2,1)} %copy-done.9), channel_id=1, source_target_pairs={{0,128},{64,192},{128,0},{192,64},{1,129},{65,193},{129,1},{193,65... | collective-permute-start | bytes 393224 | tf_op jit(solution)/shard_map/ppermute | solution.py:29
  124.3 13.4 %collective-permute-start.5 = (bf16[1,128,512]{2,1,0:T(8,128)(2,1)}, bf16[1,128,512]{2,1,0:T(8,128)(2,1)S(1)}, u32[]{:S(2)}, u32[]{:S(2)}) collective-permute-start(bf16[1,128,512]{2,1,0:T(8,128)(2,1)} %copy-done.8), channel_id=1, source_target_pairs={{0,192},{64,128},{128,64},{192,0},{1,193},{65,129},{129,65},{193,1... | collective-permute-start | bytes 393224 | tf_op jit(solution)/shard_map/ppermute | solution.py:29
  137.7 2.8 %copy-start.1 = (bf16[24,256,512]{2,1,0:T(8,128)(2,1)S(1)}, bf16[24,256,512]{2,1,0:T(8,128)(2,1)}, u32[]{:S(2)}) copy-start(bf16[24,256,512]{2,1,0:T(8,128)(2,1)} %all-gather.3.cloned.1.call-done) | copy-start | bytes 18874372
  140.5 0.9 copy-start.6
  141.4 0.8 copy-start.7
  142.2 11.9 %copy-start.2 = (bf16[24,256,512]{2,1,0:T(8,128)(2,1)S(1)}, bf16[24,256,512]{2,1,0:T(8,128)(2,1)}, u32[]{:S(2)}) copy-start(bf16[24,256,512]{2,1,0:T(8,128)(2,1)} %all-gather.3.cloned.1.call-done) | copy-start | bytes 18874372
  143.4 10.7 %collective-permute-start.6 = (bf16[128,512]{1,0:T(8,128)(2,1)S(1)}, bf16[128,512]{1,0:T(8,128)(2,1)S(1)}, u32[]{:S(2)}, u32[]{:S(2)}) collective-permute-start(bf16[128,512]{1,0:T(8,128)(2,1)S(1)} %get-tuple-element.62), channel_id=1, source_target_pairs={{0,448},{64,384},{128,320},{192,256},{1,449},{65,385},{129,321},{1... | collective-permute-start | bytes 393224 | tf_op jit(solution)/shard_map/ppermute | solution.py:257
  159.4 9.2 %collective-permute-start.7 = (bf16[128,512]{1,0:T(8,128)(2,1)S(1)}, bf16[128,512]{1,0:T(8,128)(2,1)S(1)}, u32[]{:S(2)}, u32[]{:S(2)}) collective-permute-start(bf16[128,512]{1,0:T(8,128)(2,1)S(1)} %get-tuple-element.68), channel_id=1, source_target_pairs={{0,64},{64,0},{128,192},{192,128},{1,65},{65,1},{129,193},{193,129... | collective-permute-start | bytes 393224 | tf_op jit(solution)/shard_map/ppermute | solution.py:29
  161.3 12.4 %collective-permute-start.8 = (bf16[128,512]{1,0:T(8,128)(2,1)S(1)}, bf16[128,512]{1,0:T(8,128)(2,1)S(1)}, u32[]{:S(2)}, u32[]{:S(2)}) collective-permute-start(bf16[128,512]{1,0:T(8,128)(2,1)S(1)} %get-tuple-element.69), channel_id=1, source_target_pairs={{0,128},{64,192},{128,0},{192,64},{1,129},{65,193},{129,1},{193,65... | collective-permute-start | bytes 393224 | tf_op jit(solution)/shard_map/ppermute | solution.py:29
  166.1 11.3 %collective-permute-start.9 = (bf16[128,512]{1,0:T(8,128)(2,1)S(1)}, bf16[128,512]{1,0:T(8,128)(2,1)S(1)}, u32[]{:S(2)}, u32[]{:S(2)}) collective-permute-start(bf16[128,512]{1,0:T(8,128)(2,1)S(1)} %get-tuple-element.70), channel_id=1, source_target_pairs={{0,192},{64,128},{128,64},{192,0},{1,193},{65,129},{129,65},{193,1... | collective-permute-start | bytes 393224 | tf_op jit(solution)/shard_map/ppermute | solution.py:29
Sparse Core Ops, SparseCore 0:
  18.7 75.8 all-gather.2

commit v4 on v3

--- a/solution.py
+++ b/solution.py
@@ -29,10 +29,8 @@
     return lax.ppermute(block, "stage", [(u, u ^ slot) for u in range(STAGES)])
 
 
-def spread_kernel(source_ref, blocks_ref, features_ref, out_ref, own_a_ref, own_x_ref):
+def spread_kernel(source_ref, blocks_ref, out_ref):
     tiles, picked, rows, _ = blocks_ref.shape
-    own_a_ref[...] = blocks_ref[tile_of(0), 0]
-    own_x_ref[...] = features_ref[tile_of(0)]
     out_ref[...] = jnp.zeros_like(out_ref)
     for t in range(tiles):
         for k in range(1, picked):
@@ -40,63 +38,100 @@
             out_ref[t, :, pl.ds(first, rows)] = blocks_ref[t, k]
 
 
-def spread_blocks(adj_src, adj_blocks, features, halo_rows):
+def spread_blocks(adj_src, adj_blocks, halo_rows):
     tiles, _, rows, _ = adj_blocks.shape
-    width = features.shape[2]
     return pl.pallas_call(
         spread_kernel,
-        out_shape=[
-            jax.ShapeDtypeStruct((tiles, rows, halo_rows), jnp.bfloat16),
-            jax.ShapeDtypeStruct((rows, rows), jnp.bfloat16),
-            jax.ShapeDtypeStruct((rows, width), jnp.bfloat16),
-        ],
-        in_specs=[pl.BlockSpec(memory_space=pltpu.SMEM), VMEM, VMEM],
-        out_specs=[VMEM] * 3,
+        out_shape=jax.ShapeDtypeStruct((tiles, rows, halo_rows), jnp.bfloat16),
+        in_specs=[pl.BlockSpec(memory_space=pltpu.SMEM), VMEM],
+        out_specs=VMEM,
         compiler_params=GRANT,
-    )(adj_src, adj_blocks, features)
-
-
-def pick_kernel(rows_ref, count_ref, history_ref, out_ref):
-    receivers, levels, slots, width = out_ref.shape
+    )(adj_src, adj_blocks)
+
+
+def pick_kernel(rows_ref, count_ref, history_ref, out_ref, pick_ref):
+    receivers, _, slots, width = out_ref.shape
     rows = history_ref.shape[1]
-    slot = lax.broadcasted_iota(jnp.int32, (slots, receivers), 0)
-    wanted = jnp.where(slot < count_ref[0], rows_ref[0], -1)
-    column = lax.broadcasted_iota(jnp.int32, (slots, rows), 1)
-    picks = [
-        jnp.where(wanted[:, p : p + 1] == column, 1.0, 0.0).astype(jnp.bfloat16)
-        for p in range(receivers)
-    ]
-    pick = jnp.concatenate(picks, axis=0)
-    for place in range(levels):
-        got = jnp.dot(pick, history_ref[place], preferred_element_type=jnp.float32)
-        out_ref[:, place] = got.astype(jnp.bfloat16).reshape(receivers, slots, width)
+
+    @pl.when(pl.program_id(0) == 0)
+    def _():
+        slot = lax.broadcasted_iota(jnp.int32, (slots, receivers), 0)
+        wanted = jnp.where(slot < count_ref[...], rows_ref[0], -1)
+        column = lax.broadcasted_iota(jnp.int32, (slots, rows), 1)
+        for p in range(receivers):
+            mask = jnp.where(wanted[:, p : p + 1] == column, 1.0, 0.0)
+            pick_ref[p * slots : (p + 1) * slots] = mask.astype(jnp.bfloat16)
+
+    got = jnp.dot(pick_ref[...], history_ref[0], preferred_element_type=jnp.float32)
+    out_ref[:, 0] = got.astype(jnp.bfloat16).reshape(receivers, slots, width)
 
 
 def pick_rows(levels, send_rows, send_count, history):
     parts, slots = send_rows.shape[1:]
     _, rows, width = history.shape
-    step = 16
-    steps = parts // step
-    by_slot = send_rows.reshape(steps, step, slots).swapaxes(1, 2)
     return pl.pallas_call(
         pick_kernel,
         out_shape=jax.ShapeDtypeStruct((parts, len(levels), slots, width), jnp.bfloat16),
-        grid=(steps,),
+        grid=(len(levels),),
         in_specs=[
-            pl.BlockSpec((1, slots, step), lambda g: (g, 0, 0)),
-            pl.BlockSpec((1, 1, step), lambda g: (g, 0, 0)),
-            pl.BlockSpec(
-                (len(levels), rows, width), lambda g: (levels[0] // len(levels), 0, 0)
-            ),
+            pl.BlockSpec((1, slots, parts), lambda g: (0, 0, 0)),
+            pl.BlockSpec((1, parts), lambda g: (0, 0)),
+            pl.BlockSpec((1, rows, width), lambda g: (levels[0] + g, 0, 0)),
         ],
-        out_specs=pl.BlockSpec((step, len(levels), slots, width), lambda g: (g, 0, 0, 0)),
+        out_specs=pl.BlockSpec((parts, 1, slots, width), lambda g: (0, g, 0, 0)),
+        scratch_shapes=[pltpu.VMEM((parts * slots, rows), jnp.bfloat16)],
         compiler_params=GRANT,
         cost_estimate=pl.CostEstimate(
             flops=2 * len(levels) * parts * slots * rows * width,
             bytes_accessed=2 * len(levels) * (parts * slots + rows) * width,
             transcendentals=0,
         ),
-    )(by_slot, send_count.reshape(steps, 1, step), history)
+    )(send_rows.swapaxes(1, 2), send_count, history)
+
+
+def stage_kernel(*refs):
+    sources, outs, sem = refs[: 2 * STAGES + 2], refs[2 * STAGES + 2 : -1], refs[-1]
+    own_ref, near_refs, far_refs = sources[0], sources[1:STAGES], sources[STAGES : 2 * STAGES - 1]
+    features_ref, blocks_ref, spread_ref = sources[2 * STAGES - 1 :]
+    group_ref, own_x_ref, own_a_ref, spread_out = outs
+    depth = group_ref.shape[3]
+    stage = lax.axis_index("stage")
+    core = lax.axis_index("core")
+    pairs = [
+        (spread_ref, spread_out),
+        (features_ref.at[tile_of(0)], own_x_ref),
+        (blocks_ref.at[tile_of(0), 0], own_a_ref),
+    ]
+    for c in range(CORES):
+        pairs.append((own_ref.at[:, pl.ds(c * depth, depth)], group_ref.at[stage, c]))
+    for r in range(1, STAGES):
+        pairs.append((near_refs[r - 1], group_ref.at[stage ^ r, core]))
+        pairs.append((far_refs[r - 1], group_ref.at[stage ^ r, 1 - core]))
+    copies = [pltpu.make_async_copy(*pair, sem.at[n]) for n, pair in enumerate(pairs)]
+    for copy in copies:
+        copy.start()
+    for copy in copies:
+        copy.wait()
+
+
+def stage_operands(weights, near, far, features, adj_blocks, spread):
+    levels, width, _ = weights.shape
+    tiles, rows, _ = spread.shape
+    sources = [weights, *near, *far, features, adj_blocks, spread]
+    shapes = [
+        (STAGES, CORES, levels, width // CORES, width),
+        (rows, width),
+        (rows, rows),
+        spread.shape,
+    ]
+    return pl.pallas_call(
+        stage_kernel,
+        out_shape=[jax.ShapeDtypeStruct(shape, jnp.bfloat16) for shape in shapes],
+        in_specs=[ANYWHERE] * len(sources),
+        out_specs=[VMEM] * len(shapes),
+        scratch_shapes=[pltpu.SemaphoreType.DMA((2 * STAGES + CORES + 1,))],
+        compiler_params=SMALL,
+    )(*sources)
 
 
 def halo_kernel(levels, arrived_ref, spread_ref, features_ref, *out_refs):
@@ -225,32 +260,34 @@
 
 def local(features, history, weights, send_rows, send_count, adj_src, adj_blocks):
     rows_dev, width = features.shape
-    levels = weights.shape[0]
     tile_rows = adj_blocks.shape[2]
     parts, slots = send_rows.shape[1:]
     halo_rows = parts * slots
+    tiles = features.reshape(STAGES, tile_rows, width)
+
+    outgoing = pick_rows(PIECES[0], send_rows, send_count, history)
+    outgoing, history, adj_blocks, weights = lax.optimization_barrier(
+        (outgoing, history, adj_blocks, weights)
+    )
+    arrived = lax.all_to_all(outgoing, DOM, split_axis=0, concat_axis=0, tiled=True)
+
+    depth = weights.shape[1] // CORES
     core = lax.axis_index("core")
-    tiles = features.reshape(STAGES, tile_rows, width)
-
-    outgoing = pick_rows(PIECES[0], send_rows, send_count, history)
-    outgoing, history, adj_blocks = lax.optimization_barrier((outgoing, history, adj_blocks))
-    spread, own_a, own_x = spread_blocks(adj_src, adj_blocks, tiles, halo_rows)
-    spread, weights = lax.optimization_barrier((spread, weights))
-
-    depth = width // CORES
     own = lax.dynamic_slice_in_dim(weights, core * depth, depth, 1)
-    group = lax.all_gather(own, ("stage", "core")).reshape(STAGES, CORES, levels, depth, width)
-
-    halos = []
-    for following in PIECES[1:] + (None,):
-        arrived = lax.all_to_all(outgoing, DOM, split_axis=0, concat_axis=0, tiled=True)
-        if following is not None:
-            outgoing = pick_rows(following, send_rows, send_count, history)
-            arrived, outgoing, spread = lax.optimization_barrier((arrived, outgoing, spread))
-        sums = halo_sums(arrived, spread, tiles, SMALL)
-        if following is None:
-            sums, group = lax.optimization_barrier((sums, group))
-        halos.append([exchange(block, r) for r, block in enumerate(sums)])
+    near = [exchange(own, r) for r in range(1, STAGES)]
+    spread = spread_blocks(adj_src, adj_blocks, halo_rows)
+    outgoing = pick_rows(PIECES[1], send_rows, send_count, history)
+    arrived, outgoing, spread = lax.optimization_barrier((arrived, outgoing, spread))
+
+    following = lax.all_to_all(outgoing, DOM, split_axis=0, concat_axis=0, tiled=True)
+    sums = halo_sums(arrived, spread, tiles, SMALL)
+    near, token = lax.optimization_barrier((near, sums[0]))
+    sums = [token, *sums[1:]]
+    far = [lax.ppermute(block, "core", [(0, 1), (1, 0)]) for block in near]
+    halos = [[exchange(block, r) for r, block in enumerate(sums)]]
+    group, own_x, own_a, spread = stage_operands(weights, near, far, tiles, adj_blocks, spread)
+    sums = halo_sums(following, spread, tiles, SMALL)
+    halos.append([exchange(block, r) for r, block in enumerate(sums)])
 
     *first, last = chain(0, own_x, own_a, group, halos)
     mirror = [(s, HALVES * STAGES - 1 - s) for s in range(STAGES)]

time: 186 us -> 231 us (1.24)
  the two profiles are of different devices: /device:TPU:322 before, /device:TPU:6 now
where the time goes in v4:
time: 231 us; the launch traced here: 229 us
  waiting for transfers between devices  124 us (54%)
  starting transfers between devices  74.1 us (32%)
  Pallas kernels  21.3 us (9%)
  local copies, waits for them, and re-layouts  9.53 us (4%)
    ppermute x12, waiting for transfers between devices, exchange(): return lax.ppermute(block, 'stage', [(u, u ^ slot) for u in range(STAGES)])  77.3 us
    ppermute x12, starting transfers between devices, exchange(): return lax.ppermute(block, 'stage', [(u, u ^ slot) for u in range(STAGES)])  44.6 us
    all_to_all x2, waiting for transfers between devices, local(): lax.all_to_all(outgoing, DOM, split_axis=0, concat_axis=0, tiled=True)  43.7 us
    all_to_all x2, starting transfers between devices, local(): lax.all_to_all(outgoing, DOM, split_axis=0, concat_axis=0, tiled=True)  19.2 us
    unnamed x20, local copies, waits for them, and re-layouts  8.34 us
    pallas_call x2, Pallas kernels, pick_rows(): pl.pallas_call(pick_kernel, out_shape=jax.ShapeDtypeStruct((parts, len(le...  6.57 us
    ppermute x3, starting transfers between devices, local(): far = [lax.ppermute(block, 'core', [(0, 1), (1, 0)]) for block in near]  6.24 us
    pallas_call x2, Pallas kernels, chain(): pl.pallas_call(lambda *refs: chain_kernel(which, betas, *refs), out_shape...  6.15 us
  transfers between devices with their start and end apart: 18, of which 7 were waited for; matrix products, arithmetic and copies ran while one was open for 1% of the time, Pallas kernels for 5%

profile of v4, /device:TPU:6, one launch (start us, length us, event | category | flops | bytes accessed | tf_op | source)
XLA Modules:
  0.0 228.7 jit_solution(3061155195988477642)
XLA Ops:
  0.0 3.8 %shard_map.73 = bf16[64,2,16,512]{3,2,1,0:T(8,128)(2,1)} custom-call(s32[1,16,64]{2,1,0:T(8,128)} %bitcast.6, s32[1,64]{1,0:T(1,128)} %count_ref.3, bf16[3,512,512]{2,1,0:T(8,128)(2,1)} %history_ref.2), custom_call_target="tpu_custom_call" | custom-call | flops 1073741824 | bytes 3145728 | tf_op jit(solution)/shard_map/pallas_call | solution.py:72
  3.8 11.1 %all-to-all-start = ((bf16[64,2,16,512]{3,2,1,0:T(8,128)(2,1)}), bf16[64,2,16,512]{3,2,1,0:T(8,128)(2,1)}, u32[]{:S(2)}, u32[]{:S(2)}) async-start(bf16[64,2,16,512]{3,2,1,0:T(8,128)(2,1)} %shard_map.73), calls=%async_computation | async-start | bytes 4194304 | tf_op jit(solution)/shard_map/all_to_all | solution.py:272
  14.9 2.4 %shard_map.75.refs_1_.refs_9_ = bf16[4,128,1024]{2,1,0:T(8,128)(2,1)} custom-call(s32[4,6]{1,0:T(4,128)} %source_ref.1, bf16[4,6,128,128]{3,2,1,0:T(8,128)(2,1)} %refs_8_), custom_call_target="tpu_custom_call" | custom-call | tf_op jit(solution)/shard_map/pallas_call | solution.py:43
  17.3 2.8 %shard_map.74 = bf16[64,1,16,512]{3,2,1,0:T(8,128)(2,1)} custom-call(s32[1,16,64]{2,1,0:T(8,128)} %bitcast.7, s32[1,64]{1,0:T(1,128)} %count_ref.3, bf16[3,512,512]{2,1,0:T(8,128)(2,1)} %history_ref.2), custom_call_target="tpu_custom_call" | custom-call | flops 536870912 | bytes 1572864 | tf_op jit(solution)/shard_map/pallas_call | solution.py:72
  20.1 43.7 %all-to-all-done.refs_0_ = bf16[64,2,16,512]{3,2,1,0:T(8,128)(2,1)} async-done(((bf16[64,2,16,512]{3,2,1,0:T(8,128)(2,1)}), bf16[64,2,16,512]{3,2,1,0:T(8,128)(2,1)}, u32[]{:S(2)}, u32[]{:S(2)}) %all-to-all-start) | async-done | bytes 2097184 | tf_op jit(solution)/shard_map/all_to_all | solution.py:272
  63.8 8.1 %all-to-all-start.1 = ((bf16[64,1,16,512]{3,2,1,0:T(8,128)(2,1)}), bf16[64,1,16,512]{3,2,1,0:T(8,128)(2,1)S(1)}, u32[]{:S(2)}, u32[]{:S(2)}) async-start(bf16[64,1,16,512]{3,2,1,0:T(8,128)(2,1)} %shard_map.74), calls=%async_computation.1 | async-start | bytes 2097152 | tf_op jit(solution)/shard_map/all_to_all | solution.py:282
  71.9 1.2 constant_dynamic-slice_fusion
  73.1 0.0 copy-start.3
  73.1 0.0 copy-start.4
  73.1 7.9 %collective-permute-start.2 = (bf16[3,256,512]{2,1,0:T(8,128)(2,1)S(1)}, bf16[3,256,512]{2,1,0:T(8,128)(2,1)S(1)}, u32[]{:S(2)}, u32[]{:S(2)}) collective-permute-start(bf16[3,256,512]{2,1,0:T(8,128)(2,1)S(1)} %constant_dynamic-slice_fusion), channel_id=1, source_target_pairs={{0,192},{64,128},{128,64},{192,0},{1,193},{65,129},{129,65},{193,1... | collective-permute-start | bytes 2359304 | tf_op jit(solution)/shard_map/ppermute | solution.py:29
  81.0 1.9 collective-permute-start.1
  83.0 2.5 %collective-permute-start = (bf16[3,256,512]{2,1,0:T(8,128)(2,1)S(1)}, bf16[3,256,512]{2,1,0:T(8,128)(2,1)S(1)}, u32[]{:S(2)}, u32[]{:S(2)}) collective-permute-start(bf16[3,256,512]{2,1,0:T(8,128)(2,1)S(1)} %constant_dynamic-slice_fusion), channel_id=1, source_target_pairs={{0,64},{64,0},{128,192},{192,128},{1,65},{65,1},{129,193},{193,129... | collective-permute-start | bytes 2359304 | tf_op jit(solution)/shard_map/ppermute | solution.py:29
  85.5 3.7 %shard_map.76 = (bf16[2,128,512]{2,1,0:T(8,128)(2,1)S(1)}, bf16[2,128,512]{2,1,0:T(8,128)(2,1)}, bf16[2,128,512]{2,1,0:T(8,128)(2,1)}, bf16[2,128,512]{2,1,0:T(8,128)(2,1)}) custom-call(bf16[64,2,16,512]{3,2,1,0:T(8,128)(2,1)} %all-to-all-done.refs_0_, bf16[4,128,1024]{2,1,0:T(8,128)(2,1)S(1)} %copy-done.2, bf16[4,128,512]{2,1,0:T(8,128)(2,1)S(1)} %bitcast.3), custom_call_target="tpu_custom_call" | custom-call | flops 1073741824 | bytes 4718592 | tf_op jit(solution)/shard_map/pallas_call | solution.py:153
  89.1 10.4 %collective-permute-done.2.refs_3_ = bf16[3,256,512]{2,1,0:T(8,128)(2,1)S(1)} collective-permute-done((bf16[3,256,512]{2,1,0:T(8,128)(2,1)S(1)}, bf16[3,256,512]{2,1,0:T(8,128)(2,1)S(1)}, u32[]{:S(2)}, u32[]{:S(2)}) %collective-permute-start.2) | collective-permute-done | bytes 786464 | tf_op jit(solution)/shard_map/ppermute | solution.py:29
  99.5 48.1 %collective-permute-done.1.refs_2_ = bf16[3,256,512]{2,1,0:T(8,128)(2,1)S(1)} collective-permute-done((bf16[3,256,512]{2,1,0:T(8,128)(2,1)S(1)}, bf16[3,256,512]{2,1,0:T(8,128)(2,1)S(1)}, u32[]{:S(2)}, u32[]{:S(2)}) %collective-permute-start.1) | collective-permute-done | bytes 786464 | tf_op jit(solution)/shard_map/ppermute | solution.py:29
  147.6 0.0 collective-permute-done.refs_1_
  147.6 1.9 collective-permute-start.3
  149.5 2.4 %collective-permute-start.4 = (bf16[3,256,512]{2,1,0:T(8,128)(2,1)S(1)}, bf16[3,256,512]{2,1,0:T(8,128)(2,1)S(1)}, u32[]{:S(2)}, u32[]{:S(2)}) collective-permute-start(bf16[3,256,512]{2,1,0:T(8,128)(2,1)S(1)} %collective-permute-done.1.refs_2_), channel_id=1, source_target_pairs={{0,1},{1,0},{2,3},{3,2},{4,5},{5,4},{6,7},{7,6},{8,9},{9,8},{10,11... | collective-permute-start | bytes 2359304 | tf_op jit(solution)/shard_map/ppermute | solution.py:286
  152.0 1.9 collective-permute-start.5
  153.9 1.9 collective-permute-start.6
  155.8 5.1 %collective-permute-start.7 = (bf16[2,128,512]{2,1,0:T(8,128)(2,1)}, bf16[2,128,512]{2,1,0:T(8,128)(2,1)S(1)}, u32[]{:S(2)}, u32[]{:S(2)}) collective-permute-start(bf16[2,128,512]{2,1,0:T(8,128)(2,1)} %get-tuple-element.52), channel_id=1, source_target_pairs={{0,128},{64,192},{128,0},{192,64},{1,129},{65,193},{129,1},{193,65... | collective-permute-start | bytes 786440 | tf_op jit(solution)/shard_map/ppermute | solution.py:29
  160.9 0.0 collective-permute-done.3.refs_4_
  160.9 3.1 %collective-permute-start.8 = (bf16[2,128,512]{2,1,0:T(8,128)(2,1)}, bf16[2,128,512]{2,1,0:T(8,128)(2,1)}, u32[]{:S(2)}, u32[]{:S(2)}) collective-permute-start(bf16[2,128,512]{2,1,0:T(8,128)(2,1)} %get-tuple-element.53), channel_id=1, source_target_pairs={{0,192},{64,128},{128,64},{192,0},{1,193},{65,129},{129,65},{193,1... | collective-permute-start | bytes 786440 | tf_op jit(solution)/shard_map/ppermute | solution.py:29
  164.0 0.0 collective-permute-done.4.refs_5_
  164.0 0.0 collective-permute-done.5.refs_6_
  164.1 1.0 shard_map.77
  165.1 2.6 %copy-done = bf16[4,2,3,256,512]{4,3,2,1,0:T(8,128)(2,1)} copy-done((bf16[4,2,3,256,512]{4,3,2,1,0:T(8,128)(2,1)}, bf16[4,2,3,256,512]{4,3,2,1,0:T(8,128)(2,1)S(1)}, u32[]{:S(2)}) %copy-start) | copy-done | bytes 6291480
  167.7 1.1 copy-done.6
  168.8 0.6 copy-done.8
  169.4 1.2 copy-done.7
  170.6 0.7 shard_map.78
  171.3 1.9 collective-permute-start.9
  173.3 5.1 %collective-permute-start.10 = (bf16[1,128,512]{2,1,0:T(8,128)(2,1)S(1)}, bf16[1,128,512]{2,1,0:T(8,128)(2,1)S(1)}, u32[]{:S(2)}, u32[]{:S(2)}) collective-permute-start(bf16[1,128,512]{2,1,0:T(8,128)(2,1)S(1)} %get-tuple-element.58), channel_id=1, source_target_pairs={{0,128},{64,192},{128,0},{192,64},{1,129},{65,193},{129,1},{193,65... | collective-permute-start | bytes 393224 | tf_op jit(solution)/shard_map/ppermute | solution.py:29
  178.4 0.0 collective-permute-done.6.refs_4_
  178.4 3.1 %collective-permute-start.11 = (bf16[1,128,512]{2,1,0:T(8,128)(2,1)S(1)}, bf16[1,128,512]{2,1,0:T(8,128)(2,1)S(1)}, u32[]{:S(2)}, u32[]{:S(2)}) collective-permute-start(bf16[1,128,512]{2,1,0:T(8,128)(2,1)S(1)} %get-tuple-element.59), channel_id=1, source_target_pairs={{0,192},{64,128},{128,64},{192,0},{1,193},{65,129},{129,65},{193,1... | collective-permute-start | bytes 393224 | tf_op jit(solution)/shard_map/ppermute | solution.py:29
  181.5 0.4 collective-permute-done.9.refs_8_
  181.9 11.7 %collective-permute-done.10.refs_9_ = bf16[1,128,512]{2,1,0:T(8,128)(2,1)S(1)} collective-permute-done((bf16[1,128,512]{2,1,0:T(8,128)(2,1)S(1)}, bf16[1,128,512]{2,1,0:T(8,128)(2,1)S(1)}, u32[]{:S(2)}, u32[]{:S(2)}) %collective-permute-start.10) | collective-permute-done | bytes 131104 | tf_op jit(solution)/shard_map/ppermute | solution.py:29
  193.6 2.8 %copy-done.1 = bf16[4,2,3,256,512]{4,3,2,1,0:T(8,128)(2,1)S(1)} copy-done((bf16[4,2,3,256,512]{4,3,2,1,0:T(8,128)(2,1)S(1)}, bf16[4,2,3,256,512]{4,3,2,1,0:T(8,128)(2,1)}, u32[]{:S(2)}) %copy-start.1) | copy-done | bytes 6291480
  196.4 5.2 %shard_map.79 = (bf16[128,512]{1,0:T(8,128)(2,1)S(1)}, bf16[128,512]{1,0:T(8,128)(2,1)S(1)}, bf16[128,512]{1,0:T(8,128)(2,1)S(1)}, bf16[128,512]{1,0:T(8,128)(2,1)S(1)}, bf16[128,512]{1,0:T(8,128)(2,1)S(1)}) custom-call(bf16[128,512]{1,0:T(8,128)(2,1)S(1)} %get-tuple-element.47.refs_0_, bf16[128,128]{1,0:T(8,128)(2,1)S(1)} %copy-done.9, ...), custom_call_target="tpu_custom_call" | custom-call | flops 1006632960 | bytes 7864320 | tf_op jit(solution)/shard_map/pallas_call | solution.py:227
  201.5 4.0 %collective-permute-start.12 = (bf16[128,512]{1,0:T(8,128)(2,1)S(1)}, bf16[128,512]{1,0:T(8,128)(2,1)S(1)}, u32[]{:S(2)}, u32[]{:S(2)}) collective-permute-start(bf16[128,512]{1,0:T(8,128)(2,1)S(1)} %get-tuple-element.60), channel_id=1, source_target_pairs={{0,448},{64,384},{128,320},{192,256},{1,449},{65,385},{129,321},{1... | collective-permute-start | bytes 393224 | tf_op jit(solution)/shard_map/ppermute | solution.py:294
  205.5 2.5 %collective-permute-done.12.refs_0_ = bf16[128,512]{1,0:T(8,128)(2,1)S(1)} collective-permute-done((bf16[128,512]{1,0:T(8,128)(2,1)S(1)}, bf16[128,512]{1,0:T(8,128)(2,1)S(1)}, u32[]{:S(2)}, u32[]{:S(2)}) %collective-permute-start.12) | collective-permute-done | bytes 131104 | tf_op jit(solution)/shard_map/ppermute | solution.py:294
  208.0 1.0 shard_map.80
  209.0 5.9 %collective-permute-start.13 = (bf16[128,512]{1,0:T(8,128)(2,1)S(1)}, bf16[128,512]{1,0:T(8,128)(2,1)S(1)}, u32[]{:S(2)}, u32[]{:S(2)}) collective-permute-start(bf16[128,512]{1,0:T(8,128)(2,1)S(1)} %get-tuple-element.66), channel_id=1, source_target_pairs={{0,64},{64,0},{128,192},{192,128},{1,65},{65,1},{129,193},{193,129... | collective-permute-start | bytes 393224 | tf_op jit(solution)/shard_map/ppermute | solution.py:29
  214.9 1.9 collective-permute-start.14
  216.8 4.3 %collective-permute-start.15 = (bf16[128,512]{1,0:T(8,128)(2,1)S(1)}, bf16[128,512]{1,0:T(8,128)(2,1)S(1)}, u32[]{:S(2)}, u32[]{:S(2)}) collective-permute-start(bf16[128,512]{1,0:T(8,128)(2,1)S(1)} %get-tuple-element.68), channel_id=1, source_target_pairs={{0,192},{64,128},{128,64},{192,0},{1,193},{65,129},{129,65},{193,1... | collective-permute-start | bytes 393224 | tf_op jit(solution)/shard_map/ppermute | solution.py:29
  221.1 6.8 %collective-permute-done.14.refs_2_ = bf16[128,512]{1,0:T(8,128)(2,1)S(1)} collective-permute-done((bf16[128,512]{1,0:T(8,128)(2,1)S(1)}, bf16[128,512]{1,0:T(8,128)(2,1)S(1)}, u32[]{:S(2)}, u32[]{:S(2)}) %collective-permute-start.14) | collective-permute-done | bytes 131104 | tf_op jit(solution)/shard_map/ppermute | solution.py:29
  227.9 0.0 collective-permute-done.15.refs_3_
  227.9 0.8 shard_map.81
  (18 shorter events, 0.0 us)
Async XLA Ops:
  3.8 60.0 %all-to-all-start = ((bf16[64,2,16,512]{3,2,1,0:T(8,128)(2,1)}), bf16[64,2,16,512]{3,2,1,0:T(8,128)(2,1)}, u32[]{:S(2)}, u32[]{:S(2)}) async-start(bf16[64,2,16,512]{3,2,1,0:T(8,128)(2,1)} %shard_map.73), calls=%async_computation | async-start | bytes 4194304 | tf_op jit(solution)/shard_map/all_to_all | solution.py:272
  20.1 65.3 %copy-start.2 = (bf16[4,128,1024]{2,1,0:T(8,128)(2,1)S(1)}, bf16[4,128,1024]{2,1,0:T(8,128)(2,1)}, u32[]{:S(2)}) copy-start(bf16[4,128,1024]{2,1,0:T(8,128)(2,1)} %shard_map.75.refs_1_.refs_9_) | copy-start | bytes 3145732
  20.1 65.4 %copy-start.5 = (bf16[512,512]{1,0:T(8,128)(2,1)S(1)}, bf16[512,512]{1,0:T(8,128)(2,1)}, u32[]{:S(2)}) copy-start(bf16[512,512]{1,0:T(8,128)(2,1)} %param.7) | copy-start | bytes 1572868
  63.8 105.6 %all-to-all-start.1 = ((bf16[64,1,16,512]{3,2,1,0:T(8,128)(2,1)}), bf16[64,1,16,512]{3,2,1,0:T(8,128)(2,1)S(1)}, u32[]{:S(2)}, u32[]{:S(2)}) async-start(bf16[64,1,16,512]{3,2,1,0:T(8,128)(2,1)} %shard_map.74), calls=%async_computation.1 | async-start | bytes 2097152 | tf_op jit(solution)/shard_map/all_to_all | solution.py:282
  73.1 91.0 %copy-start.3 = (bf16[3,512,512]{2,1,0:T(8,128)(2,1)S(1)}, bf16[3,512,512]{2,1,0:T(8,128)(2,1)}, u32[]{:S(2)}) copy-start(bf16[3,512,512]{2,1,0:T(8,128)(2,1)} %refs_0_) | copy-start | bytes 4718596
  73.1 91.0 %copy-start.4 = (bf16[4,6,128,128]{3,2,1,0:T(8,128)(2,1)S(1)}, bf16[4,6,128,128]{3,2,1,0:T(8,128)(2,1)}, u32[]{:S(2)}) copy-start(bf16[4,6,128,128]{3,2,1,0:T(8,128)(2,1)} %refs_8_) | copy-start | bytes 2359300
  73.1 26.4 %collective-permute-start.2 = (bf16[3,256,512]{2,1,0:T(8,128)(2,1)S(1)}, bf16[3,256,512]{2,1,0:T(8,128)(2,1)S(1)}, u32[]{:S(2)}, u32[]{:S(2)}) collective-permute-start(bf16[3,256,512]{2,1,0:T(8,128)(2,1)S(1)} %constant_dynamic-slice_fusion), channel_id=1, source_target_pairs={{0,192},{64,128},{128,64},{192,0},{1,193},{65,129},{129,65},{193,1... | collective-permute-start | bytes 2359304 | tf_op jit(solution)/shard_map/ppermute | solution.py:29
  81.0 66.6 %collective-permute-start.1 = (bf16[3,256,512]{2,1,0:T(8,128)(2,1)S(1)}, bf16[3,256,512]{2,1,0:T(8,128)(2,1)S(1)}, u32[]{:S(2)}, u32[]{:S(2)}) collective-permute-start(bf16[3,256,512]{2,1,0:T(8,128)(2,1)S(1)} %constant_dynamic-slice_fusion), channel_id=1, source_target_pairs={{0,128},{64,192},{128,0},{192,64},{1,129},{65,193},{129,1},{193,65... | collective-permute-start | bytes 2359304 | tf_op jit(solution)/shard_map/ppermute | solution.py:29
  83.0 64.7 %collective-permute-start = (bf16[3,256,512]{2,1,0:T(8,128)(2,1)S(1)}, bf16[3,256,512]{2,1,0:T(8,128)(2,1)S(1)}, u32[]{:S(2)}, u32[]{:S(2)}) collective-permute-start(bf16[3,256,512]{2,1,0:T(8,128)(2,1)S(1)} %constant_dynamic-slice_fusion), channel_id=1, source_target_pairs={{0,64},{64,0},{128,192},{192,128},{1,65},{65,1},{129,193},{193,129... | collective-permute-start | bytes 2359304 | tf_op jit(solution)/shard_map/ppermute | solution.py:29
  147.6 13.3 %collective-permute-start.3 = (bf16[3,256,512]{2,1,0:T(8,128)(2,1)S(1)}, bf16[3,256,512]{2,1,0:T(8,128)(2,1)S(1)}, u32[]{:S(2)}, u32[]{:S(2)}) collective-permute-start(bf16[3,256,512]{2,1,0:T(8,128)(2,1)S(1)} %collective-permute-done.refs_1_), channel_id=1, source_target_pairs={{0,1},{1,0},{2,3},{3,2},{4,5},{5,4},{6,7},{7,6},{8,9},{9,8},{10,11... | collective-permute-start | bytes 2359304 | tf_op jit(solution)/shard_map/ppermute | solution.py:286
  149.5 14.5 %collective-permute-start.4 = (bf16[3,256,512]{2,1,0:T(8,128)(2,1)S(1)}, bf16[3,256,512]{2,1,0:T(8,128)(2,1)S(1)}, u32[]{:S(2)}, u32[]{:S(2)}) collective-permute-start(bf16[3,256,512]{2,1,0:T(8,128)(2,1)S(1)} %collective-permute-done.1.refs_2_), channel_id=1, source_target_pairs={{0,1},{1,0},{2,3},{3,2},{4,5},{5,4},{6,7},{7,6},{8,9},{9,8},{10,11... | collective-permute-start | bytes 2359304 | tf_op jit(solution)/shard_map/ppermute | solution.py:286
  152.0 12.1 %collective-permute-start.5 = (bf16[3,256,512]{2,1,0:T(8,128)(2,1)S(1)}, bf16[3,256,512]{2,1,0:T(8,128)(2,1)S(1)}, u32[]{:S(2)}, u32[]{:S(2)}) collective-permute-start(bf16[3,256,512]{2,1,0:T(8,128)(2,1)S(1)} %collective-permute-done.2.refs_3_), channel_id=1, source_target_pairs={{0,1},{1,0},{2,3},{3,2},{4,5},{5,4},{6,7},{7,6},{8,9},{9,8},{10,11... | collective-permute-start | bytes 2359304 | tf_op jit(solution)/shard_map/ppermute | solution.py:286
  153.9 24.5 %collective-permute-start.6 = (bf16[2,128,512]{2,1,0:T(8,128)(2,1)}, bf16[2,128,512]{2,1,0:T(8,128)(2,1)S(1)}, u32[]{:S(2)}, u32[]{:S(2)}) collective-permute-start(bf16[2,128,512]{2,1,0:T(8,128)(2,1)} %get-tuple-element.51), channel_id=1, source_target_pairs={{0,64},{64,0},{128,192},{192,128},{1,65},{65,1},{129,193},{193,129... | collective-permute-start | bytes 786440 | tf_op jit(solution)/shard_map/ppermute | solution.py:29
  155.8 25.7 %collective-permute-start.7 = (bf16[2,128,512]{2,1,0:T(8,128)(2,1)}, bf16[2,128,512]{2,1,0:T(8,128)(2,1)S(1)}, u32[]{:S(2)}, u32[]{:S(2)}) collective-permute-start(bf16[2,128,512]{2,1,0:T(8,128)(2,1)} %get-tuple-element.52), channel_id=1, source_target_pairs={{0,128},{64,192},{128,0},{192,64},{1,129},{65,193},{129,1},{193,65... | collective-permute-start | bytes 786440 | tf_op jit(solution)/shard_map/ppermute | solution.py:29
  160.9 20.6 %collective-permute-start.8 = (bf16[2,128,512]{2,1,0:T(8,128)(2,1)}, bf16[2,128,512]{2,1,0:T(8,128)(2,1)}, u32[]{:S(2)}, u32[]{:S(2)}) collective-permute-start(bf16[2,128,512]{2,1,0:T(8,128)(2,1)} %get-tuple-element.53), channel_id=1, source_target_pairs={{0,192},{64,128},{128,64},{192,0},{1,193},{65,129},{129,65},{193,1... | collective-permute-start | bytes 786440 | tf_op jit(solution)/shard_map/ppermute | solution.py:29
  165.1 2.6 %copy-start = (bf16[4,2,3,256,512]{4,3,2,1,0:T(8,128)(2,1)}, bf16[4,2,3,256,512]{4,3,2,1,0:T(8,128)(2,1)S(1)}, u32[]{:S(2)}) copy-start(bf16[4,2,3,256,512]{4,3,2,1,0:T(8,128)(2,1)S(1)} %get-tuple-element.49.refs_2_) | copy-start | bytes 18874372
  167.7 1.1 copy-start.6
  168.8 0.6 copy-start.8
  169.4 1.2 copy-start.7
  170.6 22.9 %copy-start.9 = (bf16[128,128]{1,0:T(8,128)(2,1)S(1)}, bf16[128,128]{1,0:T(8,128)(2,1)}, u32[]{:S(2)}) copy-start(bf16[128,128]{1,0:T(8,128)(2,1)} %copy-done.8) | copy-start | bytes 98308
  171.3 10.5 %collective-permute-start.9 = (bf16[1,128,512]{2,1,0:T(8,128)(2,1)S(1)}, bf16[1,128,512]{2,1,0:T(8,128)(2,1)S(1)}, u32[]{:S(2)}, u32[]{:S(2)}) collective-permute-start(bf16[1,128,512]{2,1,0:T(8,128)(2,1)S(1)} %get-tuple-element.57), channel_id=1, source_target_pairs={{0,64},{64,0},{128,192},{192,128},{1,65},{65,1},{129,193},{193,129... | collective-permute-start | bytes 393224 | tf_op jit(solution)/shard_map/ppermute | solution.py:29
  173.3 20.3 %collective-permute-start.10 = (bf16[1,128,512]{2,1,0:T(8,128)(2,1)S(1)}, bf16[1,128,512]{2,1,0:T(8,128)(2,1)S(1)}, u32[]{:S(2)}, u32[]{:S(2)}) collective-permute-start(bf16[1,128,512]{2,1,0:T(8,128)(2,1)S(1)} %get-tuple-element.58), channel_id=1, source_target_pairs={{0,128},{64,192},{128,0},{192,64},{1,129},{65,193},{129,1},{193,65... | collective-permute-start | bytes 393224 | tf_op jit(solution)/shard_map/ppermute | solution.py:29
  178.4 15.2 %collective-permute-start.11 = (bf16[1,128,512]{2,1,0:T(8,128)(2,1)S(1)}, bf16[1,128,512]{2,1,0:T(8,128)(2,1)S(1)}, u32[]{:S(2)}, u32[]{:S(2)}) collective-permute-start(bf16[1,128,512]{2,1,0:T(8,128)(2,1)S(1)} %get-tuple-element.59), channel_id=1, source_target_pairs={{0,192},{64,128},{128,64},{192,0},{1,193},{65,129},{129,65},{193,1... | collective-permute-start | bytes 393224 | tf_op jit(solution)/shard_map/ppermute | solution.py:29
  193.6 2.8 %copy-start.1 = (bf16[4,2,3,256,512]{4,3,2,1,0:T(8,128)(2,1)S(1)}, bf16[4,2,3,256,512]{4,3,2,1,0:T(8,128)(2,1)}, u32[]{:S(2)}) copy-start(bf16[4,2,3,256,512]{4,3,2,1,0:T(8,128)(2,1)} %copy-done) | copy-start | bytes 18874372
  201.5 6.5 %collective-permute-start.12 = (bf16[128,512]{1,0:T(8,128)(2,1)S(1)}, bf16[128,512]{1,0:T(8,128)(2,1)S(1)}, u32[]{:S(2)}, u32[]{:S(2)}) collective-permute-start(bf16[128,512]{1,0:T(8,128)(2,1)S(1)} %get-tuple-element.60), channel_id=1, source_target_pairs={{0,448},{64,384},{128,320},{192,256},{1,449},{65,385},{129,321},{1... | collective-permute-start | bytes 393224 | tf_op jit(solution)/shard_map/ppermute | solution.py:294
  209.0 12.1 %collective-permute-start.13 = (bf16[128,512]{1,0:T(8,128)(2,1)S(1)}, bf16[128,512]{1,0:T(8,128)(2,1)S(1)}, u32[]{:S(2)}, u32[]{:S(2)}) collective-permute-start(bf16[128,512]{1,0:T(8,128)(2,1)S(1)} %get-tuple-element.66), channel_id=1, source_target_pairs={{0,64},{64,0},{128,192},{192,128},{1,65},{65,1},{129,193},{193,129... | collective-permute-start | bytes 393224 | tf_op jit(solution)/shard_map/ppermute | solution.py:29
  214.9 13.0 %collective-permute-start.14 = (bf16[128,512]{1,0:T(8,128)(2,1)S(1)}, bf16[128,512]{1,0:T(8,128)(2,1)S(1)}, u32[]{:S(2)}, u32[]{:S(2)}) collective-permute-start(bf16[128,512]{1,0:T(8,128)(2,1)S(1)} %get-tuple-element.67), channel_id=1, source_target_pairs={{0,128},{64,192},{128,0},{192,64},{1,129},{65,193},{129,1},{193,65... | collective-permute-start | bytes 393224 | tf_op jit(solution)/shard_map/ppermute | solution.py:29
  216.8 11.0 %collective-permute-start.15 = (bf16[128,512]{1,0:T(8,128)(2,1)S(1)}, bf16[128,512]{1,0:T(8,128)(2,1)S(1)}, u32[]{:S(2)}, u32[]{:S(2)}) collective-permute-start(bf16[128,512]{1,0:T(8,128)(2,1)S(1)} %get-tuple-element.68), channel_id=1, source_target_pairs={{0,192},{64,128},{128,64},{192,0},{1,193},{65,129},{129,65},{193,1... | collective-permute-start | bytes 393224 | tf_op jit(solution)/shard_map/ppermute | solution.py:29

commit v5 on v4

v5 whole, which is shorter than its diff:
```python
import jax
import jax.numpy as jnp
import numpy as np
from jax import lax
from jax.experimental import pallas as pl
from jax.experimental.pallas import tpu as pltpu
from jax.sharding import Mesh, PartitionSpec as P

HALVES = 2
STAGES = 4
CORES = 2
SEGMENT = ("half", "stage")
DOM = ("pair", "core")
ANYWHERE = pl.BlockSpec(memory_space=pl.ANY)
VMEM = pl.BlockSpec(memory_space=pltpu.VMEM)
GRANT = pltpu.CompilerParams(vmem_limit_bytes=60 * 1024 * 1024)
SMALL = pltpu.CompilerParams(vmem_limit_bytes=24 * 1024 * 1024)


def tile_of(slot):
    mirror = lax.axis_index("half") * (STAGES - 1)
    return lax.axis_index("stage") ^ mirror ^ slot


def exchange(block, slot):
    return lax.ppermute(block, "stage", [(u, u ^ slot) for u in range(STAGES)])


def exchange_all(blocks):
    return [blocks[0]] + [exchange(blocks[slot], slot) for slot in range(1, STAGES)]


def swap_cores(block):
    return lax.ppermute(block, "core", [(0, 1), (1, 0)])


def spread_kernel(source_ref, blocks_ref, out_ref):
    tiles, picked, rows, _ = blocks_ref.shape
    out_ref[...] = jnp.zeros_like(out_ref)
    for t in range(tiles):
        for k in range(1, picked):
            first = pl.multiple_of((source_ref[t, k] - 1) * rows, rows)
            out_ref[t, :, pl.ds(first, rows)] = blocks_ref[t, k]


def spread_blocks(adj_src, adj_blocks, halo_rows):
    tiles, _, rows, _ = adj_blocks.shape
    return pl.pallas_call(
        spread_kernel,
        out_shape=jax.ShapeDtypeStruct((tiles, rows, halo_rows), jnp.bfloat16),
        in_specs=[pl.BlockSpec(memory_space=pltpu.SMEM), VMEM],
        out_specs=VMEM,
        compiler_params=GRANT,
    )(adj_src, adj_blocks)


def pick_kernel(rows_ref, count_ref, history_ref, out_ref, pick_ref):
    receivers, _, slots, width = out_ref.shape
    rows = history_ref.shape[1]

    @pl.when(pl.program_id(0) == 0)
    def _():
        slot = lax.broadcasted_iota(jnp.int32, (slots, receivers), 0)
        wanted = jnp.where(slot < count_ref[...], rows_ref[0], -1)
        column = lax.broadcasted_iota(jnp.int32, (slots, rows), 1)
        for p in range(receivers):
            mask = jnp.where(wanted[:, p : p + 1] == column, 1.0, 0.0)
            pick_ref[p * slots : (p + 1) * slots] = mask.astype(jnp.bfloat16)

    got = jnp.dot(pick_ref[...], history_ref[0], preferred_element_type=jnp.float32)
    out_ref[:, 0] = got.astype(jnp.bfloat16).reshape(receivers, slots, width)


def pick_rows(send_rows, send_count, history):
    parts, slots = send_rows.shape[1:]
    levels, rows, width = history.shape
    return pl.pallas_call(
        pick_kernel,
        out_shape=jax.ShapeDtypeStruct((parts, levels, slots, width), jnp.bfloat16),
        grid=(levels,),
        in_specs=[
            pl.BlockSpec((1, slots, parts), lambda g: (0, 0, 0)),
            pl.BlockSpec((1, parts), lambda g: (0, 0)),
            pl.BlockSpec((1, rows, width), lambda g: (g, 0, 0)),
        ],
        out_specs=pl.BlockSpec((parts, 1, slots, width), lambda g: (0, g, 0, 0)),
        scratch_shapes=[pltpu.VMEM((parts * slots, rows), jnp.bfloat16)],
        compiler_params=GRANT,
        cost_estimate=pl.CostEstimate(
            flops=2 * levels * parts * slots * rows * width,
            bytes_accessed=2 * levels * (parts * slots + rows) * width,
            transcendentals=0,
        ),
    )(send_rows.swapaxes(1, 2), send_count, history)


def stage_kernel(*refs):
    shards = STAGES
    own_ref, near_refs, far_refs = refs[0], refs[1 : 1 + shards], refs[1 + shards : 1 + 2 * shards]
    features_ref, blocks_ref, group_ref, own_x_ref, own_a_ref, sem = refs[1 + 2 * shards :]
    depth = group_ref.shape[3]
    stage = lax.axis_index("stage")
    core = lax.axis_index("core")
    pairs = [
        (features_ref.at[tile_of(0)], own_x_ref),
        (blocks_ref.at[tile_of(0), 0], own_a_ref),
    ]
    for c in range(CORES):
        pairs.append((own_ref.at[:, pl.ds(c * depth, depth)], group_ref.at[stage, c]))
    for r in range(1, STAGES):
        pairs.append((near_refs[r - 1], group_ref.at[stage ^ r, core]))
        pairs.append((far_refs[r - 1], group_ref.at[stage ^ r, 1 - core]))
    copies = [pltpu.make_async_copy(*pair, sem.at[n]) for n, pair in enumerate(pairs)]
    late = len(copies) - 2
    inner = (stage == 1) | (stage == 2)
    for copy in copies[:late]:
        copy.start()

    @pl.when(inner)
    def _():
        for copy in copies[late:]:
            copy.start()

    @pl.when(jnp.logical_not(inner))
    def _():
        pltpu.make_async_copy(near_refs[-1], pairs[late][1], sem.at[late]).start()
        pltpu.make_async_copy(far_refs[-1], pairs[late + 1][1], sem.at[late + 1]).start()

    for copy in copies:
        copy.wait()


def stage_operands(weights, near, far, features, adj_blocks):
    levels, width, _ = weights.shape
    rows = adj_blocks.shape[2]
    sources = [weights, *near, *far, features, adj_blocks]
    shapes = [(STAGES, CORES, levels, width // CORES, width), (rows, width), (rows, rows)]
    return pl.pallas_call(
        stage_kernel,
        out_shape=[jax.ShapeDtypeStruct(shape, jnp.bfloat16) for shape in shapes],
        in_specs=[ANYWHERE] * len(sources),
        out_specs=[VMEM] * len(shapes),
        scratch_shapes=[pltpu.SemaphoreType.DMA((2 * STAGES + CORES,))],
        compiler_params=SMALL,
        cost_estimate=pl.CostEstimate(
            flops=0, bytes_accessed=4 * STAGES * weights.size, transcendentals=0
        ),
    )(*sources)


def halo_kernel(arrived_ref, spread_ref, features_ref, *out_refs):
    parts, _, slots, width = arrived_ref.shape
    tiles, rows, _ = spread_ref.shape
    spread = jnp.concatenate([spread_ref[tile_of(r)] for r in range(tiles)], axis=0)
    halo = arrived_ref[:, 0].reshape(parts * slots, width)
    summed = jnp.dot(spread, halo, preferred_element_type=jnp.float32)
    for r in range(tiles):
        start = 0.1 * features_ref[tile_of(r)].astype(jnp.float32)
        part = 0.9 * summed[r * rows : (r + 1) * rows] + start
        out_refs[r][0] = part.astype(jnp.bfloat16)


def halo_sums(arrived, spread, features):
    parts, levels, slots, width = arrived.shape
    tiles, rows, halo_rows = spread.shape
    return pl.pallas_call(
        halo_kernel,
        out_shape=[jax.ShapeDtypeStruct((levels, rows, width), jnp.bfloat16)] * tiles,
        grid=(levels,),
        in_specs=[
            pl.BlockSpec((parts, 1, slots, width), lambda g: (0, g, 0, 0)),
            pl.BlockSpec(spread.shape, lambda g: (0, 0, 0)),
            pl.BlockSpec(features.shape, lambda g: (0, 0, 0)),
        ],
        out_specs=[pl.BlockSpec((1, rows, width), lambda g: (g, 0, 0))] * tiles,
        compiler_params=SMALL,
        cost_estimate=pl.CostEstimate(
            flops=2 * levels * tiles * rows * halo_rows * width,
            bytes_accessed=2 * (arrived.size + spread.size + features.size * (1 + levels)),
            transcendentals=0,
        ),
    )(arrived, spread, features)


def chain_kernel(which, betas, x_ref, a_ref, w_ref, *refs):
    stages, cores, levels, depth, _ = w_ref.shape
    h_refs, refs = refs[:stages], refs[stages:]
    if which > 0:
        before_refs, refs = refs[:stages], refs[stages:]
    out_refs, h_buf = refs[:stages], refs[-1]
    half = lax.axis_index("half")
    stage = lax.axis_index("stage")

    @pl.when(half == which)
    def _():
        for r in range(stages):
            h_buf[stage ^ r] = h_refs[r][...]
        a = a_ref[...]
        x = x_ref[...]
        for s in range(stages):
            for i in range(levels):
                beta = betas[(which * stages + s) * levels + i]
                summed = jnp.dot(a, x, preferred_element_type=jnp.float32)
                support = 0.9 * summed + h_buf[s, i].astype(jnp.float32)
                rounded = support.astype(jnp.bfloat16)
                branch = sum(
                    jnp.dot(
                        rounded[:, c * depth : (c + 1) * depth],
                        w_ref[s, c, i],
                        preferred_element_type=jnp.float32,
                    )
                    for c in range(cores)
                )
                mixed = (1.0 - beta) * support + beta * branch
                x = jnp.maximum(mixed, 0.0).astype(jnp.bfloat16)
            for r in range(stages):

                @pl.when(stage ^ s == r)
                def _():
                    out_refs[r][...] = x

        if which == 0:
            refs[stages][...] = x

    if which > 0:

        @pl.when(half != which)
        def _():
            for r in range(stages):
                out_refs[r][...] = before_refs[r][...]


def chain(which, x, a, weights, halos, before=()):
    stages, _, levels, _, width = weights.shape
    rows = x.shape[0]
    order = np.arange(HALVES * stages * levels, dtype=np.float32)
    betas = [float(b) for b in np.log1p(np.float32(1.0) / (order + np.float32(1.0)))]
    outs = stages if before else stages + 1
    return pl.pallas_call(
        lambda *refs: chain_kernel(which, betas, *refs),
        out_shape=[jax.ShapeDtypeStruct((rows, width), jnp.bfloat16)] * outs,
        in_specs=[VMEM] * (3 + len(halos) + len(before)),
        out_specs=[VMEM] * outs,
        scratch_shapes=[pltpu.VMEM((stages, levels, rows, width), jnp.bfloat16)],
        compiler_params=SMALL,
        cost_estimate=pl.CostEstimate(
            flops=2 * stages * levels * rows * width * (width + rows),
            bytes_accessed=2 * stages * levels * width * (width + rows),
            transcendentals=0,
        ),
    )(x, a, weights, *halos, *before)


def place_kernel(*refs):
    in_refs, out_ref = refs[:-1], refs[-1]
    for r, ref in enumerate(in_refs):
        out_ref[0, tile_of(r)] = ref[...]


def place(tiles):
    rows, width = tiles[0].shape
    return pl.pallas_call(
        place_kernel,
        out_shape=jax.ShapeDtypeStruct((1, len(tiles), rows, width), jnp.bfloat16),
        in_specs=[VMEM] * len(tiles),
        out_specs=VMEM,
        compiler_params=SMALL,
    )(*tiles)


def local(features, history, weights, send_rows, send_count, adj_src, adj_blocks):
    rows_dev, width = features.shape
    tile_rows = adj_blocks.shape[2]
    parts, slots = send_rows.shape[1:]
    halo_rows = parts * slots
    tiles = features.reshape(STAGES, tile_rows, width)

    outgoing = pick_rows(send_rows, send_count, history)
    outgoing, adj_blocks, weights = lax.optimization_barrier((outgoing, adj_blocks, weights))
    arrived = lax.all_to_all(outgoing, DOM, split_axis=0, concat_axis=0, tiled=True)

    depth = weights.shape[1] // CORES
    core = lax.axis_index("core")
    own = lax.dynamic_slice_in_dim(weights, core * depth, depth, 1)
    two = exchange(own, 2)
    near = [exchange(own, 1), two]
    own, two = lax.optimization_barrier((own, two))
    near.append(lax.ppermute(own, "stage", [(1, 2), (2, 1)]))
    near.append(lax.ppermute(two, "stage", [(1, 0), (2, 3)]))
    far = [swap_cores(block) for block in near]
    spread = spread_blocks(adj_src, adj_blocks, halo_rows)
    arrived, spread, near, far = lax.optimization_barrier((arrived, spread, near, far))

    sums = halo_sums(arrived, spread, tiles)
    token, weights = lax.optimization_barrier((sums[0], weights))
    halos = exchange_all([token, *sums[1:]])
    group, own_x, own_a = stage_operands(weights, near, far, tiles, adj_blocks)

    *first, last = chain(0, own_x, own_a, group, halos)
    mirror = [(s, HALVES * STAGES - 1 - s) for s in range(STAGES)]
    done = chain(1, lax.ppermute(last, SEGMENT, mirror), own_a, group, halos, first)
    fresh = place(exchange_all(done))
    return fresh.reshape(1, rows_dev, width)


def solution(mesh):
    segments, parts = mesh.devices.shape
    devices = mesh.devices.reshape(HALVES, segments // HALVES, parts // CORES, CORES)
    fine = Mesh(devices, SEGMENT + DOM)
    placed = (
        P(DOM, None),
        P(SEGMENT, DOM, None),
        P(SEGMENT, None, None),
        P(DOM, None, None),
        P(DOM, None),
        P(DOM, None),
        P(DOM, None, None, None),
    )
    return jax.shard_map(
        local, mesh=fine, in_specs=placed, out_specs=P(SEGMENT, DOM, None), check_vma=False
    )
```

time: 231 us -> 171 us (0.74)
  the two profiles are of different devices: /device:TPU:6 before, /device:TPU:322 now
where the time goes in v5:
time: 171 us; the launch traced here: 170 us
  waiting for transfers between devices  96.4 us (56%)
  starting transfers between devices  52 us (30%)
  Pallas kernels  19.3 us (11%)
  local copies, waits for them, and re-layouts  2.34 us (1%)
    ppermute x8, waiting for transfers between devices, exchange(): return lax.ppermute(block, 'stage', [(u, u ^ slot) for u in range(STAGES)])  70.6 us
    ppermute x8, starting transfers between devices, exchange(): return lax.ppermute(block, 'stage', [(u, u ^ slot) for u in range(STAGES)])  25.2 us
    ppermute x1, waiting for transfers between devices, local(): near.append(lax.ppermute(own, 'stage', [(1, 2), (2, 1)]))  11.1 us
    all_to_all x1, starting transfers between devices, local(): lax.all_to_all(outgoing, DOM, split_axis=0, concat_axis=0, tiled=True)  10.9 us
    ppermute x1, waiting for transfers between devices, local(): lax.ppermute(last, SEGMENT, mirror)  8.95 us
    ppermute x4, starting transfers between devices, swap_cores(): return lax.ppermute(block, 'core', [(0, 1), (1, 0)])  8.63 us
    all_to_all x1, waiting for transfers between devices, local(): lax.all_to_all(outgoing, DOM, split_axis=0, concat_axis=0, tiled=True)  5.79 us
    pallas_call x1, Pallas kernels, pick_rows(): pl.pallas_call(pick_kernel, out_shape=jax.ShapeDtypeStruct((parts, levels...  5.3 us
  transfers between devices with their start and end apart: 16, of which 9 were waited for; matrix products, arithmetic and copies ran while one was open for 0% of the time, Pallas kernels for 3%

profile of v5, /device:TPU:322, one launch (start us, length us, event | category | flops | bytes accessed | tf_op | source)
XLA Modules:
  0.0 170.3 jit_solution(7027297099520592808)
XLA Ops:
  0.0 5.3 %shard_map.73 = bf16[64,3,16,512]{3,2,1,0:T(8,128)(2,1)} custom-call(s32[1,16,64]{2,1,0:T(8,128)} %bitcast.5, s32[1,64]{1,0:T(1,128)} %count_ref.1, bf16[3,512,512]{2,1,0:T(8,128)(2,1)} %history_ref.1), custom_call_target="tpu_custom_call" | custom-call | flops 1610612736 | bytes 4718592 | tf_op jit(solution)/shard_map/pallas_call | solution.py:77
  5.3 0.0 copy-start
  5.3 10.9 %all-to-all-start = ((bf16[64,3,16,512]{3,2,1,0:T(8,128)(2,1)}), bf16[64,3,16,512]{3,2,1,0:T(8,128)(2,1)}, u32[]{:S(2)}, u32[]{:S(2)}) async-start(bf16[64,3,16,512]{3,2,1,0:T(8,128)(2,1)} %shard_map.73), calls=%async_computation | async-start | bytes 6291456 | tf_op jit(solution)/shard_map/all_to_all | solution.py:280
  16.3 0.0 copy-done
  16.3 0.1 constant_dynamic-slice_fusion
  16.3 4.3 %collective-permute-start.1 = (bf16[3,256,512]{2,1,0:T(8,128)(2,1)S(1)}, bf16[3,256,512]{2,1,0:T(8,128)(2,1)S(1)}, u32[]{:S(2)}, u32[]{:S(2)}) collective-permute-start(bf16[3,256,512]{2,1,0:T(8,128)(2,1)S(1)} %constant_dynamic-slice_fusion), channel_id=1, source_target_pairs={{0,128},{64,192},{128,0},{192,64},{1,129},{65,193},{129,1},{193,65... | collective-permute-start | bytes 2359304 | tf_op jit(solution)/shard_map/ppermute | solution.py:26
  20.6 2.5 %collective-permute-start = (bf16[3,256,512]{2,1,0:T(8,128)(2,1)S(1)}, bf16[3,256,512]{2,1,0:T(8,128)(2,1)}, u32[]{:S(2)}, u32[]{:S(2)}) collective-permute-start(bf16[3,256,512]{2,1,0:T(8,128)(2,1)S(1)} %constant_dynamic-slice_fusion), channel_id=1, source_target_pairs={{0,64},{64,0},{128,192},{192,128},{1,65},{65,1},{129,193},{193,129... | collective-permute-start | bytes 2359304 | tf_op jit(solution)/shard_map/ppermute | solution.py:26
  23.1 31.5 %collective-permute-done.1.refs_2_ = bf16[3,256,512]{2,1,0:T(8,128)(2,1)S(1)} collective-permute-done((bf16[3,256,512]{2,1,0:T(8,128)(2,1)S(1)}, bf16[3,256,512]{2,1,0:T(8,128)(2,1)S(1)}, u32[]{:S(2)}, u32[]{:S(2)}) %collective-permute-start.1) | collective-permute-done | bytes 786464 | tf_op jit(solution)/shard_map/ppermute | solution.py:26
  54.6 1.9 %collective-permute-start.2 = (bf16[3,256,512]{2,1,0:T(8,128)(2,1)S(1)}, bf16[3,256,512]{2,1,0:T(8,128)(2,1)}, u32[]{:S(2)}, u32[]{:S(2)}) collective-permute-start(bf16[3,256,512]{2,1,0:T(8,128)(2,1)S(1)} %constant_dynamic-slice_fusion), channel_id=1, source_target_pairs={{64,128},{128,64},{65,129},{129,65},{66,130},{130,66},{67,131},{13... | collective-permute-start | bytes 2359304 | tf_op jit(solution)/shard_map/ppermute | solution.py:288
  56.6 4.1 %collective-permute-start.3 = (bf16[3,256,512]{2,1,0:T(8,128)(2,1)S(1)}, bf16[3,256,512]{2,1,0:T(8,128)(2,1)}, u32[]{:S(2)}, u32[]{:S(2)}) collective-permute-start(bf16[3,256,512]{2,1,0:T(8,128)(2,1)S(1)} %collective-permute-done.1.refs_2_), channel_id=1, source_target_pairs={{64,0},{128,192},{65,1},{129,193},{66,2},{130,194},{67,3},{131,195... | collective-permute-start | bytes 2359304 | tf_op jit(solution)/shard_map/ppermute | solution.py:289
  60.6 1.9 %collective-permute-start.5 = (bf16[3,256,512]{2,1,0:T(8,128)(2,1)S(1)}, bf16[3,256,512]{2,1,0:T(8,128)(2,1)}, u32[]{:S(2)}, u32[]{:S(2)}) collective-permute-start(bf16[3,256,512]{2,1,0:T(8,128)(2,1)S(1)} %collective-permute-done.1.refs_2_), channel_id=1, source_target_pairs={{0,1},{1,0},{2,3},{3,2},{4,5},{5,4},{6,7},{7,6},{8,9},{9,8},{10,11... | collective-permute-start | bytes 2359304 | tf_op jit(solution)/shard_map/ppermute | solution.py:34
  62.5 0.0 collective-permute-done.refs_1_
  62.6 2.4 %collective-permute-start.4 = (bf16[3,256,512]{2,1,0:T(8,128)(2,1)}, bf16[3,256,512]{2,1,0:T(8,128)(2,1)}, u32[]{:S(2)}, u32[]{:S(2)}) collective-permute-start(bf16[3,256,512]{2,1,0:T(8,128)(2,1)} %collective-permute-done.refs_1_), channel_id=1, source_target_pairs={{0,1},{1,0},{2,3},{3,2},{4,5},{5,4},{6,7},{7,6},{8,9},{9,8},{10,11... | collective-permute-start | bytes 2359304 | tf_op jit(solution)/shard_map/ppermute | solution.py:34
  65.0 11.1 %collective-permute-done.2.refs_3_ = bf16[3,256,512]{2,1,0:T(8,128)(2,1)} collective-permute-done((bf16[3,256,512]{2,1,0:T(8,128)(2,1)S(1)}, bf16[3,256,512]{2,1,0:T(8,128)(2,1)}, u32[]{:S(2)}, u32[]{:S(2)}) %collective-permute-start.2) | collective-permute-done | bytes 786464 | tf_op jit(solution)/shard_map/ppermute | solution.py:288
  76.1 1.9 %collective-permute-start.6 = (bf16[3,256,512]{2,1,0:T(8,128)(2,1)}, bf16[3,256,512]{2,1,0:T(8,128)(2,1)}, u32[]{:S(2)}, u32[]{:S(2)}) collective-permute-start(bf16[3,256,512]{2,1,0:T(8,128)(2,1)} %collective-permute-done.2.refs_3_), channel_id=1, source_target_pairs={{0,1},{1,0},{2,3},{3,2},{4,5},{5,4},{6,7},{7,6},{8,9},{9,8},{10,11... | collective-permute-start | bytes 2359304 | tf_op jit(solution)/shard_map/ppermute | solution.py:34
  78.0 0.0 collective-permute-done.3.refs_4_
  78.0 2.4 %collective-permute-start.7 = (bf16[3,256,512]{2,1,0:T(8,128)(2,1)}, bf16[3,256,512]{2,1,0:T(8,128)(2,1)}, u32[]{:S(2)}, u32[]{:S(2)}) collective-permute-start(bf16[3,256,512]{2,1,0:T(8,128)(2,1)} %collective-permute-done.3.refs_4_), channel_id=1, source_target_pairs={{0,1},{1,0},{2,3},{3,2},{4,5},{5,4},{6,7},{7,6},{8,9},{9,8},{10,11... | collective-permute-start | bytes 2359304 | tf_op jit(solution)/shard_map/ppermute | solution.py:34
  80.4 2.3 %shard_map.74.spread_ref = bf16[4,128,1024]{2,1,0:T(8,128)(2,1)} custom-call(s32[4,6]{1,0:T(4,128)} %source_ref.1, bf16[4,6,128,128]{3,2,1,0:T(8,128)(2,1)} %refs_10_), custom_call_target="tpu_custom_call" | custom-call | tf_op jit(solution)/shard_map/pallas_call | solution.py:48
  82.8 0.0 copy-start.1
  82.8 0.0 collective-permute-done.5.refs_6_
  82.8 0.0 collective-permute-done.4.refs_5_
  82.8 0.0 collective-permute-done.6.refs_7_
  82.8 0.0 collective-permute-done.7.refs_8_
  82.8 5.8 %all-to-all-done.arrived_ref = bf16[64,3,16,512]{3,2,1,0:T(8,128)(2,1)} async-done(((bf16[64,3,16,512]{3,2,1,0:T(8,128)(2,1)}), bf16[64,3,16,512]{3,2,1,0:T(8,128)(2,1)}, u32[]{:S(2)}, u32[]{:S(2)}) %all-to-all-start) | async-done | bytes 3145760 | tf_op jit(solution)/shard_map/all_to_all | solution.py:280
  88.6 0.0 copy-start.2
  88.6 1.2 copy-done.2
  89.8 0.0 copy-start.3
  89.8 1.0 copy-done.3
  90.9 4.0 %shard_map.75 = (bf16[3,128,512]{2,1,0:T(8,128)(2,1)S(1)}, bf16[3,128,512]{2,1,0:T(8,128)(2,1)S(1)}, bf16[3,128,512]{2,1,0:T(8,128)(2,1)S(1)}, bf16[3,128,512]{2,1,0:T(8,128)(2,1)S(1)}) custom-call(bf16[64,3,16,512]{3,2,1,0:T(8,128)(2,1)} %all-to-all-done.arrived_ref, bf16[4,128,1024]{2,1,0:T(8,128)(2,1)S(1)} %copy-done.2, bf16[4,128,512]{2,1,0:T(8,128)(2,1)S(1)} %bitcast.3), custom_call_target="tpu_custom_call" | custom-call | flops 1610612736 | bytes 6291456 | tf_op jit(solution)/shard_map/pallas_call | solution.py:166
  94.9 2.5 %collective-permute-start.8 = (bf16[3,128,512]{2,1,0:T(8,128)(2,1)S(1)}, bf16[3,128,512]{2,1,0:T(8,128)(2,1)S(1)}, u32[]{:S(2)}, u32[]{:S(2)}) collective-permute-start(bf16[3,128,512]{2,1,0:T(8,128)(2,1)S(1)} %get-tuple-element.59), channel_id=1, source_target_pairs={{0,64},{64,0},{128,192},{192,128},{1,65},{65,1},{129,193},{193,129... | collective-permute-start | bytes 1179656 | tf_op jit(solution)/shard_map/ppermute | solution.py:26
  97.3 4.3 %collective-permute-start.9 = (bf16[3,128,512]{2,1,0:T(8,128)(2,1)S(1)}, bf16[3,128,512]{2,1,0:T(8,128)(2,1)S(1)}, u32[]{:S(2)}, u32[]{:S(2)}) collective-permute-start(bf16[3,128,512]{2,1,0:T(8,128)(2,1)S(1)} %get-tuple-element.60), channel_id=1, source_target_pairs={{0,128},{64,192},{128,0},{192,64},{1,129},{65,193},{129,1},{193,65... | collective-permute-start | bytes 1179656 | tf_op jit(solution)/shard_map/ppermute | solution.py:26
  101.6 2.5 %collective-permute-start.10 = (bf16[3,128,512]{2,1,0:T(8,128)(2,1)S(1)}, bf16[3,128,512]{2,1,0:T(8,128)(2,1)S(1)}, u32[]{:S(2)}, u32[]{:S(2)}) collective-permute-start(bf16[3,128,512]{2,1,0:T(8,128)(2,1)S(1)} %get-tuple-element.61), channel_id=1, source_target_pairs={{0,192},{64,128},{128,64},{192,0},{1,193},{65,129},{129,65},{193,1... | collective-permute-start | bytes 1179656 | tf_op jit(solution)/shard_map/ppermute | solution.py:26
  104.1 0.0 copy-done.1
  104.1 0.0 copy-done.4
  104.1 2.7 %shard_map.76 = (bf16[4,2,3,256,512]{4,3,2,1,0:T(8,128)(2,1)S(1)}, bf16[128,512]{1,0:T(8,128)(2,1)S(1)}, bf16[128,128]{1,0:T(8,128)(2,1)S(1)}) custom-call(bf16[3,512,512]{2,1,0:T(8,128)(2,1)S(1)} %copy-done, bf16[3,256,512]{2,1,0:T(8,128)(2,1)} %collective-permute-done.refs_1_, bf16[3,256,512]{2,1,0:T(8,128)(2,1)S(1)} %collective-permute-done.1.refs_2_, ...), custom_call_target="tpu_custom_call" | custom-call | bytes 12582912 | tf_op jit(solution)/shard_map/pallas_call | solution.py:138
  106.8 6.1 %collective-permute-done.8.refs_4_ = bf16[3,128,512]{2,1,0:T(8,128)(2,1)S(1)} collective-permute-done((bf16[3,128,512]{2,1,0:T(8,128)(2,1)S(1)}, bf16[3,128,512]{2,1,0:T(8,128)(2,1)S(1)}, u32[]{:S(2)}, u32[]{:S(2)}) %collective-permute-start.8) | collective-permute-done | bytes 393248 | tf_op jit(solution)/shard_map/ppermute | solution.py:26
  112.9 15.1 %collective-permute-done.9.refs_5_ = bf16[3,128,512]{2,1,0:T(8,128)(2,1)S(1)} collective-permute-done((bf16[3,128,512]{2,1,0:T(8,128)(2,1)S(1)}, bf16[3,128,512]{2,1,0:T(8,128)(2,1)S(1)}, u32[]{:S(2)}, u32[]{:S(2)}) %collective-permute-start.9) | collective-permute-done | bytes 393248 | tf_op jit(solution)/shard_map/ppermute | solution.py:26
  128.0 9.3 %collective-permute-done.10.refs_6_ = bf16[3,128,512]{2,1,0:T(8,128)(2,1)S(1)} collective-permute-done((bf16[3,128,512]{2,1,0:T(8,128)(2,1)S(1)}, bf16[3,128,512]{2,1,0:T(8,128)(2,1)S(1)}, u32[]{:S(2)}, u32[]{:S(2)}) %collective-permute-start.10) | collective-permute-done | bytes 393248 | tf_op jit(solution)/shard_map/ppermute | solution.py:26
  137.3 1.3 collective-permute-start.11
  138.6 8.9 %collective-permute-done.11.refs_0_ = bf16[128,512]{1,0:T(8,128)(2,1)S(1)} collective-permute-done((bf16[128,512]{1,0:T(8,128)(2,1)S(1)}, bf16[128,512]{1,0:T(8,128)(2,1)S(1)}, u32[]{:S(2)}, u32[]{:S(2)}) %collective-permute-start.11) | collective-permute-done | bytes 131104 | tf_op jit(solution)/shard_map/ppermute | solution.py:301
  147.5 4.2 %shard_map.78 = (bf16[128,512]{1,0:T(8,128)(2,1)S(1)}, bf16[128,512]{1,0:T(8,128)(2,1)S(1)}, bf16[128,512]{1,0:T(8,128)(2,1)S(1)}, bf16[128,512]{1,0:T(8,128)(2,1)S(1)}) custom-call(bf16[128,512]{1,0:T(8,128)(2,1)S(1)} %collective-permute-done.11.refs_0_, bf16[128,128]{1,0:T(8,128)(2,1)S(1)} %get-tuple-element.56.refs_1_, ...), custom_call_target="tpu_custom_call" | custom-call | flops 1006632960 | bytes 7864320 | tf_op jit(solution)/shard_map/pallas_call | solution.py:239
  151.7 1.9 %collective-permute-start.12 = (bf16[128,512]{1,0:T(8,128)(2,1)S(1)}, bf16[128,512]{1,0:T(8,128)(2,1)S(1)}, u32[]{:S(2)}, u32[]{:S(2)}) collective-permute-start(bf16[128,512]{1,0:T(8,128)(2,1)S(1)} %get-tuple-element.68), channel_id=1, source_target_pairs={{0,64},{64,0},{128,192},{192,128},{1,65},{65,1},{129,193},{193,129... | collective-permute-start | bytes 393224 | tf_op jit(solution)/shard_map/ppermute | solution.py:26
  153.6 4.8 %collective-permute-start.13 = (bf16[128,512]{1,0:T(8,128)(2,1)S(1)}, bf16[128,512]{1,0:T(8,128)(2,1)S(1)}, u32[]{:S(2)}, u32[]{:S(2)}) collective-permute-start(bf16[128,512]{1,0:T(8,128)(2,1)S(1)} %get-tuple-element.69), channel_id=1, source_target_pairs={{0,128},{64,192},{128,0},{192,64},{1,129},{65,193},{129,1},{193,65... | collective-permute-start | bytes 393224 | tf_op jit(solution)/shard_map/ppermute | solution.py:26
  158.5 2.5 %collective-permute-start.14 = (bf16[128,512]{1,0:T(8,128)(2,1)S(1)}, bf16[128,512]{1,0:T(8,128)(2,1)S(1)}, u32[]{:S(2)}, u32[]{:S(2)}) collective-permute-start(bf16[128,512]{1,0:T(8,128)(2,1)S(1)} %get-tuple-element.70), channel_id=1, source_target_pairs={{0,192},{64,128},{128,64},{192,0},{1,193},{65,129},{129,65},{193,1... | collective-permute-start | bytes 393224 | tf_op jit(solution)/shard_map/ppermute | solution.py:26
  160.9 0.0 collective-permute-done.12.refs_1_
  161.0 5.2 %collective-permute-done.13.refs_2_ = bf16[128,512]{1,0:T(8,128)(2,1)S(1)} collective-permute-done((bf16[128,512]{1,0:T(8,128)(2,1)S(1)}, bf16[128,512]{1,0:T(8,128)(2,1)S(1)}, u32[]{:S(2)}, u32[]{:S(2)}) %collective-permute-start.13) | collective-permute-done | bytes 131104 | tf_op jit(solution)/shard_map/ppermute | solution.py:26
  166.1 3.4 %collective-permute-done.14.refs_3_ = bf16[128,512]{1,0:T(8,128)(2,1)S(1)} collective-permute-done((bf16[128,512]{1,0:T(8,128)(2,1)S(1)}, bf16[128,512]{1,0:T(8,128)(2,1)S(1)}, u32[]{:S(2)}, u32[]{:S(2)}) %collective-permute-start.14) | collective-permute-done | bytes 131104 | tf_op jit(solution)/shard_map/ppermute | solution.py:26
  169.5 0.8 shard_map.79
  (2 shorter events, 0.0 us)
Async XLA Ops:
  5.3 11.0 %copy-start = (bf16[3,512,512]{2,1,0:T(8,128)(2,1)S(1)}, bf16[3,512,512]{2,1,0:T(8,128)(2,1)}, u32[]{:S(2)}) copy-start(bf16[3,512,512]{2,1,0:T(8,128)(2,1)} %refs_0_) | copy-start | bytes 4718596
  5.3 83.3 %all-to-all-start = ((bf16[64,3,16,512]{3,2,1,0:T(8,128)(2,1)}), bf16[64,3,16,512]{3,2,1,0:T(8,128)(2,1)}, u32[]{:S(2)}, u32[]{:S(2)}) async-start(bf16[64,3,16,512]{3,2,1,0:T(8,128)(2,1)} %shard_map.73), calls=%async_computation | async-start | bytes 6291456 | tf_op jit(solution)/shard_map/all_to_all | solution.py:280
  16.3 38.3 %collective-permute-start.1 = (bf16[3,256,512]{2,1,0:T(8,128)(2,1)S(1)}, bf16[3,256,512]{2,1,0:T(8,128)(2,1)S(1)}, u32[]{:S(2)}, u32[]{:S(2)}) collective-permute-start(bf16[3,256,512]{2,1,0:T(8,128)(2,1)S(1)} %constant_dynamic-slice_fusion), channel_id=1, source_target_pairs={{0,128},{64,192},{128,0},{192,64},{1,129},{65,193},{129,1},{193,65... | collective-permute-start | bytes 2359304 | tf_op jit(solution)/shard_map/ppermute | solution.py:26
  20.6 41.9 %collective-permute-start = (bf16[3,256,512]{2,1,0:T(8,128)(2,1)S(1)}, bf16[3,256,512]{2,1,0:T(8,128)(2,1)}, u32[]{:S(2)}, u32[]{:S(2)}) collective-permute-start(bf16[3,256,512]{2,1,0:T(8,128)(2,1)S(1)} %constant_dynamic-slice_fusion), channel_id=1, source_target_pairs={{0,64},{64,0},{128,192},{192,128},{1,65},{65,1},{129,193},{193,129... | collective-permute-start | bytes 2359304 | tf_op jit(solution)/shard_map/ppermute | solution.py:26
  54.6 21.5 %collective-permute-start.2 = (bf16[3,256,512]{2,1,0:T(8,128)(2,1)S(1)}, bf16[3,256,512]{2,1,0:T(8,128)(2,1)}, u32[]{:S(2)}, u32[]{:S(2)}) collective-permute-start(bf16[3,256,512]{2,1,0:T(8,128)(2,1)S(1)} %constant_dynamic-slice_fusion), channel_id=1, source_target_pairs={{64,128},{128,64},{65,129},{129,65},{66,130},{130,66},{67,131},{13... | collective-permute-start | bytes 2359304 | tf_op jit(solution)/shard_map/ppermute | solution.py:288
  56.6 21.5 %collective-permute-start.3 = (bf16[3,256,512]{2,1,0:T(8,128)(2,1)S(1)}, bf16[3,256,512]{2,1,0:T(8,128)(2,1)}, u32[]{:S(2)}, u32[]{:S(2)}) collective-permute-start(bf16[3,256,512]{2,1,0:T(8,128)(2,1)S(1)} %collective-permute-done.1.refs_2_), channel_id=1, source_target_pairs={{64,0},{128,192},{65,1},{129,193},{66,2},{130,194},{67,3},{131,195... | collective-permute-start | bytes 2359304 | tf_op jit(solution)/shard_map/ppermute | solution.py:289
  60.6 22.1 %collective-permute-start.5 = (bf16[3,256,512]{2,1,0:T(8,128)(2,1)S(1)}, bf16[3,256,512]{2,1,0:T(8,128)(2,1)}, u32[]{:S(2)}, u32[]{:S(2)}) collective-permute-start(bf16[3,256,512]{2,1,0:T(8,128)(2,1)S(1)} %collective-permute-done.1.refs_2_), channel_id=1, source_target_pairs={{0,1},{1,0},{2,3},{3,2},{4,5},{5,4},{6,7},{7,6},{8,9},{9,8},{10,11... | collective-permute-start | bytes 2359304 | tf_op jit(solution)/shard_map/ppermute | solution.py:34
  62.6 20.2 %collective-permute-start.4 = (bf16[3,256,512]{2,1,0:T(8,128)(2,1)}, bf16[3,256,512]{2,1,0:T(8,128)(2,1)}, u32[]{:S(2)}, u32[]{:S(2)}) collective-permute-start(bf16[3,256,512]{2,1,0:T(8,128)(2,1)} %collective-permute-done.refs_1_), channel_id=1, source_target_pairs={{0,1},{1,0},{2,3},{3,2},{4,5},{5,4},{6,7},{7,6},{8,9},{9,8},{10,11... | collective-permute-start | bytes 2359304 | tf_op jit(solution)/shard_map/ppermute | solution.py:34
  76.1 6.7 %collective-permute-start.6 = (bf16[3,256,512]{2,1,0:T(8,128)(2,1)}, bf16[3,256,512]{2,1,0:T(8,128)(2,1)}, u32[]{:S(2)}, u32[]{:S(2)}) collective-permute-start(bf16[3,256,512]{2,1,0:T(8,128)(2,1)} %collective-permute-done.2.refs_3_), channel_id=1, source_target_pairs={{0,1},{1,0},{2,3},{3,2},{4,5},{5,4},{6,7},{7,6},{8,9},{9,8},{10,11... | collective-permute-start | bytes 2359304 | tf_op jit(solution)/shard_map/ppermute | solution.py:34
  78.0 4.8 %collective-permute-start.7 = (bf16[3,256,512]{2,1,0:T(8,128)(2,1)}, bf16[3,256,512]{2,1,0:T(8,128)(2,1)}, u32[]{:S(2)}, u32[]{:S(2)}) collective-permute-start(bf16[3,256,512]{2,1,0:T(8,128)(2,1)} %collective-permute-done.3.refs_4_), channel_id=1, source_target_pairs={{0,1},{1,0},{2,3},{3,2},{4,5},{5,4},{6,7},{7,6},{8,9},{9,8},{10,11... | collective-permute-start | bytes 2359304 | tf_op jit(solution)/shard_map/ppermute | solution.py:34
  82.8 21.3 %copy-start.1 = (bf16[4,6,128,128]{3,2,1,0:T(8,128)(2,1)S(1)}, bf16[4,6,128,128]{3,2,1,0:T(8,128)(2,1)}, u32[]{:S(2)}) copy-start(bf16[4,6,128,128]{3,2,1,0:T(8,128)(2,1)} %refs_10_) | copy-start | bytes 2359300
  88.6 1.2 copy-start.2
  89.8 1.0 copy-start.3
  90.9 13.2 %copy-start.4 = (bf16[512,512]{1,0:T(8,128)(2,1)S(1)}, bf16[512,512]{1,0:T(8,128)(2,1)}, u32[]{:S(2)}) copy-start(bf16[512,512]{1,0:T(8,128)(2,1)} %param.7) | copy-start | bytes 1572868
  94.9 18.0 %collective-permute-start.8 = (bf16[3,128,512]{2,1,0:T(8,128)(2,1)S(1)}, bf16[3,128,512]{2,1,0:T(8,128)(2,1)S(1)}, u32[]{:S(2)}, u32[]{:S(2)}) collective-permute-start(bf16[3,128,512]{2,1,0:T(8,128)(2,1)S(1)} %get-tuple-element.59), channel_id=1, source_target_pairs={{0,64},{64,0},{128,192},{192,128},{1,65},{65,1},{129,193},{193,129... | collective-permute-start | bytes 1179656 | tf_op jit(solution)/shard_map/ppermute | solution.py:26
  97.3 30.7 %collective-permute-start.9 = (bf16[3,128,512]{2,1,0:T(8,128)(2,1)S(1)}, bf16[3,128,512]{2,1,0:T(8,128)(2,1)S(1)}, u32[]{:S(2)}, u32[]{:S(2)}) collective-permute-start(bf16[3,128,512]{2,1,0:T(8,128)(2,1)S(1)} %get-tuple-element.60), channel_id=1, source_target_pairs={{0,128},{64,192},{128,0},{192,64},{1,129},{65,193},{129,1},{193,65... | collective-permute-start | bytes 1179656 | tf_op jit(solution)/shard_map/ppermute | solution.py:26
  101.6 35.6 %collective-permute-start.10 = (bf16[3,128,512]{2,1,0:T(8,128)(2,1)S(1)}, bf16[3,128,512]{2,1,0:T(8,128)(2,1)S(1)}, u32[]{:S(2)}, u32[]{:S(2)}) collective-permute-start(bf16[3,128,512]{2,1,0:T(8,128)(2,1)S(1)} %get-tuple-element.61), channel_id=1, source_target_pairs={{0,192},{64,128},{128,64},{192,0},{1,193},{65,129},{129,65},{193,1... | collective-permute-start | bytes 1179656 | tf_op jit(solution)/shard_map/ppermute | solution.py:26
  137.3 10.2 %collective-permute-start.11 = (bf16[128,512]{1,0:T(8,128)(2,1)S(1)}, bf16[128,512]{1,0:T(8,128)(2,1)S(1)}, u32[]{:S(2)}, u32[]{:S(2)}) collective-permute-start(bf16[128,512]{1,0:T(8,128)(2,1)S(1)} %get-tuple-element.62), channel_id=1, source_target_pairs={{0,448},{64,384},{128,320},{192,256},{1,449},{65,385},{129,321},{1... | collective-permute-start | bytes 393224 | tf_op jit(solution)/shard_map/ppermute | solution.py:301
  151.7 9.2 %collective-permute-start.12 = (bf16[128,512]{1,0:T(8,128)(2,1)S(1)}, bf16[128,512]{1,0:T(8,128)(2,1)S(1)}, u32[]{:S(2)}, u32[]{:S(2)}) collective-permute-start(bf16[128,512]{1,0:T(8,128)(2,1)S(1)} %get-tuple-element.68), channel_id=1, source_target_pairs={{0,64},{64,0},{128,192},{192,128},{1,65},{65,1},{129,193},{193,129... | collective-permute-start | bytes 393224 | tf_op jit(solution)/shard_map/ppermute | solution.py:26
  153.6 12.5 %collective-permute-start.13 = (bf16[128,512]{1,0:T(8,128)(2,1)S(1)}, bf16[128,512]{1,0:T(8,128)(2,1)S(1)}, u32[]{:S(2)}, u32[]{:S(2)}) collective-permute-start(bf16[128,512]{1,0:T(8,128)(2,1)S(1)} %get-tuple-element.69), channel_id=1, source_target_pairs={{0,128},{64,192},{128,0},{192,64},{1,129},{65,193},{129,1},{193,65... | collective-permute-start | bytes 393224 | tf_op jit(solution)/shard_map/ppermute | solution.py:26
  158.5 11.0 %collective-permute-start.14 = (bf16[128,512]{1,0:T(8,128)(2,1)S(1)}, bf16[128,512]{1,0:T(8,128)(2,1)S(1)}, u32[]{:S(2)}, u32[]{:S(2)}) collective-permute-start(bf16[128,512]{1,0:T(8,128)(2,1)S(1)} %get-tuple-element.70), channel_id=1, source_target_pairs={{0,192},{64,128},{128,64},{192,0},{1,193},{65,129},{129,65},{193,1... | collective-permute-start | bytes 393224 | tf_op jit(solution)/shard_map/ppermute | solution.py:26

commit v6 on v5

--- a/solution.py
+++ b/solution.py
@@ -8,6 +8,7 @@
 
 HALVES = 2
 STAGES = 4
+SLOTS = (0, 2, 3, 1)
 CORES = 2
 SEGMENT = ("half", "stage")
 DOM = ("pair", "core")
@@ -18,8 +19,7 @@
 
 
 def tile_of(slot):
-    mirror = lax.axis_index("half") * (STAGES - 1)
-    return lax.axis_index("stage") ^ mirror ^ slot
+    return lax.axis_index("stage") ^ (2 * lax.axis_index("half")) ^ slot
 
 
 def exchange(block, slot):
@@ -27,7 +27,7 @@
 
 
 def exchange_all(blocks):
-    return [blocks[0]] + [exchange(blocks[slot], slot) for slot in range(1, STAGES)]
+    return [block if slot == 0 else exchange(block, slot) for slot, block in zip(SLOTS, blocks)]
 
 
 def swap_cores(block):
@@ -54,21 +54,54 @@
     )(adj_src, adj_blocks)
 
 
-def pick_kernel(rows_ref, count_ref, history_ref, out_ref, pick_ref):
-    receivers, _, slots, width = out_ref.shape
+def pick_kernel(rows_ref, count_ref, history_ref, out_ref, *scratch):
+    history_buf, pick_buf, out_buf, in_sem, out_sem = scratch
+    receivers, levels, slots, width = out_ref.shape
     rows = history_ref.shape[1]
-
-    @pl.when(pl.program_id(0) == 0)
-    def _():
-        slot = lax.broadcasted_iota(jnp.int32, (slots, receivers), 0)
-        wanted = jnp.where(slot < count_ref[...], rows_ref[0], -1)
-        column = lax.broadcasted_iota(jnp.int32, (slots, rows), 1)
-        for p in range(receivers):
-            mask = jnp.where(wanted[:, p : p + 1] == column, 1.0, 0.0)
-            pick_ref[p * slots : (p + 1) * slots] = mask.astype(jnp.bfloat16)
-
-    got = jnp.dot(pick_ref[...], history_ref[0], preferred_element_type=jnp.float32)
-    out_ref[:, 0] = got.astype(jnp.bfloat16).reshape(receivers, slots, width)
+    parts = in_sem.shape[1]
+    some = rows // parts
+    loads = [
+        [
+            pltpu.make_async_copy(
+                history_ref.at[i, pl.ds(n * some, some)],
+                history_buf.at[i, pl.ds(n * some, some)],
+                in_sem.at[i, n],
+            )
+            for n in range(parts)
+        ]
+        for i in range(levels)
+    ]
+    for load in sum(loads, []):
+        load.start()
+
+    slot = lax.broadcasted_iota(jnp.int32, (slots, receivers), 0)
+    wanted = jnp.where(slot < count_ref[...], rows_ref[0], -1)
+    column = lax.broadcasted_iota(jnp.int32, (slots, rows), 1)
+    for p in range(receivers):
+        mask = jnp.where(wanted[:, p : p + 1] == column, 1.0, 0.0)
+        pick_buf[p * slots : (p + 1) * slots] = mask.astype(jnp.bfloat16)
+
+    chunks = out_sem.shape[1]
+    group = receivers // chunks
+    stores = []
+    for i in range(levels):
+        for load in loads[i]:
+            load.wait()
+        for n in range(chunks):
+            got = jnp.dot(
+                pick_buf[n * group * slots : (n + 1) * group * slots],
+                history_buf[i],
+                preferred_element_type=jnp.float32,
+            )
+            chosen = pl.ds(n * group, group)
+            out_buf[i, chosen] = got.astype(jnp.bfloat16).reshape(group, slots, width)
+            store = pltpu.make_async_copy(
+                out_buf.at[i, chosen], out_ref.at[chosen, i], out_sem.at[i, n]
+            )
+            store.start()
+            stores.append(store)
+    for store in stores:
+        store.wait()
 
 
 def pick_rows(send_rows, send_count, history):
@@ -77,14 +110,15 @@
     return pl.pallas_call(
         pick_kernel,
         out_shape=jax.ShapeDtypeStruct((parts, levels, slots, width), jnp.bfloat16),
-        grid=(levels,),
-        in_specs=[
-            pl.BlockSpec((1, slots, parts), lambda g: (0, 0, 0)),
-            pl.BlockSpec((1, parts), lambda g: (0, 0)),
-            pl.BlockSpec((1, rows, width), lambda g: (g, 0, 0)),
+        in_specs=[VMEM, VMEM, ANYWHERE],
+        out_specs=ANYWHERE,
+        scratch_shapes=[
+            pltpu.VMEM(history.shape, jnp.bfloat16),
+            pltpu.VMEM((parts * slots, rows), jnp.bfloat16),
+            pltpu.VMEM((levels, parts, slots, width), jnp.bfloat16),
+            pltpu.SemaphoreType.DMA((levels, 2)),
+            pltpu.SemaphoreType.DMA((levels, 4)),
         ],
-        out_specs=pl.BlockSpec((parts, 1, slots, width), lambda g: (0, g, 0, 0)),
-        scratch_shapes=[pltpu.VMEM((parts * slots, rows), jnp.bfloat16)],
         compiler_params=GRANT,
         cost_estimate=pl.CostEstimate(
             flops=2 * levels * parts * slots * rows * width,
@@ -148,34 +182,70 @@
     )(*sources)
 
 
-def halo_kernel(arrived_ref, spread_ref, features_ref, *out_refs):
-    parts, _, slots, width = arrived_ref.shape
-    tiles, rows, _ = spread_ref.shape
-    spread = jnp.concatenate([spread_ref[tile_of(r)] for r in range(tiles)], axis=0)
-    halo = arrived_ref[:, 0].reshape(parts * slots, width)
-    summed = jnp.dot(spread, halo, preferred_element_type=jnp.float32)
-    for r in range(tiles):
-        start = 0.1 * features_ref[tile_of(r)].astype(jnp.float32)
-        part = 0.9 * summed[r * rows : (r + 1) * rows] + start
-        out_refs[r][0] = part.astype(jnp.bfloat16)
+def halo_kernel(arrived_ref, spread_ref, features_ref, *refs):
+    out_refs = refs[:STAGES]
+    arrived_buf, spread_buf, features_buf, out_buf, in_sem, own_sem, out_sem = refs[STAGES:]
+    parts, levels, slots, width = arrived_ref.shape
+    rows = spread_ref.shape[1]
+    own = []
+    for n, r in enumerate(SLOTS):
+        for m, (ref, buf) in enumerate([(spread_ref, spread_buf), (features_ref, features_buf)]):
+            own.append(pltpu.make_async_copy(ref.at[tile_of(r)], buf.at[n], own_sem.at[m, n]))
+    chunks = in_sem.shape[1]
+    group = parts // chunks
+    loads = [
+        [
+            pltpu.make_async_copy(
+                arrived_ref.at[pl.ds(n * group, group), i],
+                arrived_buf.at[i, pl.ds(n * group, group)],
+                in_sem.at[i, n],
+            )
+            for n in range(chunks)
+        ]
+        for i in range(levels)
+    ]
+    for load in loads[0] + own + sum(loads[1:], []):
+        load.start()
+    for load in own:
+        load.wait()
+    spread = spread_buf[...].reshape(STAGES * rows, parts * slots)
+    stores = []
+    for i in range(levels):
+        for load in loads[i]:
+            load.wait()
+        halo = arrived_buf[i].reshape(parts * slots, width)
+        summed = jnp.dot(spread, halo, preferred_element_type=jnp.float32)
+        for n in range(STAGES):
+            start = 0.1 * features_buf[n].astype(jnp.float32)
+            part = 0.9 * summed[n * rows : (n + 1) * rows] + start
+            out_buf[n, i] = part.astype(jnp.bfloat16)
+            store = pltpu.make_async_copy(out_buf.at[n, i], out_refs[n].at[i], out_sem.at[n, i])
+            store.start()
+            stores.append(store)
+    for store in stores:
+        store.wait()
 
 
 def halo_sums(arrived, spread, features):
     parts, levels, slots, width = arrived.shape
-    tiles, rows, halo_rows = spread.shape
+    _, rows, halo_rows = spread.shape
     return pl.pallas_call(
         halo_kernel,
-        out_shape=[jax.ShapeDtypeStruct((levels, rows, width), jnp.bfloat16)] * tiles,
-        grid=(levels,),
-        in_specs=[
-            pl.BlockSpec((parts, 1, slots, width), lambda g: (0, g, 0, 0)),
-            pl.BlockSpec(spread.shape, lambda g: (0, 0, 0)),
-            pl.BlockSpec(features.shape, lambda g: (0, 0, 0)),
+        out_shape=[jax.ShapeDtypeStruct((levels, rows, width), jnp.bfloat16)] * STAGES,
+        in_specs=[ANYWHERE] * 3,
+        out_specs=[ANYWHERE] * STAGES,
+        scratch_shapes=[
+            pltpu.VMEM((levels, parts, slots, width), jnp.bfloat16),
+            pltpu.VMEM(spread.shape, jnp.bfloat16),
+            pltpu.VMEM(features.shape, jnp.bfloat16),
+            pltpu.VMEM((STAGES, levels, rows, width), jnp.bfloat16),
+            pltpu.SemaphoreType.DMA((levels, 4)),
+            pltpu.SemaphoreType.DMA((2, STAGES)),
+            pltpu.SemaphoreType.DMA((STAGES, levels)),
         ],
-        out_specs=[pl.BlockSpec((1, rows, width), lambda g: (g, 0, 0))] * tiles,
-        compiler_params=SMALL,
+        compiler_params=GRANT,
         cost_estimate=pl.CostEstimate(
-            flops=2 * levels * tiles * rows * halo_rows * width,
+            flops=2 * levels * STAGES * rows * halo_rows * width,
             bytes_accessed=2 * (arrived.size + spread.size + features.size * (1 + levels)),
             transcendentals=0,
         ),
@@ -193,8 +263,8 @@
 
     @pl.when(half == which)
     def _():
-        for r in range(stages):
-            h_buf[stage ^ r] = h_refs[r][...]
+        for r, h_ref in zip(SLOTS, h_refs):
+            h_buf[stage ^ r] = h_ref[...]
         a = a_ref[...]
         x = x_ref[...]
         for s in range(stages):
@@ -213,11 +283,11 @@
                 )
                 mixed = (1.0 - beta) * support + beta * branch
                 x = jnp.maximum(mixed, 0.0).astype(jnp.bfloat16)
-            for r in range(stages):
+            for r, out_ref in zip(SLOTS, out_refs):
 
                 @pl.when(stage ^ s == r)
                 def _():
-                    out_refs[r][...] = x
+                    out_ref[...] = x
 
         if which == 0:
             refs[stages][...] = x
@@ -253,7 +323,7 @@
 
 def place_kernel(*refs):
     in_refs, out_ref = refs[:-1], refs[-1]
-    for r, ref in enumerate(in_refs):
+    for r, ref in zip(SLOTS, in_refs):
         out_ref[0, tile_of(r)] = ref[...]
 
 
@@ -297,8 +367,8 @@
     group, own_x, own_a = stage_operands(weights, near, far, tiles, adj_blocks)
 
     *first, last = chain(0, own_x, own_a, group, halos)
-    mirror = [(s, HALVES * STAGES - 1 - s) for s in range(STAGES)]
-    done = chain(1, lax.ppermute(last, SEGMENT, mirror), own_a, group, halos, first)
+    over = [(s, STAGES + (s ^ 2)) for s in range(STAGES)]
+    done = chain(1, lax.ppermute(last, SEGMENT, over), own_a, group, halos, first)
     fresh = place(exchange_all(done))
     return fresh.reshape(1, rows_dev, width)
 

time: 171 us -> 166 us (0.971)
  the two profiles are of different devices: /device:TPU:322 before, /device:TPU:6 now
where the time goes in v6:
time: 166 us; the launch traced here: 165 us
  waiting for transfers between devices  81.1 us (49%)
  starting transfers between devices  62.8 us (38%)
  Pallas kernels  20.3 us (12%)
    ppermute x8, waiting for transfers between devices, exchange(): return lax.ppermute(block, 'stage', [(u, u ^ slot) for u in range(STAGES)])  60.3 us
    ppermute x8, starting transfers between devices, exchange(): return lax.ppermute(block, 'stage', [(u, u ^ slot) for u in range(STAGES)])  31.6 us
    ppermute x1, waiting for transfers between devices, local(): near.append(lax.ppermute(two, 'stage', [(1, 0), (2, 3)]))  13.5 us
    all_to_all x1, starting transfers between devices, local(): lax.all_to_all(outgoing, DOM, split_axis=0, concat_axis=0, tiled=True)  11.3 us
    ppermute x1, starting transfers between devices, local(): lax.ppermute(last, SEGMENT, over)  8.93 us
    ppermute x4, starting transfers between devices, swap_cores(): return lax.ppermute(block, 'core', [(0, 1), (1, 0)])  8.16 us
    pallas_call x1, Pallas kernels, halo_sums(): pl.pallas_call(halo_kernel, out_shape=[jax.ShapeDtypeStruct((levels, rows...  5.51 us
    pallas_call x1, Pallas kernels, pick_rows(): pl.pallas_call(pick_kernel, out_shape=jax.ShapeDtypeStruct((parts, levels...  4.75 us
  transfers between devices with their start and end apart: 16, of which 9 were waited for; matrix products, arithmetic and copies ran while one was open for 0% of the time, Pallas kernels for 3%

profile of v6, /device:TPU:6, one launch (start us, length us, event | category | flops | bytes accessed | tf_op | source)
XLA Modules:
  0.0 164.6 jit_solution(3443098517530569704)
XLA Ops:
  0.0 4.8 %shard_map.73 = bf16[64,3,16,512]{3,2,1,0:T(8,128)(2,1)} custom-call(s32[1,16,64]{2,1,0:T(8,128)} %bitcast.5, s32[1,64]{1,0:T(1,128)} %count_ref.1, bf16[3,512,512]{2,1,0:T(8,128)(2,1)} %history_ref.1), custom_call_target="tpu_custom_call" | custom-call | flops 1610612736 | bytes 4718592 | tf_op jit(solution)/shard_map/pallas_call | solution.py:110
  4.8 0.0 copy-start
  4.8 11.3 %all-to-all-start = ((bf16[64,3,16,512]{3,2,1,0:T(8,128)(2,1)}), bf16[64,3,16,512]{3,2,1,0:T(8,128)(2,1)}, u32[]{:S(2)}, u32[]{:S(2)}) async-start(bf16[64,3,16,512]{3,2,1,0:T(8,128)(2,1)} %shard_map.73), calls=%async_computation | async-start | bytes 6291456 | tf_op jit(solution)/shard_map/all_to_all | solution.py:350
  16.1 0.0 copy-done
  16.1 0.1 constant_dynamic-slice_fusion
  16.1 5.9 %collective-permute-start.1 = (bf16[3,256,512]{2,1,0:T(8,128)(2,1)S(1)}, bf16[3,256,512]{2,1,0:T(8,128)(2,1)S(1)}, u32[]{:S(2)}, u32[]{:S(2)}) collective-permute-start(bf16[3,256,512]{2,1,0:T(8,128)(2,1)S(1)} %constant_dynamic-slice_fusion), channel_id=1, source_target_pairs={{0,128},{64,192},{128,0},{192,64},{1,129},{65,193},{129,1},{193,65... | collective-permute-start | bytes 2359304 | tf_op jit(solution)/shard_map/ppermute | solution.py:26
  22.1 4.3 %collective-permute-start = (bf16[3,256,512]{2,1,0:T(8,128)(2,1)S(1)}, bf16[3,256,512]{2,1,0:T(8,128)(2,1)}, u32[]{:S(2)}, u32[]{:S(2)}) collective-permute-start(bf16[3,256,512]{2,1,0:T(8,128)(2,1)S(1)} %constant_dynamic-slice_fusion), channel_id=1, source_target_pairs={{0,64},{64,0},{128,192},{192,128},{1,65},{65,1},{129,193},{193,129... | collective-permute-start | bytes 2359304 | tf_op jit(solution)/shard_map/ppermute | solution.py:26
  26.4 30.5 %collective-permute-done.1.refs_2_ = bf16[3,256,512]{2,1,0:T(8,128)(2,1)S(1)} collective-permute-done((bf16[3,256,512]{2,1,0:T(8,128)(2,1)S(1)}, bf16[3,256,512]{2,1,0:T(8,128)(2,1)S(1)}, u32[]{:S(2)}, u32[]{:S(2)}) %collective-permute-start.1) | collective-permute-done | bytes 786464 | tf_op jit(solution)/shard_map/ppermute | solution.py:26
  56.9 1.6 collective-permute-start.2
  58.5 1.3 collective-permute-start.3
  59.8 1.9 %collective-permute-start.5 = (bf16[3,256,512]{2,1,0:T(8,128)(2,1)S(1)}, bf16[3,256,512]{2,1,0:T(8,128)(2,1)}, u32[]{:S(2)}, u32[]{:S(2)}) collective-permute-start(bf16[3,256,512]{2,1,0:T(8,128)(2,1)S(1)} %collective-permute-done.1.refs_2_), channel_id=1, source_target_pairs={{0,1},{1,0},{2,3},{3,2},{4,5},{5,4},{6,7},{7,6},{8,9},{9,8},{10,11... | collective-permute-start | bytes 2359304 | tf_op jit(solution)/shard_map/ppermute | solution.py:34
  61.7 0.0 collective-permute-done.refs_1_
  61.7 2.4 %collective-permute-start.4 = (bf16[3,256,512]{2,1,0:T(8,128)(2,1)}, bf16[3,256,512]{2,1,0:T(8,128)(2,1)}, u32[]{:S(2)}, u32[]{:S(2)}) collective-permute-start(bf16[3,256,512]{2,1,0:T(8,128)(2,1)} %collective-permute-done.refs_1_), channel_id=1, source_target_pairs={{0,1},{1,0},{2,3},{3,2},{4,5},{5,4},{6,7},{7,6},{8,9},{9,8},{10,11... | collective-permute-start | bytes 2359304 | tf_op jit(solution)/shard_map/ppermute | solution.py:34
  64.1 0.0 collective-permute-done.2.refs_3_
  64.1 1.9 %collective-permute-start.6 = (bf16[3,256,512]{2,1,0:T(8,128)(2,1)}, bf16[3,256,512]{2,1,0:T(8,128)(2,1)}, u32[]{:S(2)}, u32[]{:S(2)}) collective-permute-start(bf16[3,256,512]{2,1,0:T(8,128)(2,1)} %collective-permute-done.2.refs_3_), channel_id=1, source_target_pairs={{0,1},{1,0},{2,3},{3,2},{4,5},{5,4},{6,7},{7,6},{8,9},{9,8},{10,11... | collective-permute-start | bytes 2359304 | tf_op jit(solution)/shard_map/ppermute | solution.py:34
  66.1 13.5 %collective-permute-done.3.refs_4_ = bf16[3,256,512]{2,1,0:T(8,128)(2,1)} collective-permute-done((bf16[3,256,512]{2,1,0:T(8,128)(2,1)S(1)}, bf16[3,256,512]{2,1,0:T(8,128)(2,1)}, u32[]{:S(2)}, u32[]{:S(2)}) %collective-permute-start.3) | collective-permute-done | bytes 786464 | tf_op jit(solution)/shard_map/ppermute | solution.py:359
  79.6 1.9 %collective-permute-start.7 = (bf16[3,256,512]{2,1,0:T(8,128)(2,1)}, bf16[3,256,512]{2,1,0:T(8,128)(2,1)}, u32[]{:S(2)}, u32[]{:S(2)}) collective-permute-start(bf16[3,256,512]{2,1,0:T(8,128)(2,1)} %collective-permute-done.3.refs_4_), channel_id=1, source_target_pairs={{0,1},{1,0},{2,3},{3,2},{4,5},{5,4},{6,7},{7,6},{8,9},{9,8},{10,11... | collective-permute-start | bytes 2359304 | tf_op jit(solution)/shard_map/ppermute | solution.py:34
  81.5 2.3 %shard_map.74.spread_ref = bf16[4,128,1024]{2,1,0:T(8,128)(2,1)} custom-call(s32[4,6]{1,0:T(4,128)} %source_ref.1, bf16[4,6,128,128]{3,2,1,0:T(8,128)(2,1)} %refs_10_), custom_call_target="tpu_custom_call" | custom-call | tf_op jit(solution)/shard_map/pallas_call | solution.py:48
  83.9 0.0 copy-start.1
  83.9 0.0 collective-permute-done.5.refs_6_
  83.9 0.0 collective-permute-done.4.refs_5_
  83.9 0.0 collective-permute-done.6.refs_7_
  83.9 0.2 collective-permute-done.7.refs_8_
  84.1 3.3 %all-to-all-done.arrived_ref = bf16[64,3,16,512]{3,2,1,0:T(8,128)(2,1)} async-done(((bf16[64,3,16,512]{3,2,1,0:T(8,128)(2,1)}), bf16[64,3,16,512]{3,2,1,0:T(8,128)(2,1)}, u32[]{:S(2)}, u32[]{:S(2)}) %all-to-all-start) | async-done | bytes 3145760 | tf_op jit(solution)/shard_map/all_to_all | solution.py:350
  87.4 0.0 copy-start.3
  87.4 5.5 %shard_map.75 = (bf16[3,128,512]{2,1,0:T(8,128)(2,1)}, bf16[3,128,512]{2,1,0:T(8,128)(2,1)}, bf16[3,128,512]{2,1,0:T(8,128)(2,1)}, bf16[3,128,512]{2,1,0:T(8,128)(2,1)}) custom-call(bf16[64,3,16,512]{3,2,1,0:T(8,128)(2,1)} %all-to-all-done.arrived_ref, bf16[4,128,1024]{2,1,0:T(8,128)(2,1)} %shard_map.74.spread_ref, bf16[4,128,512]{2,1,0:T(8,128)(2,1)} %bitcast.3), custom_call_target="tpu_custom_call" | custom-call | flops 1610612736 | bytes 6291456 | tf_op jit(solution)/shard_map/pallas_call | solution.py:232
  92.9 5.9 %collective-permute-start.8 = (bf16[3,128,512]{2,1,0:T(8,128)(2,1)}, bf16[3,128,512]{2,1,0:T(8,128)(2,1)S(1)}, u32[]{:S(2)}, u32[]{:S(2)}) collective-permute-start(bf16[3,128,512]{2,1,0:T(8,128)(2,1)} %get-tuple-element.59), channel_id=1, source_target_pairs={{0,128},{64,192},{128,0},{192,64},{1,129},{65,193},{129,1},{193,65... | collective-permute-start | bytes 1179656 | tf_op jit(solution)/shard_map/ppermute | solution.py:26
  98.8 3.7 %collective-permute-start.9 = (bf16[3,128,512]{2,1,0:T(8,128)(2,1)}, bf16[3,128,512]{2,1,0:T(8,128)(2,1)S(1)}, u32[]{:S(2)}, u32[]{:S(2)}) collective-permute-start(bf16[3,128,512]{2,1,0:T(8,128)(2,1)} %get-tuple-element.60), channel_id=1, source_target_pairs={{0,192},{64,128},{128,64},{192,0},{1,193},{65,129},{129,65},{193,1... | collective-permute-start | bytes 1179656 | tf_op jit(solution)/shard_map/ppermute | solution.py:26
  102.6 2.5 %collective-permute-start.10 = (bf16[3,128,512]{2,1,0:T(8,128)(2,1)}, bf16[3,128,512]{2,1,0:T(8,128)(2,1)S(1)}, u32[]{:S(2)}, u32[]{:S(2)}) collective-permute-start(bf16[3,128,512]{2,1,0:T(8,128)(2,1)} %get-tuple-element.61), channel_id=1, source_target_pairs={{0,64},{64,0},{128,192},{192,128},{1,65},{65,1},{129,193},{193,129... | collective-permute-start | bytes 1179656 | tf_op jit(solution)/shard_map/ppermute | solution.py:26
  105.0 0.0 copy-done.1
  105.1 0.0 copy-done.3
  105.1 0.0 copy-start.2
  105.1 2.7 %shard_map.76 = (bf16[4,2,3,256,512]{4,3,2,1,0:T(8,128)(2,1)S(1)}, bf16[128,512]{1,0:T(8,128)(2,1)S(1)}, bf16[128,128]{1,0:T(8,128)(2,1)S(1)}) custom-call(bf16[3,512,512]{2,1,0:T(8,128)(2,1)S(1)} %copy-done, bf16[3,256,512]{2,1,0:T(8,128)(2,1)} %collective-permute-done.refs_1_, bf16[3,256,512]{2,1,0:T(8,128)(2,1)S(1)} %collective-permute-done.1.refs_2_, ...), custom_call_target="tpu_custom_call" | custom-call | bytes 12582912 | tf_op jit(solution)/shard_map/pallas_call | solution.py:172
  107.7 16.7 %collective-permute-done.8.refs_4_ = bf16[3,128,512]{2,1,0:T(8,128)(2,1)S(1)} collective-permute-done((bf16[3,128,512]{2,1,0:T(8,128)(2,1)}, bf16[3,128,512]{2,1,0:T(8,128)(2,1)S(1)}, u32[]{:S(2)}, u32[]{:S(2)}) %collective-permute-start.8) | collective-permute-done | bytes 393248 | tf_op jit(solution)/shard_map/ppermute | solution.py:26
  124.5 0.0 collective-permute-done.9.refs_5_
  124.5 6.3 %collective-permute-done.10.refs_6_ = bf16[3,128,512]{2,1,0:T(8,128)(2,1)S(1)} collective-permute-done((bf16[3,128,512]{2,1,0:T(8,128)(2,1)}, bf16[3,128,512]{2,1,0:T(8,128)(2,1)S(1)}, u32[]{:S(2)}, u32[]{:S(2)}) %collective-permute-start.10) | collective-permute-done | bytes 393248 | tf_op jit(solution)/shard_map/ppermute | solution.py:26
  130.8 0.0 copy-done.2
  130.8 4.2 %shard_map.77 = (bf16[128,512]{1,0:T(8,128)(2,1)S(1)}, bf16[128,512]{1,0:T(8,128)(2,1)S(1)}, bf16[128,512]{1,0:T(8,128)(2,1)S(1)}, bf16[128,512]{1,0:T(8,128)(2,1)S(1)}, bf16[128,512]{1,0:T(8,128)(2,1)S(1)}) custom-call(bf16[128,512]{1,0:T(8,128)(2,1)S(1)} %get-tuple-element.55.refs_0_, bf16[128,128]{1,0:T(8,128)(2,1)S(1)} %get-tuple-element.56.refs_1_, ...), custom_call_target="tpu_custom_call" | custom-call | flops 1006632960 | bytes 7864320 | tf_op jit(solution)/shard_map/pallas_call | solution.py:309
  135.0 8.9 %collective-permute-start.11 = (bf16[128,512]{1,0:T(8,128)(2,1)S(1)}, bf16[128,512]{1,0:T(8,128)(2,1)S(1)}, u32[]{:S(2)}, u32[]{:S(2)}) collective-permute-start(bf16[128,512]{1,0:T(8,128)(2,1)S(1)} %get-tuple-element.62), channel_id=1, source_target_pairs={{0,384},{64,448},{128,256},{192,320},{1,385},{65,449},{129,257},{1... | collective-permute-start | bytes 393224 | tf_op jit(solution)/shard_map/ppermute | solution.py:371
  143.9 3.8 %collective-permute-done.11.refs_0_ = bf16[128,512]{1,0:T(8,128)(2,1)S(1)} collective-permute-done((bf16[128,512]{1,0:T(8,128)(2,1)S(1)}, bf16[128,512]{1,0:T(8,128)(2,1)S(1)}, u32[]{:S(2)}, u32[]{:S(2)}) %collective-permute-start.11) | collective-permute-done | bytes 131104 | tf_op jit(solution)/shard_map/ppermute | solution.py:371
  147.7 1.9 %collective-permute-start.12 = (bf16[128,512]{1,0:T(8,128)(2,1)S(1)}, bf16[128,512]{1,0:T(8,128)(2,1)S(1)}, u32[]{:S(2)}, u32[]{:S(2)}) collective-permute-start(bf16[128,512]{1,0:T(8,128)(2,1)S(1)} %get-tuple-element.68), channel_id=1, source_target_pairs={{0,128},{64,192},{128,0},{192,64},{1,129},{65,193},{129,1},{193,65... | collective-permute-start | bytes 393224 | tf_op jit(solution)/shard_map/ppermute | solution.py:26
  149.7 3.9 %collective-permute-start.13 = (bf16[128,512]{1,0:T(8,128)(2,1)S(1)}, bf16[128,512]{1,0:T(8,128)(2,1)S(1)}, u32[]{:S(2)}, u32[]{:S(2)}) collective-permute-start(bf16[128,512]{1,0:T(8,128)(2,1)S(1)} %get-tuple-element.69), channel_id=1, source_target_pairs={{0,192},{64,128},{128,64},{192,0},{1,193},{65,129},{129,65},{193,1... | collective-permute-start | bytes 393224 | tf_op jit(solution)/shard_map/ppermute | solution.py:26
  153.5 3.4 %collective-permute-start.14 = (bf16[128,512]{1,0:T(8,128)(2,1)S(1)}, bf16[128,512]{1,0:T(8,128)(2,1)S(1)}, u32[]{:S(2)}, u32[]{:S(2)}) collective-permute-start(bf16[128,512]{1,0:T(8,128)(2,1)S(1)} %get-tuple-element.70), channel_id=1, source_target_pairs={{0,64},{64,0},{128,192},{192,128},{1,65},{65,1},{129,193},{193,129... | collective-permute-start | bytes 393224 | tf_op jit(solution)/shard_map/ppermute | solution.py:26
  157.0 4.1 %collective-permute-done.12.refs_1_ = bf16[128,512]{1,0:T(8,128)(2,1)S(1)} collective-permute-done((bf16[128,512]{1,0:T(8,128)(2,1)S(1)}, bf16[128,512]{1,0:T(8,128)(2,1)S(1)}, u32[]{:S(2)}, u32[]{:S(2)}) %collective-permute-start.12) | collective-permute-done | bytes 131104 | tf_op jit(solution)/shard_map/ppermute | solution.py:26
  161.1 0.0 collective-permute-done.13.refs_2_
  161.1 2.7 %collective-permute-done.14.refs_3_ = bf16[128,512]{1,0:T(8,128)(2,1)S(1)} collective-permute-done((bf16[128,512]{1,0:T(8,128)(2,1)S(1)}, bf16[128,512]{1,0:T(8,128)(2,1)S(1)}, u32[]{:S(2)}, u32[]{:S(2)}) %collective-permute-start.14) | collective-permute-done | bytes 131104 | tf_op jit(solution)/shard_map/ppermute | solution.py:26
  163.7 0.8 shard_map.79
  (1 shorter events, 0.0 us)
Async XLA Ops:
  4.8 11.3 %copy-start = (bf16[3,512,512]{2,1,0:T(8,128)(2,1)S(1)}, bf16[3,512,512]{2,1,0:T(8,128)(2,1)}, u32[]{:S(2)}) copy-start(bf16[3,512,512]{2,1,0:T(8,128)(2,1)} %refs_0_) | copy-start | bytes 4718596
  4.8 82.6 %all-to-all-start = ((bf16[64,3,16,512]{3,2,1,0:T(8,128)(2,1)}), bf16[64,3,16,512]{3,2,1,0:T(8,128)(2,1)}, u32[]{:S(2)}, u32[]{:S(2)}) async-start(bf16[64,3,16,512]{3,2,1,0:T(8,128)(2,1)} %shard_map.73), calls=%async_computation | async-start | bytes 6291456 | tf_op jit(solution)/shard_map/all_to_all | solution.py:350
  16.1 40.7 %collective-permute-start.1 = (bf16[3,256,512]{2,1,0:T(8,128)(2,1)S(1)}, bf16[3,256,512]{2,1,0:T(8,128)(2,1)S(1)}, u32[]{:S(2)}, u32[]{:S(2)}) collective-permute-start(bf16[3,256,512]{2,1,0:T(8,128)(2,1)S(1)} %constant_dynamic-slice_fusion), channel_id=1, source_target_pairs={{0,128},{64,192},{128,0},{192,64},{1,129},{65,193},{129,1},{193,65... | collective-permute-start | bytes 2359304 | tf_op jit(solution)/shard_map/ppermute | solution.py:26
  22.1 39.6 %collective-permute-start = (bf16[3,256,512]{2,1,0:T(8,128)(2,1)S(1)}, bf16[3,256,512]{2,1,0:T(8,128)(2,1)}, u32[]{:S(2)}, u32[]{:S(2)}) collective-permute-start(bf16[3,256,512]{2,1,0:T(8,128)(2,1)S(1)} %constant_dynamic-slice_fusion), channel_id=1, source_target_pairs={{0,64},{64,0},{128,192},{192,128},{1,65},{65,1},{129,193},{193,129... | collective-permute-start | bytes 2359304 | tf_op jit(solution)/shard_map/ppermute | solution.py:26
  56.9 7.3 %collective-permute-start.2 = (bf16[3,256,512]{2,1,0:T(8,128)(2,1)S(1)}, bf16[3,256,512]{2,1,0:T(8,128)(2,1)}, u32[]{:S(2)}, u32[]{:S(2)}) collective-permute-start(bf16[3,256,512]{2,1,0:T(8,128)(2,1)S(1)} %constant_dynamic-slice_fusion), channel_id=1, source_target_pairs={{64,128},{128,64},{65,129},{129,65},{66,130},{130,66},{67,131},{13... | collective-permute-start | bytes 2359304 | tf_op jit(solution)/shard_map/ppermute | solution.py:358
  58.5 21.1 %collective-permute-start.3 = (bf16[3,256,512]{2,1,0:T(8,128)(2,1)S(1)}, bf16[3,256,512]{2,1,0:T(8,128)(2,1)}, u32[]{:S(2)}, u32[]{:S(2)}) collective-permute-start(bf16[3,256,512]{2,1,0:T(8,128)(2,1)S(1)} %collective-permute-done.1.refs_2_), channel_id=1, source_target_pairs={{64,0},{128,192},{65,1},{129,193},{66,2},{130,194},{67,3},{131,195... | collective-permute-start | bytes 2359304 | tf_op jit(solution)/shard_map/ppermute | solution.py:359
  59.8 24.1 %collective-permute-start.5 = (bf16[3,256,512]{2,1,0:T(8,128)(2,1)S(1)}, bf16[3,256,512]{2,1,0:T(8,128)(2,1)}, u32[]{:S(2)}, u32[]{:S(2)}) collective-permute-start(bf16[3,256,512]{2,1,0:T(8,128)(2,1)S(1)} %collective-permute-done.1.refs_2_), channel_id=1, source_target_pairs={{0,1},{1,0},{2,3},{3,2},{4,5},{5,4},{6,7},{7,6},{8,9},{9,8},{10,11... | collective-permute-start | bytes 2359304 | tf_op jit(solution)/shard_map/ppermute | solution.py:34
  61.7 22.1 %collective-permute-start.4 = (bf16[3,256,512]{2,1,0:T(8,128)(2,1)}, bf16[3,256,512]{2,1,0:T(8,128)(2,1)}, u32[]{:S(2)}, u32[]{:S(2)}) collective-permute-start(bf16[3,256,512]{2,1,0:T(8,128)(2,1)} %collective-permute-done.refs_1_), channel_id=1, source_target_pairs={{0,1},{1,0},{2,3},{3,2},{4,5},{5,4},{6,7},{7,6},{8,9},{9,8},{10,11... | collective-permute-start | bytes 2359304 | tf_op jit(solution)/shard_map/ppermute | solution.py:34
  64.1 19.7 %collective-permute-start.6 = (bf16[3,256,512]{2,1,0:T(8,128)(2,1)}, bf16[3,256,512]{2,1,0:T(8,128)(2,1)}, u32[]{:S(2)}, u32[]{:S(2)}) collective-permute-start(bf16[3,256,512]{2,1,0:T(8,128)(2,1)} %collective-permute-done.2.refs_3_), channel_id=1, source_target_pairs={{0,1},{1,0},{2,3},{3,2},{4,5},{5,4},{6,7},{7,6},{8,9},{9,8},{10,11... | collective-permute-start | bytes 2359304 | tf_op jit(solution)/shard_map/ppermute | solution.py:34
  79.6 4.5 %collective-permute-start.7 = (bf16[3,256,512]{2,1,0:T(8,128)(2,1)}, bf16[3,256,512]{2,1,0:T(8,128)(2,1)}, u32[]{:S(2)}, u32[]{:S(2)}) collective-permute-start(bf16[3,256,512]{2,1,0:T(8,128)(2,1)} %collective-permute-done.3.refs_4_), channel_id=1, source_target_pairs={{0,1},{1,0},{2,3},{3,2},{4,5},{5,4},{6,7},{7,6},{8,9},{9,8},{10,11... | collective-permute-start | bytes 2359304 | tf_op jit(solution)/shard_map/ppermute | solution.py:34
  83.9 21.2 %copy-start.1 = (bf16[4,6,128,128]{3,2,1,0:T(8,128)(2,1)S(1)}, bf16[4,6,128,128]{3,2,1,0:T(8,128)(2,1)}, u32[]{:S(2)}) copy-start(bf16[4,6,128,128]{3,2,1,0:T(8,128)(2,1)} %refs_10_) | copy-start | bytes 2359300
  87.4 17.7 %copy-start.3 = (bf16[512,512]{1,0:T(8,128)(2,1)S(1)}, bf16[512,512]{1,0:T(8,128)(2,1)}, u32[]{:S(2)}) copy-start(bf16[512,512]{1,0:T(8,128)(2,1)} %param.7) | copy-start | bytes 1572868
  92.9 31.6 %collective-permute-start.8 = (bf16[3,128,512]{2,1,0:T(8,128)(2,1)}, bf16[3,128,512]{2,1,0:T(8,128)(2,1)S(1)}, u32[]{:S(2)}, u32[]{:S(2)}) collective-permute-start(bf16[3,128,512]{2,1,0:T(8,128)(2,1)} %get-tuple-element.59), channel_id=1, source_target_pairs={{0,128},{64,192},{128,0},{192,64},{1,129},{65,193},{129,1},{193,65... | collective-permute-start | bytes 1179656 | tf_op jit(solution)/shard_map/ppermute | solution.py:26
  98.8 25.6 %collective-permute-start.9 = (bf16[3,128,512]{2,1,0:T(8,128)(2,1)}, bf16[3,128,512]{2,1,0:T(8,128)(2,1)S(1)}, u32[]{:S(2)}, u32[]{:S(2)}) collective-permute-start(bf16[3,128,512]{2,1,0:T(8,128)(2,1)} %get-tuple-element.60), channel_id=1, source_target_pairs={{0,192},{64,128},{128,64},{192,0},{1,193},{65,129},{129,65},{193,1... | collective-permute-start | bytes 1179656 | tf_op jit(solution)/shard_map/ppermute | solution.py:26
  102.6 28.2 %collective-permute-start.10 = (bf16[3,128,512]{2,1,0:T(8,128)(2,1)}, bf16[3,128,512]{2,1,0:T(8,128)(2,1)S(1)}, u32[]{:S(2)}, u32[]{:S(2)}) collective-permute-start(bf16[3,128,512]{2,1,0:T(8,128)(2,1)} %get-tuple-element.61), channel_id=1, source_target_pairs={{0,64},{64,0},{128,192},{192,128},{1,65},{65,1},{129,193},{193,129... | collective-permute-start | bytes 1179656 | tf_op jit(solution)/shard_map/ppermute | solution.py:26
  105.1 25.7 %copy-start.2 = (bf16[3,128,512]{2,1,0:T(8,128)(2,1)S(1)}, bf16[3,128,512]{2,1,0:T(8,128)(2,1)}, u32[]{:S(2)}) copy-start(bf16[3,128,512]{2,1,0:T(8,128)(2,1)} %get-tuple-element.58.refs_3_) | copy-start | bytes 1179652
  135.0 12.7 %collective-permute-start.11 = (bf16[128,512]{1,0:T(8,128)(2,1)S(1)}, bf16[128,512]{1,0:T(8,128)(2,1)S(1)}, u32[]{:S(2)}, u32[]{:S(2)}) collective-permute-start(bf16[128,512]{1,0:T(8,128)(2,1)S(1)} %get-tuple-element.62), channel_id=1, source_target_pairs={{0,384},{64,448},{128,256},{192,320},{1,385},{65,449},{129,257},{1... | collective-permute-start | bytes 393224 | tf_op jit(solution)/shard_map/ppermute | solution.py:371
  147.7 13.3 %collective-permute-start.12 = (bf16[128,512]{1,0:T(8,128)(2,1)S(1)}, bf16[128,512]{1,0:T(8,128)(2,1)S(1)}, u32[]{:S(2)}, u32[]{:S(2)}) collective-permute-start(bf16[128,512]{1,0:T(8,128)(2,1)S(1)} %get-tuple-element.68), channel_id=1, source_target_pairs={{0,128},{64,192},{128,0},{192,64},{1,129},{65,193},{129,1},{193,65... | collective-permute-start | bytes 393224 | tf_op jit(solution)/shard_map/ppermute | solution.py:26
  149.7 11.4 %collective-permute-start.13 = (bf16[128,512]{1,0:T(8,128)(2,1)S(1)}, bf16[128,512]{1,0:T(8,128)(2,1)S(1)}, u32[]{:S(2)}, u32[]{:S(2)}) collective-permute-start(bf16[128,512]{1,0:T(8,128)(2,1)S(1)} %get-tuple-element.69), channel_id=1, source_target_pairs={{0,192},{64,128},{128,64},{192,0},{1,193},{65,129},{129,65},{193,1... | collective-permute-start | bytes 393224 | tf_op jit(solution)/shard_map/ppermute | solution.py:26
  153.5 10.2 %collective-permute-start.14 = (bf16[128,512]{1,0:T(8,128)(2,1)S(1)}, bf16[128,512]{1,0:T(8,128)(2,1)S(1)}, u32[]{:S(2)}, u32[]{:S(2)}) collective-permute-start(bf16[128,512]{1,0:T(8,128)(2,1)S(1)} %get-tuple-element.70), channel_id=1, source_target_pairs={{0,64},{64,0},{128,192},{192,128},{1,65},{65,1},{129,193},{193,129... | collective-permute-start | bytes 393224 | tf_op jit(solution)/shard_map/ppermute | solution.py:26

commit v7 on v6

--- a/solution.py
+++ b/solution.py
@@ -55,7 +55,7 @@
 
 
 def pick_kernel(rows_ref, count_ref, history_ref, out_ref, *scratch):
-    history_buf, pick_buf, out_buf, in_sem, out_sem = scratch
+    rows_buf, count_buf, history_buf, pick_buf, out_buf, list_sem, in_sem, out_sem = scratch
     receivers, levels, slots, width = out_ref.shape
     rows = history_ref.shape[1]
     parts = in_sem.shape[1]
@@ -71,11 +71,17 @@
         ]
         for i in range(levels)
     ]
-    for load in sum(loads, []):
+    lists = [
+        pltpu.make_async_copy(rows_ref, rows_buf, list_sem.at[0]),
+        pltpu.make_async_copy(count_ref, count_buf, list_sem.at[1]),
+    ]
+    for load in lists + sum(loads, []):
         load.start()
+    for load in lists:
+        load.wait()
 
     slot = lax.broadcasted_iota(jnp.int32, (slots, receivers), 0)
-    wanted = jnp.where(slot < count_ref[...], rows_ref[0], -1)
+    wanted = jnp.where(slot < count_buf[...], rows_buf[0], -1)
     column = lax.broadcasted_iota(jnp.int32, (slots, rows), 1)
     for p in range(receivers):
         mask = jnp.where(wanted[:, p : p + 1] == column, 1.0, 0.0)
@@ -110,12 +116,15 @@
     return pl.pallas_call(
         pick_kernel,
         out_shape=jax.ShapeDtypeStruct((parts, levels, slots, width), jnp.bfloat16),
-        in_specs=[VMEM, VMEM, ANYWHERE],
+        in_specs=[ANYWHERE] * 3,
         out_specs=ANYWHERE,
         scratch_shapes=[
+            pltpu.VMEM((1, slots, parts), jnp.int32),
+            pltpu.VMEM((1, parts), jnp.int32),
             pltpu.VMEM(history.shape, jnp.bfloat16),
             pltpu.VMEM((parts * slots, rows), jnp.bfloat16),
             pltpu.VMEM((levels, parts, slots, width), jnp.bfloat16),
+            pltpu.SemaphoreType.DMA((2,)),
             pltpu.SemaphoreType.DMA((levels, 2)),
             pltpu.SemaphoreType.DMA((levels, 4)),
         ],
@@ -182,15 +191,15 @@
     )(*sources)
 
 
-def halo_kernel(arrived_ref, spread_ref, features_ref, *refs):
+def halo_kernel(arrived_ref, spread_ref, *refs):
     out_refs = refs[:STAGES]
-    arrived_buf, spread_buf, features_buf, out_buf, in_sem, own_sem, out_sem = refs[STAGES:]
+    arrived_buf, spread_buf, out_buf, in_sem, own_sem, out_sem = refs[STAGES:]
     parts, levels, slots, width = arrived_ref.shape
     rows = spread_ref.shape[1]
-    own = []
-    for n, r in enumerate(SLOTS):
-        for m, (ref, buf) in enumerate([(spread_ref, spread_buf), (features_ref, features_buf)]):
-            own.append(pltpu.make_async_copy(ref.at[tile_of(r)], buf.at[n], own_sem.at[m, n]))
+    spreads = [
+        pltpu.make_async_copy(spread_ref.at[tile_of(r)], spread_buf.at[n], own_sem.at[n])
+        for n, r in enumerate(SLOTS)
+    ]
     chunks = in_sem.shape[1]
     group = parts // chunks
     loads = [
@@ -204,21 +213,22 @@
         ]
         for i in range(levels)
     ]
-    for load in loads[0] + own + sum(loads[1:], []):
+    for load in spreads + sum(loads, []):
         load.start()
-    for load in own:
+    for load in spreads + loads[0]:
         load.wait()
-    spread = spread_buf[...].reshape(STAGES * rows, parts * slots)
     stores = []
     for i in range(levels):
-        for load in loads[i]:
-            load.wait()
-        halo = arrived_buf[i].reshape(parts * slots, width)
-        summed = jnp.dot(spread, halo, preferred_element_type=jnp.float32)
+        if i > 0:
+            for load in loads[i]:
+                load.wait()
+        summed = jnp.dot(
+            spread_buf[...].reshape(STAGES * rows, parts * slots),
+            arrived_buf[i].reshape(parts * slots, width),
+            preferred_element_type=jnp.float32,
+        )
         for n in range(STAGES):
-            start = 0.1 * features_buf[n].astype(jnp.float32)
-            part = 0.9 * summed[n * rows : (n + 1) * rows] + start
-            out_buf[n, i] = part.astype(jnp.bfloat16)
+            out_buf[n, i] = summed[n * rows : (n + 1) * rows].astype(jnp.bfloat16)
             store = pltpu.make_async_copy(out_buf.at[n, i], out_refs[n].at[i], out_sem.at[n, i])
             store.start()
             stores.append(store)
@@ -226,33 +236,32 @@
         store.wait()
 
 
-def halo_sums(arrived, spread, features):
+def halo_sums(arrived, spread):
     parts, levels, slots, width = arrived.shape
     _, rows, halo_rows = spread.shape
     return pl.pallas_call(
         halo_kernel,
         out_shape=[jax.ShapeDtypeStruct((levels, rows, width), jnp.bfloat16)] * STAGES,
-        in_specs=[ANYWHERE] * 3,
+        in_specs=[ANYWHERE] * 2,
         out_specs=[ANYWHERE] * STAGES,
         scratch_shapes=[
             pltpu.VMEM((levels, parts, slots, width), jnp.bfloat16),
             pltpu.VMEM(spread.shape, jnp.bfloat16),
-            pltpu.VMEM(features.shape, jnp.bfloat16),
             pltpu.VMEM((STAGES, levels, rows, width), jnp.bfloat16),
             pltpu.SemaphoreType.DMA((levels, 4)),
-            pltpu.SemaphoreType.DMA((2, STAGES)),
+            pltpu.SemaphoreType.DMA((STAGES,)),
             pltpu.SemaphoreType.DMA((STAGES, levels)),
         ],
         compiler_params=GRANT,
         cost_estimate=pl.CostEstimate(
             flops=2 * levels * STAGES * rows * halo_rows * width,
-            bytes_accessed=2 * (arrived.size + spread.size + features.size * (1 + levels)),
+            bytes_accessed=2 * (arrived.size + spread.size + STAGES * levels * rows * width),
             transcendentals=0,
         ),
-    )(arrived, spread, features)
-
-
-def chain_kernel(which, betas, x_ref, a_ref, w_ref, *refs):
+    )(arrived, spread)
+
+
+def chain_kernel(which, betas, x_ref, features_ref, a_ref, w_ref, *refs):
     stages, cores, levels, depth, _ = w_ref.shape
     h_refs, refs = refs[:stages], refs[stages:]
     if which > 0:
@@ -267,11 +276,12 @@
             h_buf[stage ^ r] = h_ref[...]
         a = a_ref[...]
         x = x_ref[...]
+        start = 0.1 * features_ref[...].astype(jnp.float32)
         for s in range(stages):
             for i in range(levels):
                 beta = betas[(which * stages + s) * levels + i]
                 summed = jnp.dot(a, x, preferred_element_type=jnp.float32)
-                support = 0.9 * summed + h_buf[s, i].astype(jnp.float32)
+                support = 0.9 * (summed + h_buf[s, i].astype(jnp.float32)) + start
                 rounded = support.astype(jnp.bfloat16)
                 branch = sum(
                     jnp.dot(
@@ -300,7 +310,7 @@
                 out_refs[r][...] = before_refs[r][...]
 
 
-def chain(which, x, a, weights, halos, before=()):
+def chain(which, x, features, a, weights, halos, before=()):
     stages, _, levels, _, width = weights.shape
     rows = x.shape[0]
     order = np.arange(HALVES * stages * levels, dtype=np.float32)
@@ -309,7 +319,7 @@
     return pl.pallas_call(
         lambda *refs: chain_kernel(which, betas, *refs),
         out_shape=[jax.ShapeDtypeStruct((rows, width), jnp.bfloat16)] * outs,
-        in_specs=[VMEM] * (3 + len(halos) + len(before)),
+        in_specs=[VMEM] * (4 + len(halos) + len(before)),
         out_specs=[VMEM] * outs,
         scratch_shapes=[pltpu.VMEM((stages, levels, rows, width), jnp.bfloat16)],
         compiler_params=SMALL,
@@ -318,7 +328,7 @@
             bytes_accessed=2 * stages * levels * width * (width + rows),
             transcendentals=0,
         ),
-    )(x, a, weights, *halos, *before)
+    )(x, features, a, weights, *halos, *before)
 
 
 def place_kernel(*refs):
@@ -361,14 +371,14 @@
     spread = spread_blocks(adj_src, adj_blocks, halo_rows)
     arrived, spread, near, far = lax.optimization_barrier((arrived, spread, near, far))
 
-    sums = halo_sums(arrived, spread, tiles)
+    sums = halo_sums(arrived, spread)
     token, weights = lax.optimization_barrier((sums[0], weights))
     halos = exchange_all([token, *sums[1:]])
     group, own_x, own_a = stage_operands(weights, near, far, tiles, adj_blocks)
 
-    *first, last = chain(0, own_x, own_a, group, halos)
+    *first, last = chain(0, own_x, own_x, own_a, group, halos)
     over = [(s, STAGES + (s ^ 2)) for s in range(STAGES)]
-    done = chain(1, lax.ppermute(last, SEGMENT, over), own_a, group, halos, first)
+    done = chain(1, lax.ppermute(last, SEGMENT, over), own_x, own_a, group, halos, first)
     fresh = place(exchange_all(done))
     return fresh.reshape(1, rows_dev, width)
 

time: 166 us -> 166 us (level)
  no operation moved by 1% of the time
where the time goes in v7:
time: 166 us; the launch traced here: 164 us
  waiting for transfers between devices  81.2 us (49%)
  starting transfers between devices  62.7 us (38%)
  Pallas kernels  19.8 us (12%)
    ppermute x8, waiting for transfers between devices, exchange(): return lax.ppermute(block, 'stage', [(u, u ^ slot) for u in range(STAGES)])  60.3 us
    ppermute x8, starting transfers between devices, exchange(): return lax.ppermute(block, 'stage', [(u, u ^ slot) for u in range(STAGES)])  31.6 us
    ppermute x1, waiting for transfers between devices, local(): near.append(lax.ppermute(two, 'stage', [(1, 0), (2, 3)]))  13.5 us
    all_to_all x1, starting transfers between devices, local(): lax.all_to_all(outgoing, DOM, split_axis=0, concat_axis=0, tiled=True)  11.3 us
    ppermute x1, starting transfers between devices, local(): lax.ppermute(last, SEGMENT, over)  8.85 us
    ppermute x4, starting transfers between devices, swap_cores(): return lax.ppermute(block, 'core', [(0, 1), (1, 0)])  8.16 us
    pallas_call x1, Pallas kernels, halo_sums(): pl.pallas_call(halo_kernel, out_shape=[jax.ShapeDtypeStruct((levels, rows...  5.19 us
    pallas_call x1, Pallas kernels, pick_rows(): pl.pallas_call(pick_kernel, out_shape=jax.ShapeDtypeStruct((parts, levels...  4.43 us
  transfers between devices with their start and end apart: 16, of which 9 were waited for; matrix products, arithmetic and copies ran while one was open for 0% of the time, Pallas kernels for 3%

profile of v7, /device:TPU:6, one launch (start us, length us, event | category | flops | bytes accessed | tf_op | source)
XLA Modules:
  0.0 164.0 jit_solution(7958951109956970828)
XLA Ops:
  0.0 4.4 %shard_map.73 = bf16[64,3,16,512]{3,2,1,0:T(8,128)(2,1)} custom-call(s32[1,16,64]{2,1,0:T(8,128)} %bitcast.4, s32[1,64]{1,0:T(1,128)} %count_ref.1, bf16[3,512,512]{2,1,0:T(8,128)(2,1)} %history_ref.1), custom_call_target="tpu_custom_call" | custom-call | flops 1610612736 | bytes 4718592 | tf_op jit(solution)/shard_map/pallas_call | solution.py:116
  4.4 0.0 copy-start
  4.4 11.3 %all-to-all-start = ((bf16[64,3,16,512]{3,2,1,0:T(8,128)(2,1)}), bf16[64,3,16,512]{3,2,1,0:T(8,128)(2,1)}, u32[]{:S(2)}, u32[]{:S(2)}) async-start(bf16[64,3,16,512]{3,2,1,0:T(8,128)(2,1)} %shard_map.73), calls=%async_computation | async-start | bytes 6291456 | tf_op jit(solution)/shard_map/all_to_all | solution.py:360
  15.7 0.0 copy-done
  15.7 0.1 constant_dynamic-slice_fusion
  15.8 5.9 %collective-permute-start.1 = (bf16[3,256,512]{2,1,0:T(8,128)(2,1)S(1)}, bf16[3,256,512]{2,1,0:T(8,128)(2,1)S(1)}, u32[]{:S(2)}, u32[]{:S(2)}) collective-permute-start(bf16[3,256,512]{2,1,0:T(8,128)(2,1)S(1)} %constant_dynamic-slice_fusion), channel_id=1, source_target_pairs={{0,128},{64,192},{128,0},{192,64},{1,129},{65,193},{129,1},{193,65... | collective-permute-start | bytes 2359304 | tf_op jit(solution)/shard_map/ppermute | solution.py:26
  21.7 4.3 %collective-permute-start = (bf16[3,256,512]{2,1,0:T(8,128)(2,1)S(1)}, bf16[3,256,512]{2,1,0:T(8,128)(2,1)}, u32[]{:S(2)}, u32[]{:S(2)}) collective-permute-start(bf16[3,256,512]{2,1,0:T(8,128)(2,1)S(1)} %constant_dynamic-slice_fusion), channel_id=1, source_target_pairs={{0,64},{64,0},{128,192},{192,128},{1,65},{65,1},{129,193},{193,129... | collective-permute-start | bytes 2359304 | tf_op jit(solution)/shard_map/ppermute | solution.py:26
  26.0 30.5 %collective-permute-done.1.refs_2_ = bf16[3,256,512]{2,1,0:T(8,128)(2,1)S(1)} collective-permute-done((bf16[3,256,512]{2,1,0:T(8,128)(2,1)S(1)}, bf16[3,256,512]{2,1,0:T(8,128)(2,1)S(1)}, u32[]{:S(2)}, u32[]{:S(2)}) %collective-permute-start.1) | collective-permute-done | bytes 786464 | tf_op jit(solution)/shard_map/ppermute | solution.py:26
  56.5 1.6 collective-permute-start.2
  58.2 1.3 collective-permute-start.3
  59.4 1.9 %collective-permute-start.5 = (bf16[3,256,512]{2,1,0:T(8,128)(2,1)S(1)}, bf16[3,256,512]{2,1,0:T(8,128)(2,1)}, u32[]{:S(2)}, u32[]{:S(2)}) collective-permute-start(bf16[3,256,512]{2,1,0:T(8,128)(2,1)S(1)} %collective-permute-done.1.refs_2_), channel_id=1, source_target_pairs={{0,1},{1,0},{2,3},{3,2},{4,5},{5,4},{6,7},{7,6},{8,9},{9,8},{10,11... | collective-permute-start | bytes 2359304 | tf_op jit(solution)/shard_map/ppermute | solution.py:34
  61.4 0.0 collective-permute-done.refs_1_
  61.4 2.4 %collective-permute-start.4 = (bf16[3,256,512]{2,1,0:T(8,128)(2,1)}, bf16[3,256,512]{2,1,0:T(8,128)(2,1)}, u32[]{:S(2)}, u32[]{:S(2)}) collective-permute-start(bf16[3,256,512]{2,1,0:T(8,128)(2,1)} %collective-permute-done.refs_1_), channel_id=1, source_target_pairs={{0,1},{1,0},{2,3},{3,2},{4,5},{5,4},{6,7},{7,6},{8,9},{9,8},{10,11... | collective-permute-start | bytes 2359304 | tf_op jit(solution)/shard_map/ppermute | solution.py:34
  63.8 0.0 collective-permute-done.2.refs_3_
  63.8 1.9 %collective-permute-start.6 = (bf16[3,256,512]{2,1,0:T(8,128)(2,1)}, bf16[3,256,512]{2,1,0:T(8,128)(2,1)}, u32[]{:S(2)}, u32[]{:S(2)}) collective-permute-start(bf16[3,256,512]{2,1,0:T(8,128)(2,1)} %collective-permute-done.2.refs_3_), channel_id=1, source_target_pairs={{0,1},{1,0},{2,3},{3,2},{4,5},{5,4},{6,7},{7,6},{8,9},{9,8},{10,11... | collective-permute-start | bytes 2359304 | tf_op jit(solution)/shard_map/ppermute | solution.py:34
  65.7 13.5 %collective-permute-done.3.refs_4_ = bf16[3,256,512]{2,1,0:T(8,128)(2,1)} collective-permute-done((bf16[3,256,512]{2,1,0:T(8,128)(2,1)S(1)}, bf16[3,256,512]{2,1,0:T(8,128)(2,1)}, u32[]{:S(2)}, u32[]{:S(2)}) %collective-permute-start.3) | collective-permute-done | bytes 786464 | tf_op jit(solution)/shard_map/ppermute | solution.py:369
  79.3 1.9 %collective-permute-start.7 = (bf16[3,256,512]{2,1,0:T(8,128)(2,1)}, bf16[3,256,512]{2,1,0:T(8,128)(2,1)}, u32[]{:S(2)}, u32[]{:S(2)}) collective-permute-start(bf16[3,256,512]{2,1,0:T(8,128)(2,1)} %collective-permute-done.3.refs_4_), channel_id=1, source_target_pairs={{0,1},{1,0},{2,3},{3,2},{4,5},{5,4},{6,7},{7,6},{8,9},{9,8},{10,11... | collective-permute-start | bytes 2359304 | tf_op jit(solution)/shard_map/ppermute | solution.py:34
  81.2 2.3 %shard_map.74.spread_ref = bf16[4,128,1024]{2,1,0:T(8,128)(2,1)} custom-call(s32[4,6]{1,0:T(4,128)} %source_ref.1, bf16[4,6,128,128]{3,2,1,0:T(8,128)(2,1)} %refs_10_), custom_call_target="tpu_custom_call" | custom-call | tf_op jit(solution)/shard_map/pallas_call | solution.py:48
  83.5 0.0 copy-start.1
  83.5 0.0 collective-permute-done.5.refs_6_
  83.5 0.0 collective-permute-done.4.refs_5_
  83.5 0.0 collective-permute-done.6.refs_7_
  83.5 0.2 collective-permute-done.7.refs_8_
  83.8 3.3 %all-to-all-done.arrived_ref = bf16[64,3,16,512]{3,2,1,0:T(8,128)(2,1)} async-done(((bf16[64,3,16,512]{3,2,1,0:T(8,128)(2,1)}), bf16[64,3,16,512]{3,2,1,0:T(8,128)(2,1)}, u32[]{:S(2)}, u32[]{:S(2)}) %all-to-all-start) | async-done | bytes 3145760 | tf_op jit(solution)/shard_map/all_to_all | solution.py:360
  87.0 0.0 copy-start.3
  87.0 5.2 %shard_map.75 = (bf16[3,128,512]{2,1,0:T(8,128)(2,1)}, bf16[3,128,512]{2,1,0:T(8,128)(2,1)}, bf16[3,128,512]{2,1,0:T(8,128)(2,1)}, bf16[3,128,512]{2,1,0:T(8,128)(2,1)}) custom-call(bf16[64,3,16,512]{3,2,1,0:T(8,128)(2,1)} %all-to-all-done.arrived_ref, bf16[4,128,1024]{2,1,0:T(8,128)(2,1)} %shard_map.74.spread_ref), custom_call_target="tpu_custom_call" | custom-call | flops 1610612736 | bytes 5767168 | tf_op jit(solution)/shard_map/pallas_call | solution.py:242
  92.2 5.9 %collective-permute-start.8 = (bf16[3,128,512]{2,1,0:T(8,128)(2,1)}, bf16[3,128,512]{2,1,0:T(8,128)(2,1)S(1)}, u32[]{:S(2)}, u32[]{:S(2)}) collective-permute-start(bf16[3,128,512]{2,1,0:T(8,128)(2,1)} %get-tuple-element.59), channel_id=1, source_target_pairs={{0,128},{64,192},{128,0},{192,64},{1,129},{65,193},{129,1},{193,65... | collective-permute-start | bytes 1179656 | tf_op jit(solution)/shard_map/ppermute | solution.py:26
  98.2 3.7 %collective-permute-start.9 = (bf16[3,128,512]{2,1,0:T(8,128)(2,1)}, bf16[3,128,512]{2,1,0:T(8,128)(2,1)S(1)}, u32[]{:S(2)}, u32[]{:S(2)}) collective-permute-start(bf16[3,128,512]{2,1,0:T(8,128)(2,1)} %get-tuple-element.60), channel_id=1, source_target_pairs={{0,192},{64,128},{128,64},{192,0},{1,193},{65,129},{129,65},{193,1... | collective-permute-start | bytes 1179656 | tf_op jit(solution)/shard_map/ppermute | solution.py:26
  101.9 2.5 %collective-permute-start.10 = (bf16[3,128,512]{2,1,0:T(8,128)(2,1)}, bf16[3,128,512]{2,1,0:T(8,128)(2,1)S(1)}, u32[]{:S(2)}, u32[]{:S(2)}) collective-permute-start(bf16[3,128,512]{2,1,0:T(8,128)(2,1)} %get-tuple-element.61), channel_id=1, source_target_pairs={{0,64},{64,0},{128,192},{192,128},{1,65},{65,1},{129,193},{193,129... | collective-permute-start | bytes 1179656 | tf_op jit(solution)/shard_map/ppermute | solution.py:26
  104.4 0.0 copy-done.1
  104.4 0.0 copy-done.3
  104.4 0.0 copy-start.2
  104.4 2.7 %shard_map.76 = (bf16[4,2,3,256,512]{4,3,2,1,0:T(8,128)(2,1)S(1)}, bf16[128,512]{1,0:T(8,128)(2,1)S(1)}, bf16[128,128]{1,0:T(8,128)(2,1)S(1)}) custom-call(bf16[3,512,512]{2,1,0:T(8,128)(2,1)S(1)} %copy-done, bf16[3,256,512]{2,1,0:T(8,128)(2,1)} %collective-permute-done.refs_1_, bf16[3,256,512]{2,1,0:T(8,128)(2,1)S(1)} %collective-permute-done.1.refs_2_, ...), custom_call_target="tpu_custom_call" | custom-call | bytes 12582912 | tf_op jit(solution)/shard_map/pallas_call | solution.py:181
  107.1 16.7 %collective-permute-done.8.refs_5_ = bf16[3,128,512]{2,1,0:T(8,128)(2,1)S(1)} collective-permute-done((bf16[3,128,512]{2,1,0:T(8,128)(2,1)}, bf16[3,128,512]{2,1,0:T(8,128)(2,1)S(1)}, u32[]{:S(2)}, u32[]{:S(2)}) %collective-permute-start.8) | collective-permute-done | bytes 393248 | tf_op jit(solution)/shard_map/ppermute | solution.py:26
  123.8 0.0 collective-permute-done.9.refs_6_
  123.8 6.3 %collective-permute-done.10.refs_7_ = bf16[3,128,512]{2,1,0:T(8,128)(2,1)S(1)} collective-permute-done((bf16[3,128,512]{2,1,0:T(8,128)(2,1)}, bf16[3,128,512]{2,1,0:T(8,128)(2,1)S(1)}, u32[]{:S(2)}, u32[]{:S(2)}) %collective-permute-start.10) | collective-permute-done | bytes 393248 | tf_op jit(solution)/shard_map/ppermute | solution.py:26
  130.1 0.0 copy-done.2
  130.1 4.3 %shard_map.77 = (bf16[128,512]{1,0:T(8,128)(2,1)S(1)}, bf16[128,512]{1,0:T(8,128)(2,1)S(1)}, bf16[128,512]{1,0:T(8,128)(2,1)S(1)}, bf16[128,512]{1,0:T(8,128)(2,1)S(1)}, bf16[128,512]{1,0:T(8,128)(2,1)S(1)}) custom-call(bf16[128,512]{1,0:T(8,128)(2,1)S(1)} %get-tuple-element.55.refs_0_.refs_1_, bf16[128,512]{1,0:T(8,128)(2,1)S(1)} %get-tuple-element.55.refs_0_.refs_1_, ...), custom_call_target="tpu_custom_call" | custom-call | flops 1006632960 | bytes 7864320 | tf_op jit(solution)/shard_map/pallas_call | solution.py:319
  134.4 8.9 %collective-permute-start.11 = (bf16[128,512]{1,0:T(8,128)(2,1)S(1)}, bf16[128,512]{1,0:T(8,128)(2,1)S(1)}, u32[]{:S(2)}, u32[]{:S(2)}) collective-permute-start(bf16[128,512]{1,0:T(8,128)(2,1)S(1)} %get-tuple-element.62), channel_id=1, source_target_pairs={{0,384},{64,448},{128,256},{192,320},{1,385},{65,449},{129,257},{1... | collective-permute-start | bytes 393224 | tf_op jit(solution)/shard_map/ppermute | solution.py:381
  143.3 3.8 %collective-permute-done.11.refs_0_ = bf16[128,512]{1,0:T(8,128)(2,1)S(1)} collective-permute-done((bf16[128,512]{1,0:T(8,128)(2,1)S(1)}, bf16[128,512]{1,0:T(8,128)(2,1)S(1)}, u32[]{:S(2)}, u32[]{:S(2)}) %collective-permute-start.11) | collective-permute-done | bytes 131104 | tf_op jit(solution)/shard_map/ppermute | solution.py:381
  147.1 1.9 %collective-permute-start.12 = (bf16[128,512]{1,0:T(8,128)(2,1)S(1)}, bf16[128,512]{1,0:T(8,128)(2,1)S(1)}, u32[]{:S(2)}, u32[]{:S(2)}) collective-permute-start(bf16[128,512]{1,0:T(8,128)(2,1)S(1)} %get-tuple-element.68), channel_id=1, source_target_pairs={{0,128},{64,192},{128,0},{192,64},{1,129},{65,193},{129,1},{193,65... | collective-permute-start | bytes 393224 | tf_op jit(solution)/shard_map/ppermute | solution.py:26
  149.0 3.9 %collective-permute-start.13 = (bf16[128,512]{1,0:T(8,128)(2,1)S(1)}, bf16[128,512]{1,0:T(8,128)(2,1)S(1)}, u32[]{:S(2)}, u32[]{:S(2)}) collective-permute-start(bf16[128,512]{1,0:T(8,128)(2,1)S(1)} %get-tuple-element.69), channel_id=1, source_target_pairs={{0,192},{64,128},{128,64},{192,0},{1,193},{65,129},{129,65},{193,1... | collective-permute-start | bytes 393224 | tf_op jit(solution)/shard_map/ppermute | solution.py:26
  153.0 3.4 %collective-permute-start.14 = (bf16[128,512]{1,0:T(8,128)(2,1)S(1)}, bf16[128,512]{1,0:T(8,128)(2,1)S(1)}, u32[]{:S(2)}, u32[]{:S(2)}) collective-permute-start(bf16[128,512]{1,0:T(8,128)(2,1)S(1)} %get-tuple-element.70), channel_id=1, source_target_pairs={{0,64},{64,0},{128,192},{192,128},{1,65},{65,1},{129,193},{193,129... | collective-permute-start | bytes 393224 | tf_op jit(solution)/shard_map/ppermute | solution.py:26
  156.3 4.1 %collective-permute-done.12.refs_1_ = bf16[128,512]{1,0:T(8,128)(2,1)S(1)} collective-permute-done((bf16[128,512]{1,0:T(8,128)(2,1)S(1)}, bf16[128,512]{1,0:T(8,128)(2,1)S(1)}, u32[]{:S(2)}, u32[]{:S(2)}) %collective-permute-start.12) | collective-permute-done | bytes 131104 | tf_op jit(solution)/shard_map/ppermute | solution.py:26
  160.5 0.0 collective-permute-done.13.refs_2_
  160.5 2.7 %collective-permute-done.14.refs_3_ = bf16[128,512]{1,0:T(8,128)(2,1)S(1)} collective-permute-done((bf16[128,512]{1,0:T(8,128)(2,1)S(1)}, bf16[128,512]{1,0:T(8,128)(2,1)S(1)}, u32[]{:S(2)}, u32[]{:S(2)}) %collective-permute-start.14) | collective-permute-done | bytes 131104 | tf_op jit(solution)/shard_map/ppermute | solution.py:26
  163.2 0.8 shard_map.79
  (1 shorter events, 0.0 us)
Async XLA Ops:
  4.4 11.3 %copy-start = (bf16[3,512,512]{2,1,0:T(8,128)(2,1)S(1)}, bf16[3,512,512]{2,1,0:T(8,128)(2,1)}, u32[]{:S(2)}) copy-start(bf16[3,512,512]{2,1,0:T(8,128)(2,1)} %refs_0_) | copy-start | bytes 4718596
  4.4 82.6 %all-to-all-start = ((bf16[64,3,16,512]{3,2,1,0:T(8,128)(2,1)}), bf16[64,3,16,512]{3,2,1,0:T(8,128)(2,1)}, u32[]{:S(2)}, u32[]{:S(2)}) async-start(bf16[64,3,16,512]{3,2,1,0:T(8,128)(2,1)} %shard_map.73), calls=%async_computation | async-start | bytes 6291456 | tf_op jit(solution)/shard_map/all_to_all | solution.py:360
  15.8 40.7 %collective-permute-start.1 = (bf16[3,256,512]{2,1,0:T(8,128)(2,1)S(1)}, bf16[3,256,512]{2,1,0:T(8,128)(2,1)S(1)}, u32[]{:S(2)}, u32[]{:S(2)}) collective-permute-start(bf16[3,256,512]{2,1,0:T(8,128)(2,1)S(1)} %constant_dynamic-slice_fusion), channel_id=1, source_target_pairs={{0,128},{64,192},{128,0},{192,64},{1,129},{65,193},{129,1},{193,65... | collective-permute-start | bytes 2359304 | tf_op jit(solution)/shard_map/ppermute | solution.py:26
  21.7 39.6 %collective-permute-start = (bf16[3,256,512]{2,1,0:T(8,128)(2,1)S(1)}, bf16[3,256,512]{2,1,0:T(8,128)(2,1)}, u32[]{:S(2)}, u32[]{:S(2)}) collective-permute-start(bf16[3,256,512]{2,1,0:T(8,128)(2,1)S(1)} %constant_dynamic-slice_fusion), channel_id=1, source_target_pairs={{0,64},{64,0},{128,192},{192,128},{1,65},{65,1},{129,193},{193,129... | collective-permute-start | bytes 2359304 | tf_op jit(solution)/shard_map/ppermute | solution.py:26
  56.5 7.3 %collective-permute-start.2 = (bf16[3,256,512]{2,1,0:T(8,128)(2,1)S(1)}, bf16[3,256,512]{2,1,0:T(8,128)(2,1)}, u32[]{:S(2)}, u32[]{:S(2)}) collective-permute-start(bf16[3,256,512]{2,1,0:T(8,128)(2,1)S(1)} %constant_dynamic-slice_fusion), channel_id=1, source_target_pairs={{64,128},{128,64},{65,129},{129,65},{66,130},{130,66},{67,131},{13... | collective-permute-start | bytes 2359304 | tf_op jit(solution)/shard_map/ppermute | solution.py:368
  58.2 21.1 %collective-permute-start.3 = (bf16[3,256,512]{2,1,0:T(8,128)(2,1)S(1)}, bf16[3,256,512]{2,1,0:T(8,128)(2,1)}, u32[]{:S(2)}, u32[]{:S(2)}) collective-permute-start(bf16[3,256,512]{2,1,0:T(8,128)(2,1)S(1)} %collective-permute-done.1.refs_2_), channel_id=1, source_target_pairs={{64,0},{128,192},{65,1},{129,193},{66,2},{130,194},{67,3},{131,195... | collective-permute-start | bytes 2359304 | tf_op jit(solution)/shard_map/ppermute | solution.py:369
  59.4 24.1 %collective-permute-start.5 = (bf16[3,256,512]{2,1,0:T(8,128)(2,1)S(1)}, bf16[3,256,512]{2,1,0:T(8,128)(2,1)}, u32[]{:S(2)}, u32[]{:S(2)}) collective-permute-start(bf16[3,256,512]{2,1,0:T(8,128)(2,1)S(1)} %collective-permute-done.1.refs_2_), channel_id=1, source_target_pairs={{0,1},{1,0},{2,3},{3,2},{4,5},{5,4},{6,7},{7,6},{8,9},{9,8},{10,11... | collective-permute-start | bytes 2359304 | tf_op jit(solution)/shard_map/ppermute | solution.py:34
  61.4 22.1 %collective-permute-start.4 = (bf16[3,256,512]{2,1,0:T(8,128)(2,1)}, bf16[3,256,512]{2,1,0:T(8,128)(2,1)}, u32[]{:S(2)}, u32[]{:S(2)}) collective-permute-start(bf16[3,256,512]{2,1,0:T(8,128)(2,1)} %collective-permute-done.refs_1_), channel_id=1, source_target_pairs={{0,1},{1,0},{2,3},{3,2},{4,5},{5,4},{6,7},{7,6},{8,9},{9,8},{10,11... | collective-permute-start | bytes 2359304 | tf_op jit(solution)/shard_map/ppermute | solution.py:34
  63.8 19.7 %collective-permute-start.6 = (bf16[3,256,512]{2,1,0:T(8,128)(2,1)}, bf16[3,256,512]{2,1,0:T(8,128)(2,1)}, u32[]{:S(2)}, u32[]{:S(2)}) collective-permute-start(bf16[3,256,512]{2,1,0:T(8,128)(2,1)} %collective-permute-done.2.refs_3_), channel_id=1, source_target_pairs={{0,1},{1,0},{2,3},{3,2},{4,5},{5,4},{6,7},{7,6},{8,9},{9,8},{10,11... | collective-permute-start | bytes 2359304 | tf_op jit(solution)/shard_map/ppermute | solution.py:34
  79.3 4.5 %collective-permute-start.7 = (bf16[3,256,512]{2,1,0:T(8,128)(2,1)}, bf16[3,256,512]{2,1,0:T(8,128)(2,1)}, u32[]{:S(2)}, u32[]{:S(2)}) collective-permute-start(bf16[3,256,512]{2,1,0:T(8,128)(2,1)} %collective-permute-done.3.refs_4_), channel_id=1, source_target_pairs={{0,1},{1,0},{2,3},{3,2},{4,5},{5,4},{6,7},{7,6},{8,9},{9,8},{10,11... | collective-permute-start | bytes 2359304 | tf_op jit(solution)/shard_map/ppermute | solution.py:34
  83.5 20.9 %copy-start.1 = (bf16[4,6,128,128]{3,2,1,0:T(8,128)(2,1)S(1)}, bf16[4,6,128,128]{3,2,1,0:T(8,128)(2,1)}, u32[]{:S(2)}) copy-start(bf16[4,6,128,128]{3,2,1,0:T(8,128)(2,1)} %refs_10_) | copy-start | bytes 2359300
  87.0 17.4 %copy-start.3 = (bf16[512,512]{1,0:T(8,128)(2,1)S(1)}, bf16[512,512]{1,0:T(8,128)(2,1)}, u32[]{:S(2)}) copy-start(bf16[512,512]{1,0:T(8,128)(2,1)} %param.7) | copy-start | bytes 1572868
  92.2 31.6 %collective-permute-start.8 = (bf16[3,128,512]{2,1,0:T(8,128)(2,1)}, bf16[3,128,512]{2,1,0:T(8,128)(2,1)S(1)}, u32[]{:S(2)}, u32[]{:S(2)}) collective-permute-start(bf16[3,128,512]{2,1,0:T(8,128)(2,1)} %get-tuple-element.59), channel_id=1, source_target_pairs={{0,128},{64,192},{128,0},{192,64},{1,129},{65,193},{129,1},{193,65... | collective-permute-start | bytes 1179656 | tf_op jit(solution)/shard_map/ppermute | solution.py:26
  98.2 25.6 %collective-permute-start.9 = (bf16[3,128,512]{2,1,0:T(8,128)(2,1)}, bf16[3,128,512]{2,1,0:T(8,128)(2,1)S(1)}, u32[]{:S(2)}, u32[]{:S(2)}) collective-permute-start(bf16[3,128,512]{2,1,0:T(8,128)(2,1)} %get-tuple-element.60), channel_id=1, source_target_pairs={{0,192},{64,128},{128,64},{192,0},{1,193},{65,129},{129,65},{193,1... | collective-permute-start | bytes 1179656 | tf_op jit(solution)/shard_map/ppermute | solution.py:26
  101.9 28.2 %collective-permute-start.10 = (bf16[3,128,512]{2,1,0:T(8,128)(2,1)}, bf16[3,128,512]{2,1,0:T(8,128)(2,1)S(1)}, u32[]{:S(2)}, u32[]{:S(2)}) collective-permute-start(bf16[3,128,512]{2,1,0:T(8,128)(2,1)} %get-tuple-element.61), channel_id=1, source_target_pairs={{0,64},{64,0},{128,192},{192,128},{1,65},{65,1},{129,193},{193,129... | collective-permute-start | bytes 1179656 | tf_op jit(solution)/shard_map/ppermute | solution.py:26
  104.4 25.7 %copy-start.2 = (bf16[3,128,512]{2,1,0:T(8,128)(2,1)S(1)}, bf16[3,128,512]{2,1,0:T(8,128)(2,1)}, u32[]{:S(2)}) copy-start(bf16[3,128,512]{2,1,0:T(8,128)(2,1)} %get-tuple-element.58.refs_4_) | copy-start | bytes 1179652
  134.4 12.7 %collective-permute-start.11 = (bf16[128,512]{1,0:T(8,128)(2,1)S(1)}, bf16[128,512]{1,0:T(8,128)(2,1)S(1)}, u32[]{:S(2)}, u32[]{:S(2)}) collective-permute-start(bf16[128,512]{1,0:T(8,128)(2,1)S(1)} %get-tuple-element.62), channel_id=1, source_target_pairs={{0,384},{64,448},{128,256},{192,320},{1,385},{65,449},{129,257},{1... | collective-permute-start | bytes 393224 | tf_op jit(solution)/shard_map/ppermute | solution.py:381
  147.1 13.4 %collective-permute-start.12 = (bf16[128,512]{1,0:T(8,128)(2,1)S(1)}, bf16[128,512]{1,0:T(8,128)(2,1)S(1)}, u32[]{:S(2)}, u32[]{:S(2)}) collective-permute-start(bf16[128,512]{1,0:T(8,128)(2,1)S(1)} %get-tuple-element.68), channel_id=1, source_target_pairs={{0,128},{64,192},{128,0},{192,64},{1,129},{65,193},{129,1},{193,65... | collective-permute-start | bytes 393224 | tf_op jit(solution)/shard_map/ppermute | solution.py:26
  149.0 11.5 %collective-permute-start.13 = (bf16[128,512]{1,0:T(8,128)(2,1)S(1)}, bf16[128,512]{1,0:T(8,128)(2,1)S(1)}, u32[]{:S(2)}, u32[]{:S(2)}) collective-permute-start(bf16[128,512]{1,0:T(8,128)(2,1)S(1)} %get-tuple-element.69), channel_id=1, source_target_pairs={{0,192},{64,128},{128,64},{192,0},{1,193},{65,129},{129,65},{193,1... | collective-permute-start | bytes 393224 | tf_op jit(solution)/shard_map/ppermute | solution.py:26
  153.0 10.2 %collective-permute-start.14 = (bf16[128,512]{1,0:T(8,128)(2,1)S(1)}, bf16[128,512]{1,0:T(8,128)(2,1)S(1)}, u32[]{:S(2)}, u32[]{:S(2)}) collective-permute-start(bf16[128,512]{1,0:T(8,128)(2,1)S(1)} %get-tuple-element.70), channel_id=1, source_target_pairs={{0,64},{64,0},{128,192},{192,128},{1,65},{65,1},{129,193},{193,129... | collective-permute-start | bytes 393224 | tf_op jit(solution)/shard_map/ppermute | solution.py:26

commit v8 on v7

--- a/solution.py
+++ b/solution.py
@@ -138,9 +138,8 @@
 
 
 def stage_kernel(*refs):
-    shards = STAGES
-    own_ref, near_refs, far_refs = refs[0], refs[1 : 1 + shards], refs[1 + shards : 1 + 2 * shards]
-    features_ref, blocks_ref, group_ref, own_x_ref, own_a_ref, sem = refs[1 + 2 * shards :]
+    own_ref, near_refs, far_refs = refs[0], refs[1:STAGES], refs[STAGES : 2 * STAGES - 1]
+    features_ref, blocks_ref, group_ref, own_x_ref, own_a_ref, sem = refs[2 * STAGES - 1 :]
     depth = group_ref.shape[3]
     stage = lax.axis_index("stage")
     core = lax.axis_index("core")
@@ -154,21 +153,8 @@
         pairs.append((near_refs[r - 1], group_ref.at[stage ^ r, core]))
         pairs.append((far_refs[r - 1], group_ref.at[stage ^ r, 1 - core]))
     copies = [pltpu.make_async_copy(*pair, sem.at[n]) for n, pair in enumerate(pairs)]
-    late = len(copies) - 2
-    inner = (stage == 1) | (stage == 2)
-    for copy in copies[:late]:
+    for copy in copies:
         copy.start()
-
-    @pl.when(inner)
-    def _():
-        for copy in copies[late:]:
-            copy.start()
-
-    @pl.when(jnp.logical_not(inner))
-    def _():
-        pltpu.make_async_copy(near_refs[-1], pairs[late][1], sem.at[late]).start()
-        pltpu.make_async_copy(far_refs[-1], pairs[late + 1][1], sem.at[late + 1]).start()
-
     for copy in copies:
         copy.wait()
 
@@ -364,9 +350,7 @@
     own = lax.dynamic_slice_in_dim(weights, core * depth, depth, 1)
     two = exchange(own, 2)
     near = [exchange(own, 1), two]
-    own, two = lax.optimization_barrier((own, two))
-    near.append(lax.ppermute(own, "stage", [(1, 2), (2, 1)]))
-    near.append(lax.ppermute(two, "stage", [(1, 0), (2, 3)]))
+    near.append(exchange(two, 1))
     far = [swap_cores(block) for block in near]
     spread = spread_blocks(adj_src, adj_blocks, halo_rows)
     arrived, spread, near, far = lax.optimization_barrier((arrived, spread, near, far))

time: 166 us -> 166 us (level)
  starting transfers between devices: 62.7 us -> 60.5 us
  waiting for transfers between devices: 81.2 us -> 83.4 us
    ppermute x8 -> x9, waiting for transfers between devices: 60.3 us -> 74.5 us  [exchange(): return lax.ppermute(block, 'stage', [(u, u ^ slot) for u in range(STAGES)])]
    ppermute x2 -> x0, waiting for transfers between devices: 13.5 us -> none  [the longest x1 13.5 us: local(): near.append(lax.ppermute(two, 'stage', [(1, 0), (2, 3)]))]
    ppermute x2 -> x0, starting transfers between devices: 2.89 us -> none  [the longest x1 1.61 us: local(): near.append(lax.ppermute(own, 'stage', [(1, 2), (2, 1)]))]
    ppermute x8 -> x9, starting transfers between devices: 31.6 us -> 34.2 us  [exchange(): return lax.ppermute(block, 'stage', [(u, u ^ slot) for u in range(STAGES)])]
    ppermute x4 -> x3, starting transfers between devices: 8.16 us -> 6.24 us  [swap_cores(): return lax.ppermute(block, 'core', [(0, 1), (1, 0)])]
  transfers between devices with their start and end apart: 16 -> 14, of which waited for: 9 -> 9; matrix products, arithmetic and copies ran while one was open for 0% -> 0% of each run, Pallas kernels for 3% -> 3%
where the time goes in v8:
time: 166 us; the launch traced here: 164 us
  waiting for transfers between devices  83.4 us (50%)
  starting transfers between devices  60.5 us (36%)
  Pallas kernels  19.8 us (12%)
    ppermute x9, waiting for transfers between devices, exchange(): return lax.ppermute(block, 'stage', [(u, u ^ slot) for u in range(STAGES)])  74.5 us
    ppermute x9, starting transfers between devices, exchange(): return lax.ppermute(block, 'stage', [(u, u ^ slot) for u in range(STAGES)])  34.2 us
    all_to_all x1, starting transfers between devices, local(): lax.all_to_all(outgoing, DOM, split_axis=0, concat_axis=0, tiled=True)  11.3 us
    ppermute x1, starting transfers between devices, local(): lax.ppermute(last, SEGMENT, over)  8.85 us
    ppermute x3, starting transfers between devices, swap_cores(): return lax.ppermute(block, 'core', [(0, 1), (1, 0)])  6.24 us
    pallas_call x1, Pallas kernels, halo_sums(): pl.pallas_call(halo_kernel, out_shape=[jax.ShapeDtypeStruct((levels, rows...  5.2 us
    all_to_all x1, waiting for transfers between devices, local(): lax.all_to_all(outgoing, DOM, split_axis=0, concat_axis=0, tiled=True)  4.85 us
    pallas_call x1, Pallas kernels, pick_rows(): pl.pallas_call(pick_kernel, out_shape=jax.ShapeDtypeStruct((parts, levels...  4.51 us
  transfers between devices with their start and end apart: 14, of which 9 were waited for; matrix products, arithmetic and copies ran while one was open for 0% of the time, Pallas kernels for 3%

profile of v8, /device:TPU:6, one launch (start us, length us, event | category | flops | bytes accessed | tf_op | source)
XLA Modules:
  0.0 164.1 jit_solution(17906866151424986933)
XLA Ops:
  0.0 4.5 %shard_map.73 = bf16[64,3,16,512]{3,2,1,0:T(8,128)(2,1)} custom-call(s32[1,16,64]{2,1,0:T(8,128)} %bitcast.4, s32[1,64]{1,0:T(1,128)} %count_ref.1, bf16[3,512,512]{2,1,0:T(8,128)(2,1)} %history_ref.1), custom_call_target="tpu_custom_call" | custom-call | flops 1610612736 | bytes 4718592 | tf_op jit(solution)/shard_map/pallas_call | solution.py:116
  4.5 0.0 copy-start
  4.5 11.3 %all-to-all-start = ((bf16[64,3,16,512]{3,2,1,0:T(8,128)(2,1)}), bf16[64,3,16,512]{3,2,1,0:T(8,128)(2,1)}, u32[]{:S(2)}, u32[]{:S(2)}) async-start(bf16[64,3,16,512]{3,2,1,0:T(8,128)(2,1)} %shard_map.73), calls=%async_computation | async-start | bytes 6291456 | tf_op jit(solution)/shard_map/all_to_all | solution.py:346
  15.8 0.0 copy-done
  15.8 0.1 constant_dynamic-slice_fusion
  15.9 5.9 %collective-permute-start.1 = (bf16[3,256,512]{2,1,0:T(8,128)(2,1)S(1)}, bf16[3,256,512]{2,1,0:T(8,128)(2,1)S(1)}, u32[]{:S(2)}, u32[]{:S(2)}) collective-permute-start(bf16[3,256,512]{2,1,0:T(8,128)(2,1)S(1)} %constant_dynamic-slice_fusion), channel_id=1, source_target_pairs={{0,128},{64,192},{128,0},{192,64},{1,129},{65,193},{129,1},{193,65... | collective-permute-start | bytes 2359304 | tf_op jit(solution)/shard_map/ppermute | solution.py:26
  21.8 4.3 %collective-permute-start = (bf16[3,256,512]{2,1,0:T(8,128)(2,1)S(1)}, bf16[3,256,512]{2,1,0:T(8,128)(2,1)}, u32[]{:S(2)}, u32[]{:S(2)}) collective-permute-start(bf16[3,256,512]{2,1,0:T(8,128)(2,1)S(1)} %constant_dynamic-slice_fusion), channel_id=1, source_target_pairs={{0,64},{64,0},{128,192},{192,128},{1,65},{65,1},{129,193},{193,129... | collective-permute-start | bytes 2359304 | tf_op jit(solution)/shard_map/ppermute | solution.py:26
  26.1 30.5 %collective-permute-done.1.refs_2_ = bf16[3,256,512]{2,1,0:T(8,128)(2,1)S(1)} collective-permute-done((bf16[3,256,512]{2,1,0:T(8,128)(2,1)S(1)}, bf16[3,256,512]{2,1,0:T(8,128)(2,1)S(1)}, u32[]{:S(2)}, u32[]{:S(2)}) %collective-permute-start.1) | collective-permute-done | bytes 786464 | tf_op jit(solution)/shard_map/ppermute | solution.py:26
  56.6 2.6 %collective-permute-start.2 = (bf16[3,256,512]{2,1,0:T(8,128)(2,1)S(1)}, bf16[3,256,512]{2,1,0:T(8,128)(2,1)}, u32[]{:S(2)}, u32[]{:S(2)}) collective-permute-start(bf16[3,256,512]{2,1,0:T(8,128)(2,1)S(1)} %collective-permute-done.1.refs_2_), channel_id=1, source_target_pairs={{0,64},{64,0},{128,192},{192,128},{1,65},{65,1},{129,193},{193,129... | collective-permute-start | bytes 2359304 | tf_op jit(solution)/shard_map/ppermute | solution.py:26
  59.2 1.9 %collective-permute-start.4 = (bf16[3,256,512]{2,1,0:T(8,128)(2,1)S(1)}, bf16[3,256,512]{2,1,0:T(8,128)(2,1)}, u32[]{:S(2)}, u32[]{:S(2)}) collective-permute-start(bf16[3,256,512]{2,1,0:T(8,128)(2,1)S(1)} %collective-permute-done.1.refs_2_), channel_id=1, source_target_pairs={{0,1},{1,0},{2,3},{3,2},{4,5},{5,4},{6,7},{7,6},{8,9},{9,8},{10,11... | collective-permute-start | bytes 2359304 | tf_op jit(solution)/shard_map/ppermute | solution.py:34
  61.1 0.0 collective-permute-done.refs_1_
  61.1 2.4 %collective-permute-start.3 = (bf16[3,256,512]{2,1,0:T(8,128)(2,1)}, bf16[3,256,512]{2,1,0:T(8,128)(2,1)}, u32[]{:S(2)}, u32[]{:S(2)}) collective-permute-start(bf16[3,256,512]{2,1,0:T(8,128)(2,1)} %collective-permute-done.refs_1_), channel_id=1, source_target_pairs={{0,1},{1,0},{2,3},{3,2},{4,5},{5,4},{6,7},{7,6},{8,9},{9,8},{10,11... | collective-permute-start | bytes 2359304 | tf_op jit(solution)/shard_map/ppermute | solution.py:34
  63.6 14.2 %collective-permute-done.2.refs_3_ = bf16[3,256,512]{2,1,0:T(8,128)(2,1)} collective-permute-done((bf16[3,256,512]{2,1,0:T(8,128)(2,1)S(1)}, bf16[3,256,512]{2,1,0:T(8,128)(2,1)}, u32[]{:S(2)}, u32[]{:S(2)}) %collective-permute-start.2) | collective-permute-done | bytes 786464 | tf_op jit(solution)/shard_map/ppermute | solution.py:26
  77.7 1.9 %collective-permute-start.5 = (bf16[3,256,512]{2,1,0:T(8,128)(2,1)}, bf16[3,256,512]{2,1,0:T(8,128)(2,1)}, u32[]{:S(2)}, u32[]{:S(2)}) collective-permute-start(bf16[3,256,512]{2,1,0:T(8,128)(2,1)} %collective-permute-done.2.refs_3_), channel_id=1, source_target_pairs={{0,1},{1,0},{2,3},{3,2},{4,5},{5,4},{6,7},{7,6},{8,9},{9,8},{10,11... | collective-permute-start | bytes 2359304 | tf_op jit(solution)/shard_map/ppermute | solution.py:34
  79.7 2.3 %shard_map.74.spread_ref = bf16[4,128,1024]{2,1,0:T(8,128)(2,1)} custom-call(s32[4,6]{1,0:T(4,128)} %source_ref.1, bf16[4,6,128,128]{3,2,1,0:T(8,128)(2,1)} %refs_8_), custom_call_target="tpu_custom_call" | custom-call | tf_op jit(solution)/shard_map/pallas_call | solution.py:48
  82.0 0.0 copy-start.1
  82.0 0.0 collective-permute-done.4.refs_5_
  82.0 0.0 collective-permute-done.3.refs_4_
  82.0 0.2 collective-permute-done.5.refs_6_
  82.2 4.9 %all-to-all-done.arrived_ref = bf16[64,3,16,512]{3,2,1,0:T(8,128)(2,1)} async-done(((bf16[64,3,16,512]{3,2,1,0:T(8,128)(2,1)}), bf16[64,3,16,512]{3,2,1,0:T(8,128)(2,1)}, u32[]{:S(2)}, u32[]{:S(2)}) %all-to-all-start) | async-done | bytes 3145760 | tf_op jit(solution)/shard_map/all_to_all | solution.py:346
  87.1 0.0 copy-start.3
  87.1 5.2 %shard_map.75 = (bf16[3,128,512]{2,1,0:T(8,128)(2,1)}, bf16[3,128,512]{2,1,0:T(8,128)(2,1)}, bf16[3,128,512]{2,1,0:T(8,128)(2,1)}, bf16[3,128,512]{2,1,0:T(8,128)(2,1)}) custom-call(bf16[64,3,16,512]{3,2,1,0:T(8,128)(2,1)} %all-to-all-done.arrived_ref, bf16[4,128,1024]{2,1,0:T(8,128)(2,1)} %shard_map.74.spread_ref), custom_call_target="tpu_custom_call" | custom-call | flops 1610612736 | bytes 5767168 | tf_op jit(solution)/shard_map/pallas_call | solution.py:228
  92.3 6.0 %collective-permute-start.6 = (bf16[3,128,512]{2,1,0:T(8,128)(2,1)}, bf16[3,128,512]{2,1,0:T(8,128)(2,1)S(1)}, u32[]{:S(2)}, u32[]{:S(2)}) collective-permute-start(bf16[3,128,512]{2,1,0:T(8,128)(2,1)} %get-tuple-element.51), channel_id=1, source_target_pairs={{0,128},{64,192},{128,0},{192,64},{1,129},{65,193},{129,1},{193,65... | collective-permute-start | bytes 1179656 | tf_op jit(solution)/shard_map/ppermute | solution.py:26
  98.3 3.7 %collective-permute-start.7 = (bf16[3,128,512]{2,1,0:T(8,128)(2,1)}, bf16[3,128,512]{2,1,0:T(8,128)(2,1)S(1)}, u32[]{:S(2)}, u32[]{:S(2)}) collective-permute-start(bf16[3,128,512]{2,1,0:T(8,128)(2,1)} %get-tuple-element.52), channel_id=1, source_target_pairs={{0,192},{64,128},{128,64},{192,0},{1,193},{65,129},{129,65},{193,1... | collective-permute-start | bytes 1179656 | tf_op jit(solution)/shard_map/ppermute | solution.py:26
  102.0 2.5 %collective-permute-start.8 = (bf16[3,128,512]{2,1,0:T(8,128)(2,1)}, bf16[3,128,512]{2,1,0:T(8,128)(2,1)S(1)}, u32[]{:S(2)}, u32[]{:S(2)}) collective-permute-start(bf16[3,128,512]{2,1,0:T(8,128)(2,1)} %get-tuple-element.53), channel_id=1, source_target_pairs={{0,64},{64,0},{128,192},{192,128},{1,65},{65,1},{129,193},{193,129... | collective-permute-start | bytes 1179656 | tf_op jit(solution)/shard_map/ppermute | solution.py:26
  104.5 0.0 copy-done.1
  104.5 0.0 copy-done.3
  104.5 0.0 copy-start.2
  104.5 2.7 %shard_map.76 = (bf16[4,2,3,256,512]{4,3,2,1,0:T(8,128)(2,1)S(1)}, bf16[128,512]{1,0:T(8,128)(2,1)S(1)}, bf16[128,128]{1,0:T(8,128)(2,1)S(1)}) custom-call(bf16[3,512,512]{2,1,0:T(8,128)(2,1)S(1)} %copy-done, bf16[3,256,512]{2,1,0:T(8,128)(2,1)} %collective-permute-done.refs_1_, bf16[3,256,512]{2,1,0:T(8,128)(2,1)S(1)} %collective-permute-done.1.refs_2_, ...), custom_call_target="tpu_custom_call" | custom-call | bytes 12582912 | tf_op jit(solution)/shard_map/pallas_call | solution.py:167
  107.2 16.7 %collective-permute-done.6.refs_5_ = bf16[3,128,512]{2,1,0:T(8,128)(2,1)S(1)} collective-permute-done((bf16[3,128,512]{2,1,0:T(8,128)(2,1)}, bf16[3,128,512]{2,1,0:T(8,128)(2,1)S(1)}, u32[]{:S(2)}, u32[]{:S(2)}) %collective-permute-start.6) | collective-permute-done | bytes 393248 | tf_op jit(solution)/shard_map/ppermute | solution.py:26
  123.9 0.0 collective-permute-done.7.refs_6_
  123.9 6.3 %collective-permute-done.8.refs_7_ = bf16[3,128,512]{2,1,0:T(8,128)(2,1)S(1)} collective-permute-done((bf16[3,128,512]{2,1,0:T(8,128)(2,1)}, bf16[3,128,512]{2,1,0:T(8,128)(2,1)S(1)}, u32[]{:S(2)}, u32[]{:S(2)}) %collective-permute-start.8) | collective-permute-done | bytes 393248 | tf_op jit(solution)/shard_map/ppermute | solution.py:26
  130.2 0.0 copy-done.2
  130.2 4.3 %shard_map.77 = (bf16[128,512]{1,0:T(8,128)(2,1)S(1)}, bf16[128,512]{1,0:T(8,128)(2,1)S(1)}, bf16[128,512]{1,0:T(8,128)(2,1)S(1)}, bf16[128,512]{1,0:T(8,128)(2,1)S(1)}, bf16[128,512]{1,0:T(8,128)(2,1)S(1)}) custom-call(bf16[128,512]{1,0:T(8,128)(2,1)S(1)} %get-tuple-element.47.refs_0_.refs_1_, bf16[128,512]{1,0:T(8,128)(2,1)S(1)} %get-tuple-element.47.refs_0_.refs_1_, ...), custom_call_target="tpu_custom_call" | custom-call | flops 1006632960 | bytes 7864320 | tf_op jit(solution)/shard_map/pallas_call | solution.py:305
  134.5 8.9 %collective-permute-start.9 = (bf16[128,512]{1,0:T(8,128)(2,1)S(1)}, bf16[128,512]{1,0:T(8,128)(2,1)S(1)}, u32[]{:S(2)}, u32[]{:S(2)}) collective-permute-start(bf16[128,512]{1,0:T(8,128)(2,1)S(1)} %get-tuple-element.54), channel_id=1, source_target_pairs={{0,384},{64,448},{128,256},{192,320},{1,385},{65,449},{129,257},{1... | collective-permute-start | bytes 393224 | tf_op jit(solution)/shard_map/ppermute | solution.py:365
  143.3 3.8 %collective-permute-done.9.refs_0_ = bf16[128,512]{1,0:T(8,128)(2,1)S(1)} collective-permute-done((bf16[128,512]{1,0:T(8,128)(2,1)S(1)}, bf16[128,512]{1,0:T(8,128)(2,1)S(1)}, u32[]{:S(2)}, u32[]{:S(2)}) %collective-permute-start.9) | collective-permute-done | bytes 131104 | tf_op jit(solution)/shard_map/ppermute | solution.py:365
  147.2 1.9 %collective-permute-start.10 = (bf16[128,512]{1,0:T(8,128)(2,1)S(1)}, bf16[128,512]{1,0:T(8,128)(2,1)S(1)}, u32[]{:S(2)}, u32[]{:S(2)}) collective-permute-start(bf16[128,512]{1,0:T(8,128)(2,1)S(1)} %get-tuple-element.60), channel_id=1, source_target_pairs={{0,128},{64,192},{128,0},{192,64},{1,129},{65,193},{129,1},{193,65... | collective-permute-start | bytes 393224 | tf_op jit(solution)/shard_map/ppermute | solution.py:26
  149.1 3.9 %collective-permute-start.11 = (bf16[128,512]{1,0:T(8,128)(2,1)S(1)}, bf16[128,512]{1,0:T(8,128)(2,1)S(1)}, u32[]{:S(2)}, u32[]{:S(2)}) collective-permute-start(bf16[128,512]{1,0:T(8,128)(2,1)S(1)} %get-tuple-element.61), channel_id=1, source_target_pairs={{0,192},{64,128},{128,64},{192,0},{1,193},{65,129},{129,65},{193,1... | collective-permute-start | bytes 393224 | tf_op jit(solution)/shard_map/ppermute | solution.py:26
  153.1 3.4 %collective-permute-start.12 = (bf16[128,512]{1,0:T(8,128)(2,1)S(1)}, bf16[128,512]{1,0:T(8,128)(2,1)S(1)}, u32[]{:S(2)}, u32[]{:S(2)}) collective-permute-start(bf16[128,512]{1,0:T(8,128)(2,1)S(1)} %get-tuple-element.62), channel_id=1, source_target_pairs={{0,64},{64,0},{128,192},{192,128},{1,65},{65,1},{129,193},{193,129... | collective-permute-start | bytes 393224 | tf_op jit(solution)/shard_map/ppermute | solution.py:26
  156.4 4.1 %collective-permute-done.10.refs_1_ = bf16[128,512]{1,0:T(8,128)(2,1)S(1)} collective-permute-done((bf16[128,512]{1,0:T(8,128)(2,1)S(1)}, bf16[128,512]{1,0:T(8,128)(2,1)S(1)}, u32[]{:S(2)}, u32[]{:S(2)}) %collective-permute-start.10) | collective-permute-done | bytes 131104 | tf_op jit(solution)/shard_map/ppermute | solution.py:26
  160.6 0.0 collective-permute-done.11.refs_2_
  160.6 2.7 %collective-permute-done.12.refs_3_ = bf16[128,512]{1,0:T(8,128)(2,1)S(1)} collective-permute-done((bf16[128,512]{1,0:T(8,128)(2,1)S(1)}, bf16[128,512]{1,0:T(8,128)(2,1)S(1)}, u32[]{:S(2)}, u32[]{:S(2)}) %collective-permute-start.12) | collective-permute-done | bytes 131104 | tf_op jit(solution)/shard_map/ppermute | solution.py:26
  163.2 0.8 shard_map.79
  (1 shorter events, 0.0 us)
Async XLA Ops:
  4.5 11.3 %copy-start = (bf16[3,512,512]{2,1,0:T(8,128)(2,1)S(1)}, bf16[3,512,512]{2,1,0:T(8,128)(2,1)}, u32[]{:S(2)}) copy-start(bf16[3,512,512]{2,1,0:T(8,128)(2,1)} %refs_0_) | copy-start | bytes 4718596
  4.5 82.6 %all-to-all-start = ((bf16[64,3,16,512]{3,2,1,0:T(8,128)(2,1)}), bf16[64,3,16,512]{3,2,1,0:T(8,128)(2,1)}, u32[]{:S(2)}, u32[]{:S(2)}) async-start(bf16[64,3,16,512]{3,2,1,0:T(8,128)(2,1)} %shard_map.73), calls=%async_computation | async-start | bytes 6291456 | tf_op jit(solution)/shard_map/all_to_all | solution.py:346
  15.9 40.7 %collective-permute-start.1 = (bf16[3,256,512]{2,1,0:T(8,128)(2,1)S(1)}, bf16[3,256,512]{2,1,0:T(8,128)(2,1)S(1)}, u32[]{:S(2)}, u32[]{:S(2)}) collective-permute-start(bf16[3,256,512]{2,1,0:T(8,128)(2,1)S(1)} %constant_dynamic-slice_fusion), channel_id=1, source_target_pairs={{0,128},{64,192},{128,0},{192,64},{1,129},{65,193},{129,1},{193,65... | collective-permute-start | bytes 2359304 | tf_op jit(solution)/shard_map/ppermute | solution.py:26
  21.8 39.3 %collective-permute-start = (bf16[3,256,512]{2,1,0:T(8,128)(2,1)S(1)}, bf16[3,256,512]{2,1,0:T(8,128)(2,1)}, u32[]{:S(2)}, u32[]{:S(2)}) collective-permute-start(bf16[3,256,512]{2,1,0:T(8,128)(2,1)S(1)} %constant_dynamic-slice_fusion), channel_id=1, source_target_pairs={{0,64},{64,0},{128,192},{192,128},{1,65},{65,1},{129,193},{193,129... | collective-permute-start | bytes 2359304 | tf_op jit(solution)/shard_map/ppermute | solution.py:26
  56.6 21.1 %collective-permute-start.2 = (bf16[3,256,512]{2,1,0:T(8,128)(2,1)S(1)}, bf16[3,256,512]{2,1,0:T(8,128)(2,1)}, u32[]{:S(2)}, u32[]{:S(2)}) collective-permute-start(bf16[3,256,512]{2,1,0:T(8,128)(2,1)S(1)} %collective-permute-done.1.refs_2_), channel_id=1, source_target_pairs={{0,64},{64,0},{128,192},{192,128},{1,65},{65,1},{129,193},{193,129... | collective-permute-start | bytes 2359304 | tf_op jit(solution)/shard_map/ppermute | solution.py:26
  59.2 22.8 %collective-permute-start.4 = (bf16[3,256,512]{2,1,0:T(8,128)(2,1)S(1)}, bf16[3,256,512]{2,1,0:T(8,128)(2,1)}, u32[]{:S(2)}, u32[]{:S(2)}) collective-permute-start(bf16[3,256,512]{2,1,0:T(8,128)(2,1)S(1)} %collective-permute-done.1.refs_2_), channel_id=1, source_target_pairs={{0,1},{1,0},{2,3},{3,2},{4,5},{5,4},{6,7},{7,6},{8,9},{9,8},{10,11... | collective-permute-start | bytes 2359304 | tf_op jit(solution)/shard_map/ppermute | solution.py:34
  61.1 20.9 %collective-permute-start.3 = (bf16[3,256,512]{2,1,0:T(8,128)(2,1)}, bf16[3,256,512]{2,1,0:T(8,128)(2,1)}, u32[]{:S(2)}, u32[]{:S(2)}) collective-permute-start(bf16[3,256,512]{2,1,0:T(8,128)(2,1)} %collective-permute-done.refs_1_), channel_id=1, source_target_pairs={{0,1},{1,0},{2,3},{3,2},{4,5},{5,4},{6,7},{7,6},{8,9},{9,8},{10,11... | collective-permute-start | bytes 2359304 | tf_op jit(solution)/shard_map/ppermute | solution.py:34
  77.7 4.5 %collective-permute-start.5 = (bf16[3,256,512]{2,1,0:T(8,128)(2,1)}, bf16[3,256,512]{2,1,0:T(8,128)(2,1)}, u32[]{:S(2)}, u32[]{:S(2)}) collective-permute-start(bf16[3,256,512]{2,1,0:T(8,128)(2,1)} %collective-permute-done.2.refs_3_), channel_id=1, source_target_pairs={{0,1},{1,0},{2,3},{3,2},{4,5},{5,4},{6,7},{7,6},{8,9},{9,8},{10,11... | collective-permute-start | bytes 2359304 | tf_op jit(solution)/shard_map/ppermute | solution.py:34
  82.0 22.5 %copy-start.1 = (bf16[4,6,128,128]{3,2,1,0:T(8,128)(2,1)S(1)}, bf16[4,6,128,128]{3,2,1,0:T(8,128)(2,1)}, u32[]{:S(2)}) copy-start(bf16[4,6,128,128]{3,2,1,0:T(8,128)(2,1)} %refs_8_) | copy-start | bytes 2359300
  87.1 17.4 %copy-start.3 = (bf16[512,512]{1,0:T(8,128)(2,1)S(1)}, bf16[512,512]{1,0:T(8,128)(2,1)}, u32[]{:S(2)}) copy-start(bf16[512,512]{1,0:T(8,128)(2,1)} %param.7) | copy-start | bytes 1572868
  92.3 31.6 %collective-permute-start.6 = (bf16[3,128,512]{2,1,0:T(8,128)(2,1)}, bf16[3,128,512]{2,1,0:T(8,128)(2,1)S(1)}, u32[]{:S(2)}, u32[]{:S(2)}) collective-permute-start(bf16[3,128,512]{2,1,0:T(8,128)(2,1)} %get-tuple-element.51), channel_id=1, source_target_pairs={{0,128},{64,192},{128,0},{192,64},{1,129},{65,193},{129,1},{193,65... | collective-permute-start | bytes 1179656 | tf_op jit(solution)/shard_map/ppermute | solution.py:26
  98.3 25.6 %collective-permute-start.7 = (bf16[3,128,512]{2,1,0:T(8,128)(2,1)}, bf16[3,128,512]{2,1,0:T(8,128)(2,1)S(1)}, u32[]{:S(2)}, u32[]{:S(2)}) collective-permute-start(bf16[3,128,512]{2,1,0:T(8,128)(2,1)} %get-tuple-element.52), channel_id=1, source_target_pairs={{0,192},{64,128},{128,64},{192,0},{1,193},{65,129},{129,65},{193,1... | collective-permute-start | bytes 1179656 | tf_op jit(solution)/shard_map/ppermute | solution.py:26
  102.0 28.2 %collective-permute-start.8 = (bf16[3,128,512]{2,1,0:T(8,128)(2,1)}, bf16[3,128,512]{2,1,0:T(8,128)(2,1)S(1)}, u32[]{:S(2)}, u32[]{:S(2)}) collective-permute-start(bf16[3,128,512]{2,1,0:T(8,128)(2,1)} %get-tuple-element.53), channel_id=1, source_target_pairs={{0,64},{64,0},{128,192},{192,128},{1,65},{65,1},{129,193},{193,129... | collective-permute-start | bytes 1179656 | tf_op jit(solution)/shard_map/ppermute | solution.py:26
  104.5 25.7 %copy-start.2 = (bf16[3,128,512]{2,1,0:T(8,128)(2,1)S(1)}, bf16[3,128,512]{2,1,0:T(8,128)(2,1)}, u32[]{:S(2)}) copy-start(bf16[3,128,512]{2,1,0:T(8,128)(2,1)} %get-tuple-element.50.refs_4_) | copy-start | bytes 1179652
  134.5 12.7 %collective-permute-start.9 = (bf16[128,512]{1,0:T(8,128)(2,1)S(1)}, bf16[128,512]{1,0:T(8,128)(2,1)S(1)}, u32[]{:S(2)}, u32[]{:S(2)}) collective-permute-start(bf16[128,512]{1,0:T(8,128)(2,1)S(1)} %get-tuple-element.54), channel_id=1, source_target_pairs={{0,384},{64,448},{128,256},{192,320},{1,385},{65,449},{129,257},{1... | collective-permute-start | bytes 393224 | tf_op jit(solution)/shard_map/ppermute | solution.py:365
  147.2 13.4 %collective-permute-start.10 = (bf16[128,512]{1,0:T(8,128)(2,1)S(1)}, bf16[128,512]{1,0:T(8,128)(2,1)S(1)}, u32[]{:S(2)}, u32[]{:S(2)}) collective-permute-start(bf16[128,512]{1,0:T(8,128)(2,1)S(1)} %get-tuple-element.60), channel_id=1, source_target_pairs={{0,128},{64,192},{128,0},{192,64},{1,129},{65,193},{129,1},{193,65... | collective-permute-start | bytes 393224 | tf_op jit(solution)/shard_map/ppermute | solution.py:26
  149.1 11.5 %collective-permute-start.11 = (bf16[128,512]{1,0:T(8,128)(2,1)S(1)}, bf16[128,512]{1,0:T(8,128)(2,1)S(1)}, u32[]{:S(2)}, u32[]{:S(2)}) collective-permute-start(bf16[128,512]{1,0:T(8,128)(2,1)S(1)} %get-tuple-element.61), channel_id=1, source_target_pairs={{0,192},{64,128},{128,64},{192,0},{1,193},{65,129},{129,65},{193,1... | collective-permute-start | bytes 393224 | tf_op jit(solution)/shard_map/ppermute | solution.py:26
  153.1 10.2 %collective-permute-start.12 = (bf16[128,512]{1,0:T(8,128)(2,1)S(1)}, bf16[128,512]{1,0:T(8,128)(2,1)S(1)}, u32[]{:S(2)}, u32[]{:S(2)}) collective-permute-start(bf16[128,512]{1,0:T(8,128)(2,1)S(1)} %get-tuple-element.62), channel_id=1, source_target_pairs={{0,64},{64,0},{128,192},{192,128},{1,65},{65,1},{129,193},{193,129... | collective-permute-start | bytes 393224 | tf_op jit(solution)/shard_map/ppermute | solution.py:26
